TPU v7x, 32 devices: a whole 2x2x4 slice. The times are simulated.
32 devices in a mesh: dp: 16 (over z, y, x), seq: 2 (over core).
Axes of the slice: x: 2, y: 2, z: 4, core: 2. Of those that a mesh axis runs over, the one named last changes fastest.
Arguments:
- inputs: bfloat16 [16, 512, 768], P('dp', 'seq'), may hold values from -6 to 6
- pair_lengths: int32 [16, 8], P('dp'), may hold values from 1 to 175, as said below
- w_query: bfloat16 [768, 768], replicated, may hold values from -0.21875 to 0.21875
- w_key: bfloat16 [768, 768], replicated, may hold values from -0.21875 to 0.21875
- w_value: bfloat16 [768, 768], replicated, may hold values from -0.21875 to 0.21875
- w_out: bfloat16 [768, 768], replicated, may hold values from -0.625 to 0.625
- w_up: bfloat16 [768, 3072], replicated, may hold values from -0.21875 to 0.21875
- w_down: bfloat16 [3072, 768], replicated, may hold values from -0.15625 to 0.15625
- a_query: bfloat16 [768, 8], replicated, may hold values from -0.21875 to 0.21875
- b_query: bfloat16 [8, 768], replicated, may hold values from -1 to 1
- a_value: bfloat16 [768, 8], replicated, may hold values from -0.21875 to 0.21875
- b_value: bfloat16 [8, 768], replicated, may hold values from -1 to 1
- gain_one: float32 [768], replicated, may hold values from 0.5 to 1.5
- shift_one: float32 [768], replicated, may hold values from -3 to 3
- gain_two: float32 [768], replicated, may hold values from 0.5 to 1.5
- shift_two: float32 [768], replicated, may hold values from -3 to 3
- cotangent: bfloat16 [16, 512, 768], P('dp', 'seq'), may hold values from -6 to 6
Outputs:
- output: bfloat16 [16, 512, 768], P('dp', 'seq')
- grad_inputs: float32 [16, 512, 768], P('dp', 'seq')
- grad_a_query: float32 [768, 8], replicated
- grad_b_query: float32 [8, 768], replicated
- grad_a_value: float32 [768, 8], replicated
- grad_b_value: float32 [8, 768], replicated
- grad_gain_one: float32 [768], replicated
- grad_shift_one: float32 [768], replicated
- grad_gain_two: float32 [768], replicated
- grad_shift_two: float32 [768], replicated
Inputs may be any that keep to these rules, and one draw needn't show every extreme that they name: `pair_lengths`: each row's entries sum to at least 384 and at most 512; positions past the sum are padding. Some row in every draw has no padding and a last pair of the largest length.
All inputs are finite; a program needn't handle non-finite values.
Results may differ from a plain program's by a relative error of at most 0.015.
Values may be sent and summed in bfloat16 or wider, within the bound.
No kernel may reach another device: no remote copies, remote signals or barrier semaphores. Data moves between devices by JAX's collectives and lax.ppermute only.
A program may use at most 128 MiB of HBM per device.

v0:
```python
import math

import jax
import jax.numpy as jnp
from jax import lax
from jax.sharding import PartitionSpec as P

DH = 64


norm_epsilon = 1e-05


def matmul(former, latter):
    return jnp.dot(former, latter, preferred_element_type=jnp.float32)


def row_inner(former, latter):
    return lax.dot_general(
        former, latter, (((0,), (0,)), ((), ())), preferred_element_type=jnp.float32
    )


def segment_ids(lengths, span_length):
    pair_ends = jnp.cumsum(lengths, axis=-1)
    places = jnp.arange(span_length, dtype=jnp.int32)
    return jnp.sum((places[None, :, None] >= pair_ends[:, None, :]).astype(jnp.int32), axis=-1)


def norm_rows(values, gain_vec, shift_vec):
    centred = values - jnp.mean(values, axis=-1, keepdims=True)
    variance = jnp.mean(centred * centred, axis=-1, keepdims=True)
    return centred * lax.rsqrt(variance + norm_epsilon) * gain_vec + shift_vec


def gelu_exact(values):
    return jax.nn.gelu(values, approximate=False)


def body(
    inputs,
    pair_lengths,
    w_query,
    w_key,
    w_value,
    w_out,
    w_up,
    w_down,
    a_query,
    b_query,
    a_value,
    b_value,
    gain_one,
    shift_one,
    gain_two,
    shift_two,
    cotangent,
):
    seq_count, half_len, model_width = inputs.shape
    group_size = lax.axis_size("seq")
    span_length = half_len * group_size
    head_count = model_width // DH
    scale_factor = 1.0 / math.sqrt(DH)
    row_count = seq_count * half_len
    own_start = lax.axis_index("seq") * half_len
    flat_inputs = inputs.reshape(row_count, model_width)
    query_low = matmul(flat_inputs, a_query).astype(jnp.bfloat16)
    queries = (matmul(flat_inputs, w_query) + 2.0 * matmul(query_low, b_query)).astype(jnp.bfloat16)
    value_low = matmul(flat_inputs, a_value).astype(jnp.bfloat16)
    key_rows = matmul(flat_inputs, w_key).astype(jnp.bfloat16)
    value_rows = (matmul(flat_inputs, w_value) + 2.0 * matmul(value_low, b_value)).astype(
        jnp.bfloat16
    )
    key_all, value_all = (
        lax.all_gather(
            key_rows.reshape(seq_count, half_len, model_width), "seq", axis=1, tiled=True
        ),
        lax.all_gather(
            value_rows.reshape(seq_count, half_len, model_width), "seq", axis=1, tiled=True
        ),
    )
    segments = segment_ids(pair_lengths, span_length)
    own_segments = lax.dynamic_slice_in_dim(segments, own_start, half_len, 1)
    allowed = own_segments[:, :, None] == segments[:, None, :]
    query_heads = queries.reshape(seq_count, half_len, head_count, DH)
    key_heads = key_all.reshape(seq_count, span_length, head_count, DH)
    value_heads = value_all.reshape(seq_count, span_length, head_count, DH)

    def masked_scores():
        raw_scores = jnp.einsum(
            "sqhd,skhd->shqk", query_heads, key_heads, preferred_element_type=jnp.float32
        )
        return jnp.where(allowed[:, None, :, :], raw_scores * scale_factor, -1e30)

    scores = masked_scores()
    row_peak = jnp.max(scores, axis=-1, keepdims=True)
    raised = jnp.exp(scores - row_peak)
    row_total = jnp.sum(raised, axis=-1, keepdims=True)
    weights = raised / row_total
    log_total = row_peak + jnp.log(row_total)
    context = jnp.einsum(
        "shqk,skhd->sqhd",
        weights.astype(jnp.bfloat16),
        value_heads,
        preferred_element_type=jnp.float32,
    )
    context = context.reshape(row_count, model_width).astype(jnp.bfloat16)
    resid_one = flat_inputs.astype(jnp.float32) + matmul(context, w_out)
    hidden_one, pull_one = jax.vjp(norm_rows, resid_one, gain_one, shift_one)
    upward = matmul(hidden_one.astype(jnp.bfloat16), w_up)
    gelu_values, pull_gelu = jax.vjp(gelu_exact, upward)
    active = gelu_values.astype(jnp.bfloat16)
    resid_two = hidden_one + matmul(active, w_down)
    normed_two, pull_two = jax.vjp(norm_rows, resid_two, gain_two, shift_two)
    grad_out = cotangent.reshape(row_count, model_width).astype(jnp.float32)
    grad_resid_two, grad_gain_two, grad_shift_two = pull_two(grad_out)
    grad_active = matmul(grad_resid_two.astype(jnp.bfloat16), w_down.T)
    grad_up = pull_gelu(grad_active)[0].astype(jnp.bfloat16)
    grad_hidden = grad_resid_two + matmul(grad_up, w_up.T)
    grad_resid_one, grad_gain_one, grad_shift_one = pull_one(grad_hidden)
    grad_context = matmul(grad_resid_one.astype(jnp.bfloat16), w_out.T).astype(jnp.bfloat16)
    grad_context_heads = grad_context.reshape(seq_count, half_len, head_count, DH)
    again = jnp.exp(masked_scores() - log_total)
    grad_weights = jnp.einsum(
        "sqhd,skhd->shqk", grad_context_heads, value_heads, preferred_element_type=jnp.float32
    )
    grad_value_all = jnp.einsum(
        "shqk,sqhd->skhd",
        again.astype(jnp.bfloat16),
        grad_context_heads,
        preferred_element_type=jnp.float32,
    )
    inner_sum = jnp.sum(again * grad_weights, axis=-1, keepdims=True)
    grad_scores = (again * (grad_weights - inner_sum)).astype(jnp.bfloat16)
    grad_query = (
        jnp.einsum("shqk,skhd->sqhd", grad_scores, key_heads, preferred_element_type=jnp.float32)
        * scale_factor
    )
    grad_key_all = (
        jnp.einsum("shqk,sqhd->skhd", grad_scores, query_heads, preferred_element_type=jnp.float32)
        * scale_factor
    )
    returned_key, returned_value = (
        lax.psum_scatter(
            grad_key_all.reshape(seq_count, span_length, model_width),
            "seq",
            scatter_dimension=1,
            tiled=True,
        ),
        lax.psum_scatter(
            grad_value_all.reshape(seq_count, span_length, model_width),
            "seq",
            scatter_dimension=1,
            tiled=True,
        ),
    )
    grad_key = returned_key.reshape(row_count, model_width).astype(jnp.bfloat16)
    grad_value = returned_value.reshape(row_count, model_width).astype(jnp.bfloat16)
    grad_query_low = grad_query.reshape(row_count, model_width).astype(jnp.bfloat16)
    grad_qa = (2.0 * matmul(grad_query_low, b_query.T)).astype(jnp.bfloat16)
    grad_va = (2.0 * matmul(grad_value, b_value.T)).astype(jnp.bfloat16)
    grad_inputs = (
        grad_resid_one
        + matmul(grad_query_low, w_query.T)
        + matmul(grad_key, w_key.T)
        + matmul(grad_value, w_value.T)
        + matmul(grad_qa, a_query.T)
        + matmul(grad_va, a_value.T)
    )
    grad_a_query = row_inner(flat_inputs, grad_qa)
    grad_b_query = 2.0 * row_inner(query_low, grad_query_low)
    grad_a_value = row_inner(flat_inputs, grad_va)
    grad_b_value = 2.0 * row_inner(value_low, grad_value)
    summed = lax.psum(
        (
            grad_a_query,
            grad_b_query,
            grad_a_value,
            grad_b_value,
            grad_gain_one,
            grad_shift_one,
            grad_gain_two,
            grad_shift_two,
        ),
        ("dp", "seq"),
    )
    output = normed_two.astype(jnp.bfloat16).reshape(seq_count, half_len, model_width)
    return (
        output,
        grad_inputs.reshape(seq_count, half_len, model_width),
        summed[0],
        summed[1],
        summed[2],
        summed[3],
        summed[4],
        summed[5],
        summed[6],
        summed[7],
    )


def solution(mesh):
    in_specs = (
        P("dp", "seq", None),
        P("dp", None),
        P(),
        P(),
        P(),
        P(),
        P(),
        P(),
        P(),
        P(),
        P(),
        P(),
        P(),
        P(),
        P(),
        P(),
        P("dp", "seq", None),
    )
    out_specs = (P("dp", "seq", None), P("dp", "seq", None), P(), P(), P(), P(), P(), P(), P(), P())
    return jax.shard_map(body, mesh=mesh, in_specs=in_specs, out_specs=out_specs, check_vma=False)
```

profile of v0, /device:TPU:0, one launch (start us, length us, event | category | flops | bytes accessed | tf_op | source)
XLA Modules:
  0.0 384.4 jit_solution(6557806141332048322)
XLA Ops:
  7.3 2.0 fusion.48
  11.5 2.4 all-gather
  15.1 1.7 fusion.45
  19.4 2.5 all-gather.1
  21.9 1.4 copy.41
  23.9 1.3 fusion.71
  25.2 1.6 fusion
  26.8 1.6 copy-done.1
  28.4 2.4 fusion.23
  32.2 1.5 fusion.33
  34.1 8.0 %fusion.73 = (f32[256]{0:T(256)S(1)}, f32[256,768]{1,0:T(8,128)S(1)}) fusion(bf16[3072,768]{1,0:T(8,128)(2,1)S(1)} %bitcast.146, f32[256,3072]{1,0:T(8,128)S(1)} %fusion.33, f32[768]{0:T(1024)S(1)} %copy-done.36, f32[768]{0:T(1024)S(1)} %copy-done.32, f32[256]{0:T(256)S(1)} %fusion.58, f32[256,768]{1,0:T(8,128)S(1)} %get-tuple-element.33, ...), kind=kOutput, calls=%fused_computation.129 | convolution fusion | flops 1260257024 | bytes 9446400 | tf_op jit(solution)/shard_map/dot_general | solution.py:15
  43.0 1.8 fusion.31
  45.3 16.4 %multiply_reduce_fusion.1 = (f32[768]{0:T(1024)}, f32[256]{0:T(256)}, f32[768]{0:T(1024)}, f32[256,768]{1,0:T(8,128)}) fusion(f32[256,768]{1,0:T(8,128)S(1)} %get-tuple-element.33, f32[256]{0:T(256)} %copy-done.33, f32[256]{0:T(256)} %copy-done.28, f32[768]{0:T(1024)} %param.29, bf16[768,3072]{1,0:T(8,128)(2,1)} %param.23, f32[256,3072]{1,0:T(8,128)} %copy-done.38, ...), kind=kOutput, calls=%fused_computation.72 | convolution fusion | flops 2477652224 | bytes 15354880 | tf_op jit(solution)/shard_map/dot_general | solution.py:15
  62.4 1.7 fusion.70
  64.7 1.3 convolution_convert_fusion
  67.2 4.4 %multiply_reduce_fusion = (f32[12,256]{1,0:T(8,128)S(1)}, f32[12,256,512]{2,1,0:T(8,128)S(1)}) fusion(f32[12,256,512]{2,1,0:T(8,128)} %copy-done.1, f32[12,256]{1,0:T(8,128)S(1)} %log_add_fusion, bf16[256,12,64]{0,2,1:T(8,128)(2,1)S(1)} %bitcast.137, bf16[512,12,64]{0,2,1:T(8,128)(2,1)} %bitcast.141), kind=kOutput, calls=%fused_computation.1 | convolution fusion | flops 206042112 | bytes 13787136 | tf_op jit(solution)/shard_map/sqhd,skhd->shqk/dot_general | solution.py:124
  72.1 1.4 multiply_convert_fusion
  73.5 1.7 copy-done.2
  75.2 1.8 convolution_multiply_fusion
  77.4 5.1 %fusion.3 = f32[12,64,512]{2,1,0:T(8,128)} fusion(bf16[256,12,64]{0,2,1:T(8,128)(2,1)S(1)} %bitcast.138, f32[12,256,512]{2,1,0:T(8,128)} %copy-done.1, f32[12,256]{1,0:T(8,128)S(1)} %log_add_fusion), kind=kOutput, calls=%fused_computation.10 | convolution fusion | flops 204472320 | bytes 8269824 | tf_op jit(solution)/shard_map/shqk,sqhd->skhd/dot_general | solution.py:127
  82.6 1.8 convert_reduce_fusion
  84.3 3.4 fusion.20
  89.6 1.4 convolution_add_fusion.4
  91.0 2.3 convolution_add_fusion.3
  93.4 8.1 %reduce-scatter.5.cloned.1.call-done = f32[1,256,768]{1,2,0:T(8,128)} async-done(((f32[1,512,768]{1,2,0:T(8,128)}), f32[1,256,768]{1,2,0:T(8,128)}) %reduce-scatter.5.cloned.1.call-update) | async-done | bytes 786448 | tf_op jit(solution)/shard_map/reduce_scatter | solution.py:150
  101.5 1.7 convolution_add_fusion.2
  106.7 260.7 %all-reduce.3.cloned.1.call-done = (f32[768,8]{0,1:T(8,128)}, f32[8,768]{1,0:T(8,128)}, f32[768,8]{0,1:T(8,128)}, f32[8,768]{1,0:T(8,128)}, f32[768]{0:T(1024)},...) async-done(((f32[768,8]{0,1:T(8,128)}, f32[8,768]{1,0:T(8,128)}, f32[768,8]{0,1:T(8,128)}, f32[8,768]{1,0:T(8,128)}, f32[768]{0:T(1024)}, /*index=5*/f32[768]{0:T(1024)}, ...) | async-done | bytes 110608 | tf_op jit(solution)/shard_map/psum | solution.py:174
  367.4 1.3 copy.51
  368.7 1.3 copy.52
  370.1 1.3 copy.53
  371.4 1.3 copy.54
  372.8 1.3 copy.55
  (132 shorter events, 22.1 us)
Async XLA Ops:
  7.2 23.6 %copy-start = (bf16[768,768]{1,0:T(8,128)(2,1)S(1)}, bf16[768,768]{1,0:T(8,128)(2,1)}, u32[]{:S(2)}) copy-start(bf16[768,768]{1,0:T(8,128)(2,1)} %param.22) | copy-start | bytes 3538948
  7.2 83.9 %reduce-scatter.3.cloned.1.call-start = ((), (), s32[]{:S(2)}) async-start(), calls=%async_computation.2 | async-start | bytes 2359296 | tf_op jit(solution)/shard_map/reduce_scatter | solution.py:144
  7.2 7.9 %copy-start.3 = (bf16[1,256,768]{2,1,0:T(8,128)(2,1)S(1)}, bf16[1,256,768]{2,1,0:T(8,128)(2,1)}, u32[]{:S(2)}) copy-start(bf16[1,256,768]{2,1,0:T(8,128)(2,1)} %param.17) | copy-start | bytes 1179652
  10.4 8.0 %copy-start.14 = (bf16[8,768]{1,0:T(8,128)(2,1)S(1)}, bf16[8,768]{1,0:T(8,128)(2,1)}, u32[]{:S(2)}) copy-start(bf16[8,768]{1,0:T(8,128)(2,1)} %param.26) | copy-start | bytes 36868
  14.0 5.0 %copy-start.6 = (bf16[768,768]{1,0:T(8,128)(2,1)S(1)}, bf16[768,768]{1,0:T(8,128)(2,1)}, u32[]{:S(2)}) copy-start(bf16[768,768]{1,0:T(8,128)(2,1)} %param.20) | copy-start | bytes 3538948
  18.5 4.9 %copy-start.37 = (s32[1,8]{1,0:T(1,128)S(1)}, s32[1,8]{1,0:T(1,128)}, u32[]{:S(2)}) copy-start(s32[1,8]{1,0:T(1,128)} %param.18) | copy-start | bytes 100
  18.9 6.2 %copy-start.10 = (bf16[256,768]{0,1:T(8,128)(2,1)}, bf16[256,768]{0,1:T(8,128)(2,1)S(1)}, u32[]{:S(2)}) copy-start(bf16[256,768]{0,1:T(8,128)(2,1)S(1)} %copy.40) | copy-start | bytes 1179652
  25.2 3.2 copy-start.1
  25.2 3.2 copy-start.13
  25.2 7.0 %slice-start.4 = ((s8[4718592]{0:T(1024)(128)(4,1)}), s8[4194304]{0:T(1024)(128)(4,1)S(1)}, s32[]{:S(2)}) async-start(s8[4718592]{0:T(1024)(128)(4,1)} %bitcast.147), calls=%async_computation.9 | async-start | bytes 8388608
  28.4 3.8 slice-start.5
  31.3 14.0 %copy-start.5 = (f32[256,768]{1,0:T(8,128)}, f32[256,768]{1,0:T(8,128)S(1)}, u32[]{:S(2)}) copy-start(f32[256,768]{1,0:T(8,128)S(1)} %get-tuple-element.33) | copy-start | bytes 2359300
  31.4 2.4 copy-start.28
  31.4 2.5 slice-start.2
  34.1 8.0 %copy-start.38 = (f32[256,3072]{1,0:T(8,128)}, f32[256,3072]{1,0:T(8,128)S(1)}, u32[]{:S(2)}) copy-start(f32[256,3072]{1,0:T(8,128)S(1)} %fusion.33) | copy-start | bytes 9437188
  34.1 8.0 %copy-start.9 = (bf16[1,256,768]{2,1,0:T(8,128)(2,1)S(1)}, bf16[1,256,768]{2,1,0:T(8,128)(2,1)}, u32[]{:S(2)}) copy-start(bf16[1,256,768]{2,1,0:T(8,128)(2,1)} %param.33) | copy-start | bytes 1179652
  34.1 8.0 %copy-start.25 = (f32[768]{0:T(1024)S(1)}, f32[768]{0:T(1024)}, u32[]{:S(2)}) copy-start(f32[768]{0:T(1024)} %param.31) | copy-start | bytes 9220
  34.1 8.8 %copy-start.31 = (f32[768]{0:T(1024)S(1)}, f32[768]{0:T(1024)}, u32[]{:S(2)}) copy-start(f32[768]{0:T(1024)} %param.32) | copy-start | bytes 9220
  42.1 2.7 copy-start.30
  42.5 2.3 copy-start.34
  67.1 4.4 %slice-start = ((s8[6291456]{0:T(1024)(128)(4,1)}), s8[4194304]{0:T(1024)(128)(4,1)S(1)}, s32[]{:S(2)}) async-start(s8[6291456]{0:T(1024)(128)(4,1)} %bitcast.128), calls=%async_computation.5 | async-start | bytes 8388608
  67.1 4.9 %slice-start.1 = ((s8[6291456]{0:T(1024)(128)(4,1)}), s8[2097152]{0:T(1024)(128)(4,1)S(1)}, s32[]{:S(2)}) async-start(s8[6291456]{0:T(1024)(128)(4,1)} %bitcast.128), calls=%async_computation.6 | async-start | bytes 4194304
  72.1 3.1 copy-start.11
  77.1 24.5 %reduce-scatter.5.cloned.1.call-start = ((), (), s32[]{:S(2)}) async-start(), calls=%async_computation.3 | async-start | bytes 2359296 | tf_op jit(solution)/shard_map/reduce_scatter | solution.py:150
  82.5 5.3 %copy-start.15 = (bf16[8,768]{1,0:T(8,128)(2,1)S(1)}, bf16[8,768]{1,0:T(8,128)(2,1)}, u32[]{:S(2)}) copy-start(bf16[8,768]{1,0:T(8,128)(2,1)} %param.26) | copy-start | bytes 36868
  82.5 5.5 %copy-start.22 = (bf16[256,8]{0,1:T(8,128)(2,1)S(1)}, bf16[256,8]{0,1:T(8,128)(2,1)}, u32[]{:S(2)}) copy-start(bf16[256,8]{0,1:T(8,128)(2,1)} %copy-done.21) | copy-start | bytes 12292
  82.5 7.1 %copy-start.27 = (f32[256]{0:T(256)S(1)}, f32[256]{0:T(256)}, u32[]{:S(2)}) copy-start(f32[256]{0:T(256)} %copy-done.26) | copy-start | bytes 3076
  82.5 284.8 %all-reduce.3.cloned.1.call-start = ((), (), s32[]{:S(2)}) async-start(), calls=%async_computation.4 | async-start | bytes 229376 | tf_op jit(solution)/shard_map/psum | solution.py:174
  82.6 7.1 %copy-start.8 = (bf16[768,768]{1,0:T(8,128)(2,1)S(1)}, bf16[768,768]{1,0:T(8,128)(2,1)}, u32[]{:S(2)}) copy-start(bf16[768,768]{1,0:T(8,128)(2,1)} %param.19) | copy-start | bytes 3538948
  91.0 10.5 %copy-start.7 = (bf16[768,768]{1,0:T(8,128)(2,1)S(1)}, bf16[768,768]{1,0:T(8,128)(2,1)}, u32[]{:S(2)}) copy-start(bf16[768,768]{1,0:T(8,128)(2,1)} %param.21) | copy-start | bytes 3538948
  91.0 12.2 %copy-start.16 = (bf16[768,8]{0,1:T(8,128)(2,1)S(1)}, bf16[768,8]{0,1:T(8,128)(2,1)}, u32[]{:S(2)}) copy-start(bf16[768,8]{0,1:T(8,128)(2,1)} %param.25) | copy-start | bytes 36868
  93.4 11.2 %copy-start.20 = (bf16[256,8]{0,1:T(8,128)(2,1)S(1)}, bf16[256,8]{0,1:T(8,128)(2,1)}, u32[]{:S(2)}) copy-start(bf16[256,8]{0,1:T(8,128)(2,1)} %copy-done.19) | copy-start | bytes 12292
  (16 other events, 23.2 us)
Sparse Core Ops, SparseCore 0:
  77.2 11.6 reduce-scatter.2
  91.2 10.2 reduce-scatter.4
  109.1 258.2 all-reduce.2
where the time goes:
time: 385 us; the launch traced here: 384 us
  waiting for transfers between devices  269 us (70%)
  matrix products  64.3 us (17%)
  local copies, waits for them, and re-layouts  21.1 us (5%)
  between operations  14.3 us (4%)
  other arithmetic  10.5 us (3%)
  blocking collectives  4.95 us (1%)
    psum x1, waiting for transfers between devices, body(): lax.psum((grad_a_query, grad_b_query, grad_a_value, grad_b_value, grad_ga...  261 us
    dot_general x19, matrix products, matmul(): return jnp.dot(former, latter, preferred_element_type=jnp.float32)  42.5 us
    unnamed x98, local copies, waits for them, and re-layouts  17.1 us
    reduce_scatter x1, waiting for transfers between devices, body(): lax.psum_scatter(grad_value_all.reshape(seq_count, span_length, model_wid...  8.13 us
  transfers between devices with their start and end apart: 3, of which 2 were waited for; matrix products, arithmetic and copies ran while one was open for 4% of the time, Pallas kernels for 0%

commit v1 on v0

--- a/solution.py
+++ b/solution.py
@@ -35,6 +35,27 @@
 
 def gelu_exact(values):
     return jax.nn.gelu(values, approximate=False)
+
+
+def swap_and_add(values, axis, partners):
+    size = lax.axis_size(axis)
+    sent = values.astype(jnp.bfloat16)
+    arrived = [
+        lax.ppermute(sent, axis, [(i, i ^ p) for i in range(size)]) for p in partners
+    ]
+    for one in arrived:
+        values = values + one.astype(jnp.float32)
+    return values
+
+
+def sum_everywhere(values):
+    values = swap_and_add(values, "seq", (1,))
+    stride, size = 1, lax.axis_size("dp")
+    while stride < size:
+        radix = min(4, size // stride)
+        values = swap_and_add(values, "dp", [stride * k for k in range(1, radix)])
+        stride *= radix
+    return values
 
 
 def body(
@@ -171,18 +192,23 @@
     grad_b_query = 2.0 * row_inner(query_low, grad_query_low)
     grad_a_value = row_inner(flat_inputs, grad_va)
     grad_b_value = 2.0 * row_inner(value_low, grad_value)
-    summed = lax.psum(
-        (
-            grad_a_query,
+    packed = jnp.concatenate(
+        [
+            grad_a_query.T,
             grad_b_query,
-            grad_a_value,
+            grad_a_value.T,
             grad_b_value,
-            grad_gain_one,
-            grad_shift_one,
-            grad_gain_two,
-            grad_shift_two,
-        ),
-        ("dp", "seq"),
+            grad_gain_one[None],
+            grad_shift_one[None],
+            grad_gain_two[None],
+            grad_shift_two[None],
+        ]
+    )
+    total = sum_everywhere(packed)
+    rank = a_query.shape[1]
+    low, high = total[: 2 * rank], total[2 * rank : 4 * rank]
+    summed = (low[:rank].T, low[rank:], high[:rank].T, high[rank:]) + tuple(
+        total[4 * rank + i] for i in range(4)
     )
     output = normed_two.astype(jnp.bfloat16).reshape(seq_count, half_len, model_width)
     return (

time: 385 us -> 133 us (0.35)
  waiting for transfers between devices: 269 us -> 7.01 us
  starting transfers between devices: 0.38 us -> 9.27 us
    psum x1 -> x0, waiting for transfers between devices: 261 us -> none  [body(): lax.psum((grad_a_query, grad_b_query, grad_a_value, grad_b_value, grad_ga...]
    unnamed x98 -> x104, local copies, waits for them, and re-layouts: 17.1 us -> 6.07 us
    ppermute x0 -> x7, starting transfers between devices: none -> 9.19 us  [swap_and_add(): lax.ppermute(sent, axis, [(i, i ^ p) for i in range(size)])]
    reduce_scatter x1, waiting for transfers between devices: 8.13 us -> 0.01 us  [body(): lax.psum_scatter(grad_value_all.reshape(seq_count, span_length, model_wid...]
    ppermute x0 -> x7, waiting for transfers between devices: none -> 6.98 us  [swap_and_add(): lax.ppermute(sent, axis, [(i, i ^ p) for i in range(size)])]
  transfers between devices with their start and end apart: 3 -> 9, of which waited for: 2 -> 5; matrix products, arithmetic and copies ran while one was open for 4% -> 23% of each run, Pallas kernels for 0% -> 0%
where the time goes in v1:
time: 133 us; the launch traced here: 132 us
  matrix products  65.1 us (49%)
  local copies, waits for them, and re-layouts  18.7 us (14%)
  between operations  14.7 us (11%)
  other arithmetic  12.1 us (9%)
  starting transfers between devices  9.27 us (7%)
  waiting for transfers between devices  7.01 us (5%)
  blocking collectives  4.95 us (4%)
    dot_general x19, matrix products, matmul(): return jnp.dot(former, latter, preferred_element_type=jnp.float32)  43.3 us
    ppermute x7, starting transfers between devices, swap_and_add(): lax.ppermute(sent, axis, [(i, i ^ p) for i in range(size)])  9.19 us
    ppermute x7, waiting for transfers between devices, swap_and_add(): lax.ppermute(sent, axis, [(i, i ^ p) for i in range(size)])  6.98 us
    unnamed x104, local copies, waits for them, and re-layouts  6.07 us
    dot_general x1, matrix products, body(): jnp.einsum('shqk,sqhd->skhd', again.astype(jnp.bfloat16), grad_context_he...  5.1 us
    dot_general x1, matrix products, body(): jnp.einsum('sqhd,skhd->shqk', grad_context_heads, value_heads, preferred_...  4.47 us
    dot_general x4, matrix products, row_inner(): lax.dot_general(former, latter, (((0,), (0,)), ((), ())), preferred_eleme...  3.84 us
    reshape x4, local copies, waits for them, and re-layouts, norm_rows(): return centred * lax.rsqrt(variance + norm_epsilon) * gain_vec + shift_vec  3.82 us
  transfers between devices with their start and end apart: 9, of which 5 were waited for; matrix products, arithmetic and copies ran while one was open for 23% of the time, Pallas kernels for 0%

profile of v1, /device:TPU:0, one launch (start us, length us, event | category | flops | bytes accessed | tf_op | source)
XLA Modules:
  0.0 131.8 jit_solution(15782223200083241342)
XLA Ops:
  7.3 2.0 %fusion.50 = f32[256,768]{1,0:T(8,128)S(1)} fusion(bf16[768,768]{1,0:T(8,128)(2,1)} %param.21, bf16[1,256,768]{2,1,0:T(8,128)(2,1)} %param.17), kind=kOutput, calls=%fused_computation.95 | convolution fusion | flops 301989888 | bytes 2359296 | tf_op jit(solution)/shard_map/dot_general | solution.py:15
  11.5 2.4 %all-gather = bf16[512,768]{1,0:T(8,128)(2,1)S(1)} all-gather(bf16[256,768]{1,0:T(8,128)(2,1)S(1)} %fusion.21), channel_id=2, replica_groups=mesh['dp'=16,'seq'=2] {'seq'}, dimensions={0}, use_global_device_ids=true | all-gather | bytes 1179648 | tf_op jit(solution)/shard_map/all_gather | solution.py:99
  15.1 1.7 %fusion.47 = f32[256,768]{1,0:T(8,128)S(1)} fusion(bf16[768,768]{1,0:T(8,128)(2,1)} %param.19, bf16[1,256,768]{2,1,0:T(8,128)(2,1)S(1)} %copy-done.3), kind=kOutput, calls=%fused_computation.92 | convolution fusion | flops 301989888 | bytes 2359296 | tf_op jit(solution)/shard_map/dot_general | solution.py:15
  19.5 1.9 %copy.40 = bf16[256,768]{0,1:T(8,128)(2,1)} copy(bf16[256,768]{1,0:T(8,128)(2,1)} %fusion.22) | data formatting | bytes 786432 | tf_op jit(solution)/shard_map/convert_element_type | solution.py:89
  21.9 2.5 %all-gather.1 = bf16[512,768]{1,0:T(8,128)(2,1)S(1)} all-gather(bf16[256,768]{1,0:T(8,128)(2,1)S(1)} %convolution_convert_fusion.1), channel_id=3, replica_groups=mesh['dp'=16,'seq'=2] {'seq'}, dimensions={0}, use_global_device_ids=true | all-gather | bytes 1179648 | tf_op jit(solution)/shard_map/all_gather | solution.py:96
  25.2 1.3 fusion.76
  26.5 1.6 %fusion = f32[12,256]{1,0:T(8,128)S(1)} fusion(f32[12,256,512]{2,1,0:T(8,128)S(1)} %get-tuple-element.31, f32[12,256]{1,0:T(8,128)S(1)} %get-tuple-element.30), kind=kLoop, calls=%fused_computation.6 | loop fusion | flops 3142656 | bytes 6316032 | tf_op jit(solution)/shard_map/reduce_sum | solution.py:119
  28.1 1.6 %copy-done.1 = f32[12,256,512]{2,1,0:T(8,128)} copy-done((f32[12,256,512]{2,1,0:T(8,128)}, f32[12,256,512]{2,1,0:T(8,128)S(1)}, u32[]{:S(2)}) %copy-start.1) | copy-done | bytes 6291480
  29.7 2.4 %fusion.23 = bf16[12,64,256]{2,1,0:T(8,128)(2,1)S(1)} fusion(bf16[512,12,64]{0,2,1:T(8,128)(2,1)S(1)} %bitcast.140, f32[12,256,512]{2,1,0:T(8,128)S(1)} %get-tuple-element.31, f32[12,256]{1,0:T(8,128)S(1)} %fusion, f32[12,256]{1,0:T(8,128)S(1)} %get-tuple-element.30), kind=kOutput, calls=%fused_computation.51 | convolution fusion | flops 206241792 | bytes 7495680 | tf_op jit(solution)/shard_map/shqk,skhd->sqhd/dot_general | solution.py:122
  33.6 1.5 %fusion.33 = f32[256,3072]{1,0:T(8,128)S(1)} fusion(bf16[768,3072]{1,0:T(8,128)(2,1)S(1)} %bitcast.146, f32[256,768]{1,0:T(8,128)S(1)} %get-tuple-element.33, f32[768]{0:T(1024)S(1)} %copy-done.45, f32[768]{0:T(1024)S(1)} %copy-done.41, f32[256]{0:T(256)S(1)} %fusion.61, f32[256]{0:T(256)S(1)} %broadcast_multiply_fusion.1), kind=kOutput, calls=%fused_computation.79 | convolution fusion | flops 1208942592 | bytes 8658944 | tf_op jit(solution)/shard_map/dot_general | solution.py:15
  35.5 8.0 %fusion.78 = (f32[256]{0:T(256)S(1)}, f32[256,768]{1,0:T(8,128)S(1)}) fusion(bf16[3072,768]{1,0:T(8,128)(2,1)S(1)} %bitcast.144, f32[256,3072]{1,0:T(8,128)S(1)} %fusion.33, f32[768]{0:T(1024)S(1)} %copy-done.45, f32[768]{0:T(1024)S(1)} %copy-done.41, f32[256]{0:T(256)S(1)} %fusion.61, f32[256,768]{1,0:T(8,128)S(1)} %get-tuple-element.33, ...), kind=kOutput, calls=%fused_computation.141 | convolution fusion | flops 1260257024 | bytes 9446400 | tf_op jit(solution)/shard_map/dot_general | solution.py:15
  44.3 1.8 %fusion.31 = (f32[768]{0:T(1024)}, f32[256]{0:T(256)S(1)}, bf16[1,256,768]{2,1,0:T(8,128)(2,1)}) fusion(bf16[1,256,768]{2,1,0:T(8,128)(2,1)S(1)} %copy-done.9, f32[256,768]{1,0:T(8,128)S(1)} %get-tuple-element.35, f32[256]{0:T(256)S(1)} %get-tuple-element.29, f32[256]{0:T(256)S(1)} %broadcast_multiply_fusion, f32[256]{0:T(256)S(1)} %get-tuple-element.28, ...), kind=kLoop, calls=%fused_computation.69 | loop fusion | flops 2751488 | bytes 1586176 | tf_op jit(solution)/shard_map/transpose(jvp())/reduce_sum | solution.py:33
  46.7 16.4 %multiply_reduce_fusion.1 = (f32[768]{0:T(1024)}, f32[256]{0:T(256)}, f32[768]{0:T(1024)}, f32[256,768]{1,0:T(8,128)}) fusion(f32[256,768]{1,0:T(8,128)S(1)} %get-tuple-element.33, f32[256]{0:T(256)} %copy-done.42, f32[256]{0:T(256)} %copy-done.37, f32[768]{0:T(1024)} %param.29, bf16[768,3072]{1,0:T(8,128)(2,1)} %param.23, f32[256,3072]{1,0:T(8,128)} %copy-done.47, ...), kind=kOutput, calls=%fused_computation.70 | convolution fusion | flops 2477652224 | bytes 15354880 | tf_op jit(solution)/shard_map/dot_general | solution.py:15
  63.7 1.7 %fusion.74 = (f32[256]{0:T(256)S(1)}, f32[256,768]{1,0:T(8,128)S(1)}) fusion(f32[256]{0:T(256)S(1)} %multiply_multiply_fusion.5, f32[256,768]{1,0:T(8,128)} %copy-done.5, f32[256]{0:T(256)} %copy-done.37, f32[256]{0:T(256)} %copy-done.42, f32[256,768]{1,0:T(8,128)} %get-tuple-element.36, f32[768]{0:T(1024)} %param.29), kind=kLoop, calls=%fused_computation.137 | loop fusion | flops 1376000 | bytes 2366464 | tf_op jit(solution)/shard_map/transpose(jvp())/reduce_sum | solution.py:31
  66.0 1.3 convolution_convert_fusion
  68.5 5.1 %fusion.3 = f32[12,64,512]{2,1,0:T(8,128)} fusion(bf16[256,12,64]{0,2,1:T(8,128)(2,1)S(1)} %bitcast.135, f32[12,256,512]{2,1,0:T(8,128)} %copy-done.1, f32[12,256]{1,0:T(8,128)S(1)} %log_add_fusion), kind=kOutput, calls=%fused_computation.10 | convolution fusion | flops 204472320 | bytes 8269824 | tf_op jit(solution)/shard_map/shqk,sqhd->skhd/dot_general | solution.py:148
  73.7 4.5 %multiply_reduce_fusion = (f32[12,256]{1,0:T(8,128)S(1)}, f32[12,256,512]{2,1,0:T(8,128)S(1)}) fusion(f32[12,256,512]{2,1,0:T(8,128)} %copy-done.1, f32[12,256]{1,0:T(8,128)S(1)} %log_add_fusion, bf16[256,12,64]{0,2,1:T(8,128)(2,1)S(1)} %bitcast.136, bf16[512,12,64]{0,2,1:T(8,128)(2,1)} %bitcast.139), kind=kOutput, calls=%fused_computation.1 | convolution fusion | flops 206042112 | bytes 13787136 | tf_op jit(solution)/shard_map/sqhd,skhd->shqk/dot_general | solution.py:145
  78.2 3.7 %multiply_convert_fusion = bf16[12,256,512]{2,1,0:T(8,128)(2,1)S(1)} fusion(f32[12,256,512]{2,1,0:T(8,128)S(1)} %get-tuple-element.38, f32[12,256,512]{2,1,0:T(8,128)} %copy-done.1, f32[12,256]{1,0:T(8,128)S(1)} %get-tuple-element.37, f32[12,256]{1,0:T(8,128)S(1)} %log_add_fusion), kind=kLoop, calls=%fused_computation | loop fusion | flops 6291456 | bytes 15753216 | tf_op jit(solution)/shard_map/convert_element_type | solution.py:155
  81.8 1.6 %copy-done.2 = bf16[12,256,512]{2,1,0:T(8,128)(2,1)} copy-done((bf16[12,256,512]{2,1,0:T(8,128)(2,1)}, bf16[12,256,512]{2,1,0:T(8,128)(2,1)S(1)}, u32[]{:S(2)}) %copy-start.2) | copy-done | bytes 3145752
  83.5 1.8 %convolution_multiply_fusion = f32[12,64,512]{2,1,0:T(8,128)} fusion(bf16[256,12,64]{0,2,1:T(8,128)(2,1)S(1)} %bitcast.138, bf16[12,256,512]{2,1,0:T(8,128)(2,1)S(1)} %multiply_convert_fusion), kind=kOutput, calls=%fused_computation.31 | convolution fusion | flops 201719808 | bytes 5111808 | tf_op jit(solution)/shard_map/shqk,sqhd->skhd/dot_general | solution.py:161
  85.3 1.4 %reshape.313 = f32[1,768]{1,0:T(1,128)} reshape(f32[768]{0:T(1024)} %get-tuple-element.10) | data formatting | bytes 6144 | tf_op jit(solution)/shard_map/transpose(jvp())/reshape | solution.py:33
  89.2 3.0 %fusion.20 = bf16[12,64,256]{2,1,0:T(8,128)(2,1)S(1)} fusion(bf16[512,12,64]{0,2,1:T(8,128)(2,1)S(1)} %bitcast.129, bf16[12,256,512]{2,1,0:T(8,128)(2,1)} %copy-done.2), kind=kOutput, calls=%fused_computation.46 | convolution fusion | flops 201719808 | bytes 4325376 | tf_op jit(solution)/shard_map/shqk,skhd->sqhd/dot_general | solution.py:157
  94.1 1.4 %convolution_add_fusion.4 = f32[256,768]{1,0:T(8,128)} fusion(bf16[256,768]{0,1:T(8,128)(2,1)S(1)} %bitcast.133, bf16[768,768]{1,0:T(8,128)(2,1)S(1)} %copy-done.8, f32[256,768]{1,0:T(8,128)S(1)} %get-tuple-element.22, f32[256]{0:T(256)S(1)} %copy-done.36), kind=kOutput, calls=%fused_computation.41 | convolution fusion | flops 302383104 | bytes 3146752 | tf_op jit(solution)/shard_map/dot_general | solution.py:15
  95.5 1.4 %fusion.25 = bf16[256,8]{0,1:T(8,128)(2,1)S(1)} fusion(bf16[8,768]{1,0:T(8,128)(2,1)} %param.28, f32[1,256,768]{1,2,0:T(8,128)} %reduce-scatter.5.cloned.1.call-done), kind=kOutput, calls=%fused_computation.59 | convolution fusion | flops 3346432 | bytes 802816 | tf_op jit(solution)/shard_map/dot_general | solution.py:15
  97.7 1.4 %convolution_multiply_fusion.4 = f32[8,768]{1,0:T(8,128)S(1)} fusion(bf16[256,8]{0,1:T(8,128)(2,1)S(1)} %copy-done.24, f32[1,256,768]{1,2,0:T(8,128)} %reduce-scatter.5.cloned.1.call-done), kind=kOutput, calls=%fused_computation.54 | convolution fusion | flops 3348480 | bytes 815104 | tf_op jit(solution)/shard_map/dot_general | solution.py:19
  99.1 3.0 %concatenate.3 = f32[36,768]{1,0:T(8,128)S(1)} concatenate(f32[8,768]{1,0:T(8,128)} %fusion.43, f32[8,768]{1,0:T(8,128)} %convolution_multiply_fusion.5, f32[8,768]{1,0:T(8,128)} %fusion.41, f32[8,768]{1,0:T(8,128)S(1)} %convolution_multiply_fusion.4, f32[1,768]{1,0:T(1,128)S(1)} %copy-done.33, f32[1,768]{1,0:T(1,128)S(1)} %copy-done.34, f32[1,768]{1,0:T(1,128)} %reshape.315, ...), dimensions={0} | concatenate | bytes 221184 | tf_op jit(solution)/shard_map/concatenate | solution.py:195
  102.6 2.2 %convolution_add_fusion.3 = f32[256,768]{1,0:T(8,128)S(1)} fusion(f32[256,768]{1,0:T(8,128)} %convolution_add_fusion.4, bf16[768,768]{1,0:T(8,128)(2,1)} %param.20, f32[1,256,768]{1,2,0:T(8,128)} %reduce-scatter.3.cloned.1.call-done), kind=kOutput, calls=%fused_computation.40 | convolution fusion | flops 302383104 | bytes 3538944 | tf_op jit(solution)/shard_map/dot_general | solution.py:15
  105.5 3.7 %collective-permute-start.3 = (bf16[36,768]{1,0:T(8,128)(2,1)S(1)}, bf16[36,768]{1,0:T(8,128)(2,1)S(1)}, u32[]{:S(2)}, u32[]{:S(2)}) collective-permute-start(bf16[36,768]{1,0:T(8,128)(2,1)S(1)} %fusion.60), channel_id=1, source_target_pairs={{0,6},{2,4},{4,2},{6,0},{8,14},{10,12},{12,10},{14,8},{16,22},{18,... | collective-permute-start | bytes 165896 | tf_op jit(solution)/shard_map/ppermute | solution.py:44
  110.1 1.6 %collective-permute-done.3 = bf16[36,768]{1,0:T(8,128)(2,1)S(1)} collective-permute-done((bf16[36,768]{1,0:T(8,128)(2,1)S(1)}, bf16[36,768]{1,0:T(8,128)(2,1)S(1)}, u32[]{:S(2)}, u32[]{:S(2)}) %collective-permute-start.3) | collective-permute-done | bytes 55328 | tf_op jit(solution)/shard_map/ppermute | solution.py:44
  111.7 1.7 %collective-permute-done.2 = bf16[36,768]{1,0:T(8,128)(2,1)S(1)} collective-permute-done((bf16[36,768]{1,0:T(8,128)(2,1)S(1)}, bf16[36,768]{1,0:T(8,128)(2,1)S(1)}, u32[]{:S(2)}, u32[]{:S(2)}) %collective-permute-start.2) | collective-permute-done | bytes 55328 | tf_op jit(solution)/shard_map/ppermute | solution.py:44
  114.8 3.7 %collective-permute-start.6 = (bf16[36,768]{1,0:T(8,128)(2,1)S(1)}, bf16[36,768]{1,0:T(8,128)(2,1)S(1)}, u32[]{:S(2)}, u32[]{:S(2)}) collective-permute-start(bf16[36,768]{1,0:T(8,128)(2,1)S(1)} %fusion.70), channel_id=1, source_target_pairs={{0,24},{2,26},{4,28},{6,30},{8,16},{10,18},{12,20},{14,22},{16,8},... | collective-permute-start | bytes 165896 | tf_op jit(solution)/shard_map/ppermute | solution.py:44
  120.9 2.7 %collective-permute-done.5 = bf16[36,768]{1,0:T(8,128)(2,1)S(1)} collective-permute-done((bf16[36,768]{1,0:T(8,128)(2,1)S(1)}, bf16[36,768]{1,0:T(8,128)(2,1)S(1)}, u32[]{:S(2)}, u32[]{:S(2)}) %collective-permute-start.5) | collective-permute-done | bytes 55328 | tf_op jit(solution)/shard_map/ppermute | solution.py:44
  (159 shorter events, 25.5 us)
Async XLA Ops:
  7.2 24.9 %copy-start = (bf16[768,768]{1,0:T(8,128)(2,1)S(1)}, bf16[768,768]{1,0:T(8,128)(2,1)}, u32[]{:S(2)}) copy-start(bf16[768,768]{1,0:T(8,128)(2,1)} %param.22) | copy-start | bytes 3538948
  7.2 88.3 %reduce-scatter.5.cloned.1.call-start = ((), (), s32[]{:S(2)}) async-start(), calls=%async_computation.3 | async-start | bytes 2359296 | tf_op jit(solution)/shard_map/reduce_scatter | solution.py:171
  7.2 7.9 %copy-start.3 = (bf16[1,256,768]{2,1,0:T(8,128)(2,1)S(1)}, bf16[1,256,768]{2,1,0:T(8,128)(2,1)}, u32[]{:S(2)}) copy-start(bf16[1,256,768]{2,1,0:T(8,128)(2,1)} %param.17) | copy-start | bytes 1179652
  10.4 8.0 %copy-start.19 = (bf16[8,768]{1,0:T(8,128)(2,1)S(1)}, bf16[8,768]{1,0:T(8,128)(2,1)}, u32[]{:S(2)}) copy-start(bf16[8,768]{1,0:T(8,128)(2,1)} %param.26) | copy-start | bytes 36868
  14.0 7.4 %copy-start.6 = (bf16[768,768]{1,0:T(8,128)(2,1)S(1)}, bf16[768,768]{1,0:T(8,128)(2,1)}, u32[]{:S(2)}) copy-start(bf16[768,768]{1,0:T(8,128)(2,1)} %param.20) | copy-start | bytes 3538948
  26.5 7.0 %slice-start.2 = ((s8[4718592]{0:T(1024)(128)(4,1)}), s8[4194304]{0:T(1024)(128)(4,1)S(1)}, s32[]{:S(2)}) async-start(s8[4718592]{0:T(1024)(128)(4,1)} %bitcast.145), calls=%async_computation.6 | async-start | bytes 8388608
  32.7 14.0 %copy-start.5 = (f32[256,768]{1,0:T(8,128)}, f32[256,768]{1,0:T(8,128)S(1)}, u32[]{:S(2)}) copy-start(f32[256,768]{1,0:T(8,128)S(1)} %get-tuple-element.33) | copy-start | bytes 2359300
  35.4 8.0 %copy-start.47 = (f32[256,3072]{1,0:T(8,128)}, f32[256,3072]{1,0:T(8,128)S(1)}, u32[]{:S(2)}) copy-start(f32[256,3072]{1,0:T(8,128)S(1)} %fusion.33) | copy-start | bytes 9437188
  35.4 8.0 %copy-start.9 = (bf16[1,256,768]{2,1,0:T(8,128)(2,1)S(1)}, bf16[1,256,768]{2,1,0:T(8,128)(2,1)}, u32[]{:S(2)}) copy-start(bf16[1,256,768]{2,1,0:T(8,128)(2,1)} %param.33) | copy-start | bytes 1179652
  35.5 8.0 %copy-start.31 = (f32[768]{0:T(1024)S(1)}, f32[768]{0:T(1024)}, u32[]{:S(2)}) copy-start(f32[768]{0:T(1024)} %param.31) | copy-start | bytes 9220
  35.5 8.8 %copy-start.40 = (f32[768]{0:T(1024)S(1)}, f32[768]{0:T(1024)}, u32[]{:S(2)}) copy-start(f32[768]{0:T(1024)} %param.32) | copy-start | bytes 9220
  73.6 29.0 %reduce-scatter.3.cloned.1.call-start = ((), (), s32[]{:S(2)}) async-start(), calls=%async_computation.2 | async-start | bytes 2359296 | tf_op jit(solution)/shard_map/reduce_scatter | solution.py:165
  85.3 6.9 %copy-start.20 = (bf16[8,768]{1,0:T(8,128)(2,1)S(1)}, bf16[8,768]{1,0:T(8,128)(2,1)}, u32[]{:S(2)}) copy-start(bf16[8,768]{1,0:T(8,128)(2,1)} %param.26) | copy-start | bytes 36868
  85.3 7.1 %copy-start.26 = (bf16[256,8]{0,1:T(8,128)(2,1)S(1)}, bf16[256,8]{0,1:T(8,128)(2,1)}, u32[]{:S(2)}) copy-start(bf16[256,8]{0,1:T(8,128)(2,1)} %copy-done.25) | copy-start | bytes 12292
  85.3 8.8 %copy-start.8 = (bf16[768,768]{1,0:T(8,128)(2,1)S(1)}, bf16[768,768]{1,0:T(8,128)(2,1)}, u32[]{:S(2)}) copy-start(bf16[768,768]{1,0:T(8,128)(2,1)} %param.19) | copy-start | bytes 3538948
  85.3 8.8 %copy-start.36 = (f32[256]{0:T(256)S(1)}, f32[256]{0:T(256)}, u32[]{:S(2)}) copy-start(f32[256]{0:T(256)} %copy-done.35) | copy-start | bytes 3076
  92.4 6.7 %copy-start.33 = (f32[1,768]{1,0:T(1,128)S(1)}, f32[1,768]{1,0:T(1,128)}, u32[]{:S(2)}) copy-start(f32[1,768]{1,0:T(1,128)} %reshape.313) | copy-start | bytes 9220
  95.5 9.4 %copy-start.7 = (bf16[768,768]{1,0:T(8,128)(2,1)S(1)}, bf16[768,768]{1,0:T(8,128)(2,1)}, u32[]{:S(2)}) copy-start(bf16[768,768]{1,0:T(8,128)(2,1)} %param.21) | copy-start | bytes 3538948
  95.5 9.4 %copy-start.4 = (f32[1,256,768]{1,2,0:T(8,128)S(1)}, f32[1,256,768]{1,2,0:T(8,128)}, u32[]{:S(2)}) copy-start(f32[1,256,768]{1,2,0:T(8,128)} %reduce-scatter.5.cloned.1.call-done) | copy-start | bytes 2359300
  102.1 7.7 %copy-start.21 = (bf16[768,8]{0,1:T(8,128)(2,1)S(1)}, bf16[768,8]{0,1:T(8,128)(2,1)}, u32[]{:S(2)}) copy-start(bf16[768,8]{0,1:T(8,128)(2,1)} %param.25) | copy-start | bytes 36868
  102.1 7.6 %copy-start.30 = (bf16[256,8]{0,1:T(8,128)(2,1)S(1)}, bf16[256,8]{0,1:T(8,128)(2,1)}, u32[]{:S(2)}) copy-start(bf16[256,8]{0,1:T(8,128)(2,1)} %copy-done.29) | copy-start | bytes 12292
  102.2 3.3 %collective-permute-start = (bf16[36,768]{1,0:T(8,128)(2,1)S(1)}, bf16[36,768]{1,0:T(8,128)(2,1)S(1)}, u32[]{:S(2)}, u32[]{:S(2)}) collective-permute-start(bf16[36,768]{1,0:T(8,128)(2,1)S(1)} %convert_element_type.173), channel_id=1, source_target_pairs={{0,1},{1,0},{2,3},{3,2},{4,5},{5,4},{6,7},{7,6},{8,9},{9,8},{10,11... | collective-permute-start | bytes 165896 | tf_op jit(solution)/shard_map/ppermute | solution.py:44
  104.9 14.4 %copy-start.22 = (bf16[768,8]{0,1:T(8,128)(2,1)S(1)}, bf16[768,8]{0,1:T(8,128)(2,1)}, u32[]{:S(2)}) copy-start(bf16[768,8]{0,1:T(8,128)(2,1)} %param.27) | copy-start | bytes 36868
  104.9 14.4 %copy-start.28 = (bf16[256,8]{0,1:T(8,128)(2,1)S(1)}, bf16[256,8]{0,1:T(8,128)(2,1)}, u32[]{:S(2)}) copy-start(bf16[256,8]{0,1:T(8,128)(2,1)} %copy-done.27) | copy-start | bytes 12292
  105.5 18.2 %copy-start.16 = (f32[36,768]{1,0:T(8,128)S(1)}, f32[36,768]{1,0:T(8,128)}, u32[]{:S(2)}) copy-start(f32[36,768]{1,0:T(8,128)} %copy-done.15) | copy-start | bytes 331780
  105.5 6.2 %collective-permute-start.3 = (bf16[36,768]{1,0:T(8,128)(2,1)S(1)}, bf16[36,768]{1,0:T(8,128)(2,1)S(1)}, u32[]{:S(2)}, u32[]{:S(2)}) collective-permute-start(bf16[36,768]{1,0:T(8,128)(2,1)S(1)} %fusion.60), channel_id=1, source_target_pairs={{0,6},{2,4},{4,2},{6,0},{8,14},{10,12},{12,10},{14,8},{16,22},{18,... | collective-permute-start | bytes 165896 | tf_op jit(solution)/shard_map/ppermute | solution.py:44
  109.1 4.2 %collective-permute-start.2 = (bf16[36,768]{1,0:T(8,128)(2,1)S(1)}, bf16[36,768]{1,0:T(8,128)(2,1)S(1)}, u32[]{:S(2)}, u32[]{:S(2)}) collective-permute-start(bf16[36,768]{1,0:T(8,128)(2,1)S(1)} %fusion.60), channel_id=1, source_target_pairs={{0,4},{2,6},{4,0},{6,2},{8,12},{10,14},{12,8},{14,10},{16,20},{18,... | collective-permute-start | bytes 165896 | tf_op jit(solution)/shard_map/ppermute | solution.py:44
  109.7 4.2 %collective-permute-start.1 = (bf16[36,768]{1,0:T(8,128)(2,1)S(1)}, bf16[36,768]{1,0:T(8,128)(2,1)S(1)}, u32[]{:S(2)}, u32[]{:S(2)}) collective-permute-start(bf16[36,768]{1,0:T(8,128)(2,1)S(1)} %fusion.60), channel_id=1, source_target_pairs={{0,2},{2,0},{4,6},{6,4},{8,10},{10,8},{12,14},{14,12},{16,18},{18,... | collective-permute-start | bytes 165896 | tf_op jit(solution)/shard_map/ppermute | solution.py:44
  109.8 13.9 %copy-start.18 = (bf16[36,768]{1,0:T(8,128)(2,1)S(1)}, bf16[36,768]{1,0:T(8,128)(2,1)}, u32[]{:S(2)}) copy-start(bf16[36,768]{1,0:T(8,128)(2,1)} %copy-done.17) | copy-start | bytes 165892
  114.8 6.1 %collective-permute-start.6 = (bf16[36,768]{1,0:T(8,128)(2,1)S(1)}, bf16[36,768]{1,0:T(8,128)(2,1)S(1)}, u32[]{:S(2)}, u32[]{:S(2)}) collective-permute-start(bf16[36,768]{1,0:T(8,128)(2,1)S(1)} %fusion.70), channel_id=1, source_target_pairs={{0,24},{2,26},{4,28},{6,30},{8,16},{10,18},{12,20},{14,22},{16,8},... | collective-permute-start | bytes 165896 | tf_op jit(solution)/shard_map/ppermute | solution.py:44
  118.5 5.1 %collective-permute-start.5 = (bf16[36,768]{1,0:T(8,128)(2,1)S(1)}, bf16[36,768]{1,0:T(8,128)(2,1)S(1)}, u32[]{:S(2)}, u32[]{:S(2)}) collective-permute-start(bf16[36,768]{1,0:T(8,128)(2,1)S(1)} %fusion.70), channel_id=1, source_target_pairs={{0,16},{2,18},{4,20},{6,22},{8,24},{10,26},{12,28},{14,30},{16,0},... | collective-permute-start | bytes 165896 | tf_op jit(solution)/shard_map/ppermute | solution.py:44
  118.5 5.1 %collective-permute-start.4 = (bf16[36,768]{1,0:T(8,128)(2,1)S(1)}, bf16[36,768]{1,0:T(8,128)(2,1)S(1)}, u32[]{:S(2)}, u32[]{:S(2)}) collective-permute-start(bf16[36,768]{1,0:T(8,128)(2,1)S(1)} %fusion.70), channel_id=1, source_target_pairs={{0,8},{2,10},{4,12},{6,14},{8,0},{10,2},{12,4},{14,6},{16,24},{18,... | collective-permute-start | bytes 165896 | tf_op jit(solution)/shard_map/ppermute | solution.py:44
  (29 other events, 85.3 us)
Sparse Core Ops, SparseCore 0:
  73.7 11.6 reduce-scatter.4
  87.8 10.2 reduce-scatter.2

commit v2 on v1

v2 whole, which is shorter than its diff:
```python
import functools
import math

import jax
import jax.numpy as jnp
from jax import lax
from jax.experimental import pallas as pl
from jax.experimental.pallas import tpu as pltpu
from jax.sharding import PartitionSpec as P

DH = 64
LANES = 128
EPSILON = 1e-05
LOG2_E = math.log2(math.e)
FAR_AWAY = -1e30
BF16 = jnp.bfloat16
F32 = jnp.float32
NN = ((1,), (0,))
NT = ((1,), (1,))
TN = ((0,), (0,))
TT = ((0,), (1,))


def dot(former, latter, dims=NN):
    return lax.dot_general(former, latter, (dims, ((), ())), preferred_element_type=F32)


def normed(values):
    centred = values - jnp.mean(values, axis=-1, keepdims=True)
    variance = jnp.mean(centred * centred, axis=-1, keepdims=True)
    inverse = lax.rsqrt(variance + EPSILON)
    return centred * inverse, inverse


def norm_back(grad, normal, inverse):
    return inverse * (
        grad
        - jnp.mean(grad, axis=-1, keepdims=True)
        - normal * jnp.mean(grad * normal, axis=-1, keepdims=True)
    )


def gelu_and_slope(values):
    size = jnp.abs(values)
    inv = 1.0 / (1.0 + (0.3275911 / math.sqrt(2.0)) * size)
    bell = jnp.exp2(values * values * (-0.5 * LOG2_E))
    tail = inv * (
        0.5 * 0.254829592
        + inv
        * (
            0.5 * -0.284496736
            + inv * (0.5 * 1.421413741 + inv * (0.5 * -1.453152027 + inv * (0.5 * 1.061405429)))
        )
    )
    tail = tail * bell
    below = jnp.where(values < 0.0, tail, 1.0 - tail)
    return values * below, below + values * bell * (1.0 / math.sqrt(2.0 * math.pi))


def segment_codes(lengths_ref, start_near, start_far, rows):
    row = lax.broadcasted_iota(jnp.int32, (rows, LANES), 0)
    half = rows // 2
    place = jnp.where(row < half, start_near + row, start_far + row - half)
    segment = jnp.zeros_like(place)
    end = jnp.int32(0)
    for pair in range(lengths_ref.shape[1]):
        end = end + lengths_ref[0, pair]
        segment = segment + (place >= end).astype(jnp.int32)
    return segment


def crosses_widely(lengths_ref, middle, half):
    end = jnp.int32(0)
    left = jnp.int32(middle)
    right = jnp.int32(middle)
    for pair in range(lengths_ref.shape[1]):
        end = end + lengths_ref[0, pair]
        left = jnp.where(end < middle, middle - end, left)
        right = jnp.where(end >= middle, jnp.minimum(right, end - middle), right)
    return (right > 0) & ((left > half) | (right > half))


def layer_kernel(
    lengths_ref,
    x_hbm,
    other_hbm,
    wq_hbm,
    wk_hbm,
    wv_hbm,
    wo_hbm,
    wu_hbm,
    wd_hbm,
    small_hbm,
    gains_hbm,
    cot_hbm,
    out_hbm,
    gr_hbm,
    dqt_hbm,
    dk_hbm,
    dv_hbm,
    packed_ref,
    x_s,
    wq,
    wk,
    wv,
    wo,
    wu,
    wd,
    small,
    gains,
    cot_s,
    q_s,
    k_s,
    v_s,
    kt_s,
    vt_s,
    po_s,
    ph_s,
    inv_s,
    ct_s,
    normal_s,
    rstd_s,
    hidden_s,
    active_s,
    slope_s,
    total_s,
    out_s,
    gr_s,
    dot_s,
    dqt_s,
    dk_s,
    dv_s,
    sems,
):
    tokens, width = x_hbm.shape[1:]
    half = tokens // 2
    hidden = wu_hbm.shape[1]
    rank = small_hbm.shape[0] // 4
    heads = width // DH
    side = lax.axis_index("seq")
    near = pl.multiple_of((1 - side) * half, half)
    far = pl.multiple_of(side * half, half)

    copies = []

    def fetch(source, target):
        copy = pltpu.make_async_copy(source, target, sems.at[len(copies)])
        copies.append(copy)
        copy.start()
        return copy

    get_x = [
        fetch(x_hbm.at[0, pl.ds(near, half)], x_s.at[pl.ds(0, half)]),
        fetch(x_hbm.at[0, pl.ds(far, half)], x_s.at[pl.ds(half, half)]),
        fetch(other_hbm.at[0, pl.ds(far, half)], x_s.at[pl.ds(tokens, half)]),
        fetch(other_hbm.at[0, pl.ds(near, half)], x_s.at[pl.ds(tokens + half, half)]),
        fetch(small_hbm, small),
    ]
    get_q = fetch(wq_hbm, wq)
    get_k = fetch(wk_hbm, wk)
    get_v = fetch(wv_hbm, wv)
    get_o = fetch(wo_hbm, wo)
    get_gains = fetch(gains_hbm, gains)
    chunks = hidden // width
    get_u, get_d = [], []
    for c in range(chunks):
        get_u.append(
            fetch(wu_hbm.at[:, pl.ds(c * width, width)], wu.at[:, pl.ds(c * width, width)])
        )
        get_d.append(fetch(wd_hbm.at[pl.ds(c * width, width)], wd.at[pl.ds(c * width, width)]))
    get_cot = [
        fetch(cot_hbm.at[0, pl.ds(near, half)], cot_s.at[pl.ds(0, half)]),
        fetch(cot_hbm.at[0, pl.ds(far, half)], cot_s.at[pl.ds(half, half)]),
    ]

    wide = crosses_widely(lengths_ref, tokens, half)
    own_segment = segment_codes(lengths_ref, side * tokens + near, side * tokens + far, tokens)
    halo_base = (1 - side) * tokens
    halo_segment = segment_codes(lengths_ref, halo_base + far, halo_base + near, tokens)
    lane = lax.broadcasted_iota(jnp.int32, (tokens, LANES), 1)
    code = lane & (DH - 1)
    low_half = lane < DH
    marks = lengths_ref.shape[1] + 1
    q_code = jnp.where(code == own_segment, 1.0, 0.0).astype(BF16)

    def key_code(segment):
        return jnp.where((code < marks) & (code != segment), FAR_AWAY, 0.0).astype(BF16)

    ko_code = key_code(own_segment)
    kh_code = key_code(halo_segment)

    for copy in get_x:
        copy.wait()
    narrow = tokens + half
    aqt, bq = small[pl.ds(0, rank)], small[pl.ds(rank, rank)]
    avt, bv = small[pl.ds(2 * rank, rank)], small[pl.ds(3 * rank, rank)]
    x_all = x_s[pl.ds(0, narrow)]
    x_own = x_s[pl.ds(0, tokens)]
    qlow_t = dot(aqt, x_own, NT).astype(BF16)
    vlow_t = dot(avt, x_s[...], NT).astype(BF16)
    get_q.wait()
    q_s[...] = (
        (dot(x_own, wq[...]) + 2.0 * dot(qlow_t, bq, TN)) * (LOG2_E / math.sqrt(DH))
    ).astype(BF16)
    get_k.wait()
    keys = dot(x_all, wk[...]).astype(BF16)
    k_s[pl.ds(0, narrow)] = keys
    kt_s[:, pl.ds(0, narrow)] = keys.T
    get_v.wait()
    vals = (dot(x_all, wv[...]) + 2.0 * dot(vlow_t[:, :narrow], bv, TN)).astype(BF16)
    v_s[pl.ds(0, narrow)] = vals
    vt_s[:, pl.ds(0, narrow)] = vals.T

    @pl.when(wide)
    def _():
        x_far = x_s[pl.ds(narrow, half)]
        keys = dot(x_far, wk[...]).astype(BF16)
        k_s[pl.ds(narrow, half)] = keys
        kt_s[:, pl.ds(narrow, half)] = keys.T
        vals = (dot(x_far, wv[...]) + 2.0 * dot(vlow_t[:, narrow:], bv, TN)).astype(BF16)
        v_s[pl.ds(narrow, half)] = vals
        vt_s[:, pl.ds(narrow, half)] = vals.T

    def joined(own, halo, reach, join):
        if reach == tokens:
            return join(own, halo)
        return jnp.concatenate([join(own[:, :reach], halo), own[:, reach:]], axis=1)

    def attend(pair, reach):
        lanes = pl.ds(pl.multiple_of(pair * LANES, LANES), LANES)
        q_pair = q_s[:, lanes]
        ko_pair = k_s[pl.ds(0, tokens), lanes]
        kh_pair = k_s[pl.ds(tokens, reach), lanes]
        for odd in range(2):
            head = 2 * pair + odd
            rows = pl.ds(pl.multiple_of(head * DH, DH), DH)

            def mixed(values, codes):
                mask = low_half[: values.shape[0]]
                if odd:
                    return jnp.where(mask, codes, values)
                return jnp.where(mask, values, codes)

            q_head = mixed(q_pair, q_code)
            own = dot(mixed(ko_pair, ko_code), q_head, NT)
            halo = dot(mixed(kh_pair, kh_code[:reach]), q_head[:reach], NT)
            peak = joined(
                jnp.max(own, axis=0, keepdims=True),
                jnp.max(halo, axis=0, keepdims=True),
                reach,
                jnp.maximum,
            )
            own = jnp.exp2(own - peak)
            halo = jnp.exp2(halo - peak[:, :reach])
            inverse = 1.0 / joined(
                jnp.sum(own, axis=0, keepdims=True),
                jnp.sum(halo, axis=0, keepdims=True),
                reach,
                jnp.add,
            )
            own, halo = own.astype(BF16), halo.astype(BF16)
            po_s[head] = own
            ph_s[head, pl.ds(0, reach), pl.ds(0, reach)] = halo
            inv_s[head] = jnp.broadcast_to(inverse, inv_s.shape[1:])
            context = joined(
                dot(vt_s[rows, pl.ds(0, tokens)], own),
                dot(vt_s[rows, pl.ds(tokens, reach)], halo),
                reach,
                jnp.add,
            )
            ct_s[rows, :] = (context * inverse).astype(BF16)

    def attend_back(pair, reach):
        lanes = pl.ds(pl.multiple_of(pair * LANES, LANES), LANES)
        q_pair = q_s[:, lanes]
        vo_pair = v_s[pl.ds(0, tokens), lanes]
        vh_pair = v_s[pl.ds(tokens, reach), lanes]
        dv_own, dv_halo, dk_own, dk_halo = [], [], [], []
        for odd in range(2):
            head = 2 * pair + odd
            rows = pl.ds(pl.multiple_of(head * DH, DH), DH)
            inverse = inv_s[head, pl.ds(0, 1), :]
            grad = (dot_s[rows, :] * inverse).astype(BF16)
            blank = jnp.zeros_like(grad)
            grad = jnp.concatenate([blank, grad] if odd else [grad, blank], axis=0)
            po, ph = po_s[head], ph_s[head, pl.ds(0, reach), pl.ds(0, reach)]
            own = po.astype(F32) * dot(vo_pair, grad)
            halo = ph.astype(F32) * dot(vh_pair, grad[:, :reach])
            inner = inverse * joined(
                jnp.sum(own, axis=0, keepdims=True),
                jnp.sum(halo, axis=0, keepdims=True),
                reach,
                jnp.add,
            )
            own = (own - po.astype(F32) * inner).astype(BF16)
            halo = (halo - ph.astype(F32) * inner[:, :reach]).astype(BF16)
            dv_own.append(dot(po, grad, NT))
            dv_halo.append(dot(ph, grad[:, :reach], NT))
            dk_own.append(dot(own, q_pair))
            dk_halo.append(dot(halo, q_pair[:reach]))
            dqt = joined(
                dot(kt_s[rows, pl.ds(0, tokens)], own),
                dot(kt_s[rows, pl.ds(tokens, reach)], halo),
                reach,
                jnp.add,
            )
            dqt_s[rows, :] = (dqt * (1.0 / math.sqrt(DH))).astype(BF16)
        unscale = 1.0 / LOG2_E
        dv_s[pl.ds(0, tokens), lanes] = (dv_own[0] + dv_own[1]).astype(BF16)
        dv_s[pl.ds(tokens, reach), lanes] = (dv_halo[0] + dv_halo[1]).astype(BF16)
        dk_s[pl.ds(0, tokens), lanes] = (
            jnp.where(low_half, dk_own[0], dk_own[1]) * unscale
        ).astype(BF16)
        dk_s[pl.ds(tokens, reach), lanes] = (
            jnp.where(low_half[:reach], dk_halo[0], dk_halo[1]) * unscale
        ).astype(BF16)

    def for_pairs(step):
        @pl.when(jnp.logical_not(wide))
        def _():
            for pair in range(heads // 2):
                step(pair, half)

        @pl.when(wide)
        def _():
            lax.fori_loop(0, heads // 2, lambda pair, none: step(pair, tokens), None)

    for_pairs(attend)

    get_o.wait()
    get_gains.wait()
    resid_one = x_own.astype(F32) + dot(ct_s[...], wo[...], TN)
    normal, inverse = normed(resid_one)
    normal_s[...] = normal
    rstd_s[...] = jnp.broadcast_to(inverse, rstd_s.shape)
    gain_one, shift_one = gains[pl.ds(0, 1), :], gains[pl.ds(1, 1), :]
    gain_two, shift_two = gains[pl.ds(2, 1), :], gains[pl.ds(3, 1), :]
    hidden_one = normal * gain_one + shift_one
    hidden_s[...] = hidden_one.astype(BF16)
    total_s[...] = hidden_one
    for c in range(chunks):
        part = pl.ds(c * width, width)
        get_u[c].wait()
        upward = dot(hidden_s[...], wu[:, part])
        value, slope = gelu_and_slope(upward)
        active_s[:, part] = value.astype(BF16)
        slope_s[:, part] = slope.astype(BF16)
        get_d[c].wait()
        total_s[...] += dot(active_s[:, part], wd[part, :])
    normal_two, inverse_two = normed(total_s[...])
    out_s[...] = (normal_two * gain_two + shift_two).astype(BF16)

    def put(source, target):
        return fetch(source, target)

    puts = [
        put(out_s.at[pl.ds(0, half)], out_hbm.at[0, pl.ds(near, half)]),
        put(out_s.at[pl.ds(half, half)], out_hbm.at[0, pl.ds(far, half)]),
    ]
    for copy in get_cot:
        copy.wait()
    grad_out = cot_s[...].astype(F32)
    packed_ref[pl.ds(4 * rank + 2, 1), :] = jnp.sum(grad_out * normal_two, axis=0, keepdims=True)
    packed_ref[pl.ds(4 * rank + 3, 1), :] = jnp.sum(grad_out, axis=0, keepdims=True)
    grad_two = norm_back(grad_out * gain_two, normal_two, inverse_two)
    hidden_s[...] = grad_two.astype(BF16)
    total_s[...] = grad_two
    for c in range(chunks):
        part = pl.ds(c * width, width)
        grad_up = slope_s[:, part].astype(F32) * dot(hidden_s[...], wd[part, :], NT)
        active_s[:, part] = grad_up.astype(BF16)
        total_s[...] += dot(active_s[:, part], wu[:, part], NT)
    grad_hidden = total_s[...]
    normal = normal_s[...]
    packed_ref[pl.ds(4 * rank, 1), :] = jnp.sum(grad_hidden * normal, axis=0, keepdims=True)
    packed_ref[pl.ds(4 * rank + 1, 1), :] = jnp.sum(grad_hidden, axis=0, keepdims=True)
    grad_one = norm_back(grad_hidden * gain_one, normal, rstd_s[:, :1])
    gr_s[...] = grad_one
    puts.append(put(gr_s, gr_hbm))
    dot_s[...] = dot(wo[...], grad_one.astype(BF16), NT)

    @pl.when(jnp.logical_not(wide))
    def _():
        dk_s[pl.ds(narrow, half)] = jnp.zeros((half, width), BF16)
        dv_s[pl.ds(narrow, half)] = jnp.zeros((half, width), BF16)

    for_pairs(attend_back)

    puts.append(put(dqt_s, dqt_hbm))
    puts.append(put(dk_s, dk_hbm))
    puts.append(put(dv_s, dv_hbm))
    grad_qlow_t = (2.0 * dot(bq, dqt_s[...])).astype(BF16)
    packed_ref[pl.ds(0, rank), :] = dot(grad_qlow_t, x_own)
    packed_ref[pl.ds(rank, rank), :] = 2.0 * dot(qlow_t, dqt_s[...], NT)
    grad_vlow_t = (2.0 * dot(bv, dv_s[...], NT)).astype(BF16)
    packed_ref[pl.ds(2 * rank, rank), :] = dot(grad_vlow_t, x_s[...])
    packed_ref[pl.ds(3 * rank, rank), :] = 2.0 * dot(vlow_t, dv_s[...])
    spare = packed_ref.shape[0] - 4 * rank - 4
    packed_ref[pl.ds(4 * rank + 4, spare), :] = jnp.zeros((spare, width), F32)
    for copy in puts:
        copy.wait()


def call_layer(lengths, x, other, weights, small, gains, cotangent):
    wq, wk, wv, wo, wu, wd = weights
    _, tokens, width = x.shape
    hidden = wu.shape[1]
    heads = width // DH
    rank = small.shape[0] // 4
    packed_rows = -(-(4 * rank + 4) // 16) * 16
    hbm = pl.BlockSpec(memory_space=pltpu.HBM)
    shape = jax.ShapeDtypeStruct
    vmem = pltpu.VMEM
    return pl.pallas_call(
        layer_kernel,
        out_shape=(
            shape((1, tokens, width), BF16),
            shape((tokens, width), F32),
            shape((width, tokens), BF16),
            shape((2 * tokens, width), BF16),
            shape((2 * tokens, width), BF16),
            shape((packed_rows, width), F32),
        ),
        in_specs=[pl.BlockSpec(memory_space=pltpu.SMEM)] + [hbm] * 11,
        out_specs=(hbm,) * 5 + (pl.BlockSpec(memory_space=pltpu.VMEM),),
        scratch_shapes=[
            vmem((2 * tokens, width), BF16),
            vmem(wq.shape, BF16),
            vmem(wk.shape, BF16),
            vmem(wv.shape, BF16),
            vmem(wo.shape, BF16),
            vmem(wu.shape, BF16),
            vmem(wd.shape, BF16),
            vmem(small.shape, BF16),
            vmem(gains.shape, F32),
            vmem((tokens, width), BF16),
            vmem((tokens, width), BF16),
            vmem((2 * tokens, width), BF16),
            vmem((2 * tokens, width), BF16),
            vmem((width, 2 * tokens), BF16),
            vmem((width, 2 * tokens), BF16),
            vmem((heads, tokens, tokens), BF16),
            vmem((heads, tokens, tokens), BF16),
            vmem((heads, 8, tokens), F32),
            vmem((width, tokens), BF16),
            vmem((tokens, width), F32),
            vmem((tokens, LANES), F32),
            vmem((tokens, width), BF16),
            vmem((tokens, hidden), BF16),
            vmem((tokens, hidden), BF16),
            vmem((tokens, width), F32),
            vmem((tokens, width), BF16),
            vmem((tokens, width), F32),
            vmem((width, tokens), F32),
            vmem((width, tokens), BF16),
            vmem((2 * tokens, width), BF16),
            vmem((2 * tokens, width), BF16),
            pltpu.SemaphoreType.DMA((32,)),
        ],
        compiler_params=pltpu.CompilerParams(vmem_limit_bytes=60 * 2**20),
    )(lengths, x, other, wq, wk, wv, wo, wu, wd, small, gains, cotangent)


def inputs_kernel(
    gr_ref, dqt_ref, dk_ref, dv_ref, hk_ref, hv_ref, wq, wk, wv, small, out_hbm, out_s, sems
):
    tokens, width = gr_ref.shape
    half = tokens // 2
    rank = small.shape[0] // 4
    side = lax.axis_index("seq")
    near = pl.multiple_of((1 - side) * half, half)
    far = pl.multiple_of(side * half, half)
    aqt, bq = small[pl.ds(0, rank)], small[pl.ds(rank, rank)]
    avt, bv = small[pl.ds(2 * rank, rank)], small[pl.ds(3 * rank, rank)]
    dqt = dqt_ref[...]
    dk = (dk_ref[...].astype(F32) + hk_ref[...].astype(F32)).astype(BF16)
    dv = (dv_ref[...].astype(F32) + hv_ref[...].astype(F32)).astype(BF16)
    grad_qlow_t = (2.0 * dot(bq, dqt)).astype(BF16)
    grad_vlow_t = (2.0 * dot(bv, dv, NT)).astype(BF16)
    out_s[...] = (
        gr_ref[...]
        + dot(dqt, wq[...], TT)
        + dot(dk, wk[...], NT)
        + dot(dv, wv[...], NT)
        + dot(grad_qlow_t, aqt, TN)
        + dot(grad_vlow_t, avt, TN)
    )
    puts = [
        pltpu.make_async_copy(
            out_s.at[pl.ds(0, half)], out_hbm.at[0, pl.ds(near, half)], sems.at[0]
        ),
        pltpu.make_async_copy(
            out_s.at[pl.ds(half, half)], out_hbm.at[0, pl.ds(far, half)], sems.at[1]
        ),
    ]
    for copy in puts:
        copy.start()
    for copy in puts:
        copy.wait()


def call_inputs(gr, dqt, dk, dv, hk, hv, wq, wk, wv, small):
    tokens, width = gr.shape

    def top(rows):
        return pl.BlockSpec((rows, width), lambda i: (0, 0))

    whole = pl.BlockSpec((width, width), lambda i: (0, 0))
    return pl.pallas_call(
        inputs_kernel,
        grid=(1,),
        out_shape=jax.ShapeDtypeStruct((1, tokens, width), F32),
        in_specs=[
            top(tokens),
            pl.BlockSpec((width, tokens), lambda i: (0, 0)),
            top(tokens),
            top(tokens),
            top(tokens),
            top(tokens),
            whole,
            whole,
            whole,
            top(small.shape[0]),
        ],
        out_specs=pl.BlockSpec(memory_space=pltpu.HBM),
        scratch_shapes=[pltpu.VMEM((tokens, width), F32), pltpu.SemaphoreType.DMA((2,))],
        compiler_params=pltpu.CompilerParams(vmem_limit_bytes=60 * 2**20),
    )(gr, dqt, dk, dv, hk, hv, wq, wk, wv, small)


def swap_and_add(values, axis, partners):
    size = lax.axis_size(axis)
    arrived = [
        lax.ppermute(values, axis, [(i, i ^ p) for i in range(size)]) for p in partners
    ]
    total = values.astype(F32)
    for one in arrived:
        total = total + one.astype(F32)
    return total


def sum_everywhere(values):
    values = swap_and_add(values.astype(BF16), "seq", (1,))
    stride, size = 1, lax.axis_size("dp")
    while stride < size:
        radix = min(4, size // stride)
        values = swap_and_add(
            values.astype(BF16), "dp", [stride * k for k in range(1, radix)]
        )
        stride *= radix
    return values


def body(
    inputs,
    pair_lengths,
    w_query,
    w_key,
    w_value,
    w_out,
    w_up,
    w_down,
    a_query,
    b_query,
    a_value,
    b_value,
    gain_one,
    shift_one,
    gain_two,
    shift_two,
    cotangent,
):
    tokens = inputs.shape[1]
    rank = a_query.shape[1]
    swap = [(0, 1), (1, 0)]
    other = lax.ppermute(inputs, "seq", swap)
    small = jnp.concatenate([a_query.T, b_query, a_value.T, b_value])
    gains = jnp.stack([gain_one, shift_one, gain_two, shift_two])
    output, gr, dqt, dk, dv, packed = call_layer(
        pair_lengths,
        inputs,
        other,
        (w_query, w_key, w_value, w_out, w_up, w_down),
        small,
        gains,
        cotangent,
    )
    total = sum_everywhere(packed)
    hk = lax.ppermute(dk[tokens:], "seq", swap)
    hv = lax.ppermute(dv[tokens:], "seq", swap)
    grad_inputs = call_inputs(gr, dqt, dk, dv, hk, hv, w_query, w_key, w_value, small)
    return (
        output,
        grad_inputs,
        total[:rank].T,
        total[rank : 2 * rank],
        total[2 * rank : 3 * rank].T,
        total[3 * rank : 4 * rank],
        total[4 * rank],
        total[4 * rank + 1],
        total[4 * rank + 2],
        total[4 * rank + 3],
    )


def solution(mesh):
    tokens = P("dp", "seq", None)
    in_specs = (tokens, P("dp", None)) + (P(),) * 14 + (tokens,)
    out_specs = (tokens, tokens) + (P(),) * 8
    return jax.shard_map(body, mesh=mesh, in_specs=in_specs, out_specs=out_specs, check_vma=False)
```

time: 133 us -> 61.6 us (0.46)
  matrix products: 65.1 us -> 0 us
  Pallas kernels: 0 us -> 30.8 us
  between operations: 14.7 us -> 0.9 us
  local copies, waits for them, and re-layouts: 18.7 us -> 6.7 us
  other arithmetic: 12.1 us -> 3.99 us
  blocking collectives: 4.95 us -> 0 us
  waiting for transfers between devices: 7.01 us -> 8.82 us
    dot_general x29 -> x0, matrix products: 65.1 us -> none  [the longest x19 43.3 us: matmul(): return jnp.dot(former, latter, preferred_element_type=jnp.float32)]
    pallas_call x0 -> x2, Pallas kernels: none -> 30.8 us  [the longest x1 25.7 us: call_layer(): pl.pallas_call(layer_kernel, out_shape=(shape((1, tokens, width), BF16),...]
    reduce_sum x7 -> x0, other arithmetic: 5.79 us -> none  [the longest x3 2.21 us: norm_rows(): return centred * lax.rsqrt(variance + norm_epsilon) * gain_vec + shift_vec]
    all_gather x2 -> x0, blocking collectives: 4.95 us -> none  [the longest x1 2.5 us: body(): lax.all_gather(key_rows.reshape(seq_count, half_len, model_width), 'seq',...]
    unnamed x104 -> x8, local copies, waits for them, and re-layouts: 6.07 us -> 1.64 us
    reshape x4 -> x0, local copies, waits for them, and re-layouts: 3.82 us -> none  [norm_rows(): return centred * lax.rsqrt(variance + norm_epsilon) * gain_vec + shift_vec]
    convert_element_type x2 -> x0, local copies, waits for them, and re-layouts: 3.07 us -> none  [the longest x1 1.91 us: body(): (matmul(flat_inputs, w_query) + 2.0 * matmul(query_low, b_query)).astype(...]
    concatenate x1 -> x0, local copies, waits for them, and re-layouts: 2.98 us -> none  [body(): jnp.concatenate([grad_a_query.T, grad_b_query, grad_a_value.T, grad_b_val...]
  transfers between devices with their start and end apart: 9 -> 10, of which waited for: 5 -> 6; matrix products, arithmetic and copies ran while one was open for 23% -> 12% of each run, Pallas kernels for 0% -> 0%
where the time goes in v2:
time: 61.6 us; the launch traced here: 61.2 us
  Pallas kernels  30.8 us (50%)
  starting transfers between devices  9.96 us (16%)
  waiting for transfers between devices  8.82 us (14%)
  local copies, waits for them, and re-layouts  6.7 us (11%)
  other arithmetic  3.99 us (6%)
  between operations  0.9 us (1%)
    pallas_call x1, Pallas kernels, call_layer(): pl.pallas_call(layer_kernel, out_shape=(shape((1, tokens, width), BF16),...  25.7 us
    ppermute x7, starting transfers between devices, swap_and_add(): lax.ppermute(values, axis, [(i, i ^ p) for i in range(size)])  8.87 us
    ppermute x7, waiting for transfers between devices, swap_and_add(): lax.ppermute(values, axis, [(i, i ^ p) for i in range(size)])  8.81 us
    pallas_call x1, Pallas kernels, call_inputs(): pl.pallas_call(inputs_kernel, grid=(1,), out_shape=jax.ShapeDtypeStruct((...  5.17 us
    another operation x4, local copies, waits for them, and re-layouts, body(): gains = jnp.stack([gain_one, shift_one, gain_two, shift_two])  2.76 us
    unnamed x8, local copies, waits for them, and re-layouts  1.64 us
    concatenate x1, other arithmetic, body(): small = jnp.concatenate([a_query.T, b_query, a_value.T, b_value])  1.37 us
  transfers between devices with their start and end apart: 10, of which 6 were waited for; matrix products, arithmetic and copies ran while one was open for 12% of the time, Pallas kernels for 0%

profile of v2, /device:TPU:0, one launch (start us, length us, event | category | flops | bytes accessed | tf_op | source)
XLA Modules:
  0.0 61.2 jit_solution(6113970892192108393)
XLA Ops:
  0.6 0.5 collective-permute-start
  1.2 0.7 %stack.15 = f32[1,768]{1,0:T(1,128)S(1)} reshape(f32[768]{0:T(1024)} %param.29) | data formatting | bytes 6144 | tf_op jit(solution)/shard_map/stack | solution.py:578
  1.8 0.7 %stack.16 = f32[1,768]{1,0:T(1,128)S(1)} reshape(f32[768]{0:T(1024)} %param.30) | data formatting | bytes 6144 | tf_op jit(solution)/shard_map/stack | solution.py:578
  2.5 0.7 %stack.17 = f32[1,768]{1,0:T(1,128)S(1)} reshape(f32[768]{0:T(1024)} %param.31) | data formatting | bytes 6144 | tf_op jit(solution)/shard_map/stack | solution.py:578
  3.2 0.7 %stack.18 = f32[1,768]{1,0:T(1,128)S(1)} reshape(f32[768]{0:T(1024)} %param.32) | data formatting | bytes 6144 | tf_op jit(solution)/shard_map/stack | solution.py:578
  3.9 0.6 %pad_maximum_fusion.1.gains_hbm = f32[4,768]{1,0:T(4,128)} fusion(f32[1,768]{1,0:T(1,128)S(1)} %stack.18, f32[1,768]{1,0:T(1,128)S(1)} %stack.17, f32[1,768]{1,0:T(1,128)S(1)} %stack.16, f32[1,768]{1,0:T(1,128)S(1)} %stack.15), kind=kLoop, calls=%fused_computation.6 | loop fusion | flops 9216 | bytes 24576 | tf_op jit(solution)/shard_map/stack | solution.py:578
  4.5 1.4 %pad_maximum_fusion.small_hbm.small = bf16[32,768]{1,0:T(8,128)(2,1)} fusion(bf16[8,768]{1,0:T(8,128)(2,1)} %param.28, bf16[8,768]{1,0:T(8,128)(2,1)} %bitcast.6, bf16[8,768]{1,0:T(8,128)(2,1)} %param.26, bf16[8,768]{1,0:T(8,128)(2,1)} %bitcast.7), kind=kLoop, calls=%fused_computation.3 | loop fusion | flops 196608 | bytes 98304 | tf_op jit(solution)/shard_map/concatenate | solution.py:577
  5.9 0.7 %copy-done.3 = bf16[1,256,768]{2,1,0:T(8,128)(2,1)} copy-done((bf16[1,256,768]{2,1,0:T(8,128)(2,1)}, bf16[1,256,768]{2,1,0:T(8,128)(2,1)S(1)}, u32[]{:S(2)}) %copy-start.3) | copy-done | bytes 393240
  6.7 25.7 %shard_map.240 = (bf16[1,256,768]{2,1,0:T(8,128)(2,1)}, f32[256,768]{1,0:T(8,128)}, bf16[768,256]{1,0:T(8,128)(2,1)}, bf16[512,768]{1,0:T(8,128)(2,1)}, bf16[512,768]{1,0:T(8,128)(2,1)}, /*index=5*/f32[48,768]{1,0:T(8,128)}) custom-call(s32[1,8]{1,0:T(1,128)} %lengths_ref.1, bf16[1,256,768]{2,1,0:T(8,128)(2,1)} %x_hbm.1, bf16[1,256,768]{2,1,0:T(8,128)(2,1)} %copy-done.3, ...), custom_call_target="tpu_custom_call" | custom-call | tf_op jit(solution)/shard_map/pallas_call | solution.py:414
  32.3 1.0 %convert_element_type.39 = bf16[48,768]{1,0:T(8,128)(2,1)S(1)} convert(f32[48,768]{1,0:T(8,128)} %get-tuple-element.21) | non-fusion elementwise | flops 36864 | bytes 221184 | tf_op jit(solution)/shard_map/convert_element_type | solution.py:543
  33.3 0.1 collective-permute-start.3
  33.4 1.2 %collective-permute-done.3 = bf16[48,768]{1,0:T(8,128)(2,1)S(1)} collective-permute-done((bf16[48,768]{1,0:T(8,128)(2,1)S(1)}, bf16[48,768]{1,0:T(8,128)(2,1)S(1)}, u32[]{:S(2)}, u32[]{:S(2)}) %collective-permute-start.3) | collective-permute-done | bytes 73760 | tf_op jit(solution)/shard_map/ppermute | solution.py:534
  34.7 0.9 %add_convert_fusion.1 = bf16[48,768]{1,0:T(8,128)(2,1)S(1)} fusion(bf16[48,768]{1,0:T(8,128)(2,1)S(1)} %collective-permute-done.3, f32[48,768]{1,0:T(8,128)} %get-tuple-element.21), kind=kLoop, calls=%fused_computation.2 | loop fusion | flops 184320 | bytes 294912 | tf_op jit(solution)/shard_map/convert_element_type | solution.py:548
  35.6 3.7 %collective-permute-start.6 = (bf16[48,768]{1,0:T(8,128)(2,1)S(1)}, bf16[48,768]{1,0:T(8,128)(2,1)S(1)}, u32[]{:S(2)}, u32[]{:S(2)}) collective-permute-start(bf16[48,768]{1,0:T(8,128)(2,1)S(1)} %add_convert_fusion.1), channel_id=1, source_target_pairs={{0,6},{2,4},{4,2},{6,0},{8,14},{10,12},{12,10},{14,8},{16,22},{18,... | collective-permute-start | bytes 221192 | tf_op jit(solution)/shard_map/ppermute | solution.py:534
  39.2 0.5 collective-permute-start.5
  39.8 0.1 collective-permute-start.4
  39.9 2.2 %collective-permute-done.6 = bf16[48,768]{1,0:T(8,128)(2,1)S(1)} collective-permute-done((bf16[48,768]{1,0:T(8,128)(2,1)S(1)}, bf16[48,768]{1,0:T(8,128)(2,1)S(1)}, u32[]{:S(2)}, u32[]{:S(2)}) %collective-permute-start.6) | collective-permute-done | bytes 73760 | tf_op jit(solution)/shard_map/ppermute | solution.py:534
  42.0 1.6 %collective-permute-done.5 = bf16[48,768]{1,0:T(8,128)(2,1)S(1)} collective-permute-done((bf16[48,768]{1,0:T(8,128)(2,1)S(1)}, bf16[48,768]{1,0:T(8,128)(2,1)S(1)}, u32[]{:S(2)}, u32[]{:S(2)}) %collective-permute-start.5) | collective-permute-done | bytes 73760 | tf_op jit(solution)/shard_map/ppermute | solution.py:534
  43.6 0.5 collective-permute-done.4
  44.2 3.7 %collective-permute-start.9 = (bf16[48,768]{1,0:T(8,128)(2,1)S(1)}, bf16[48,768]{1,0:T(8,128)(2,1)S(1)}, u32[]{:S(2)}, u32[]{:S(2)}) collective-permute-start(bf16[48,768]{1,0:T(8,128)(2,1)S(1)} %add_convert_fusion), channel_id=1, source_target_pairs={{0,24},{2,26},{4,28},{6,30},{8,16},{10,18},{12,20},{14,22},{16,8},... | collective-permute-start | bytes 221192 | tf_op jit(solution)/shard_map/ppermute | solution.py:534
  47.8 0.8 %collective-permute-start.7 = (bf16[48,768]{1,0:T(8,128)(2,1)S(1)}, bf16[48,768]{1,0:T(8,128)(2,1)S(1)}, u32[]{:S(2)}, u32[]{:S(2)}) collective-permute-start(bf16[48,768]{1,0:T(8,128)(2,1)S(1)} %add_convert_fusion), channel_id=1, source_target_pairs={{0,8},{2,10},{4,12},{6,14},{8,0},{10,2},{12,4},{14,6},{16,24},{18,... | collective-permute-start | bytes 221192 | tf_op jit(solution)/shard_map/ppermute | solution.py:534
  48.6 1.0 %slice.30 = bf16[256,768]{1,0:T(8,128)(2,1)S(1)} slice(bf16[512,768]{1,0:T(8,128)(2,1)} %get-tuple-element.19.dk_ref), slice={[256:512], [0:768]} | slice | bytes 786432 | tf_op jit(solution)/shard_map/slice | solution.py:589
  49.7 0.1 collective-permute-start.2
  49.8 0.5 collective-permute-start.1
  50.3 0.7 %collective-permute-done.9 = bf16[48,768]{1,0:T(8,128)(2,1)S(1)} collective-permute-done((bf16[48,768]{1,0:T(8,128)(2,1)S(1)}, bf16[48,768]{1,0:T(8,128)(2,1)S(1)}, u32[]{:S(2)}, u32[]{:S(2)}) %collective-permute-start.9) | collective-permute-done | bytes 73760 | tf_op jit(solution)/shard_map/ppermute | solution.py:534
  51.0 2.6 %collective-permute-done.8 = bf16[48,768]{1,0:T(8,128)(2,1)S(1)} collective-permute-done((bf16[48,768]{1,0:T(8,128)(2,1)S(1)}, bf16[48,768]{1,0:T(8,128)(2,1)S(1)}, u32[]{:S(2)}, u32[]{:S(2)}) %collective-permute-start.8) | collective-permute-done | bytes 73760 | tf_op jit(solution)/shard_map/ppermute | solution.py:534
  53.6 0.0 collective-permute-done.7
  53.7 0.6 %slice_reduce_fusion = (f32[768]{0:T(1024)}, f32[768]{0:T(1024)}, f32[768]{0:T(1024)}, f32[768]{0:T(1024)}) fusion(f32[48,768]{1,0:T(8,128)S(1)} %convert_add_fusion), kind=kLoop, calls=%fused_computation.7 | loop fusion | bytes 24576 | tf_op jit(solution)/shard_map/slice | solution.py:602
  54.3 0.6 %fusion = (f32[8,768]{1,0:T(8,128)}, f32[768,8]{0,1:T(8,128)}, f32[8,768]{1,0:T(8,128)}, f32[768,8]{0,1:T(8,128)}) fusion(f32[48,768]{1,0:T(8,128)S(1)} %convert_add_fusion), kind=kLoop, calls=%fused_computation.11 | loop fusion | bytes 196608 | tf_op jit(solution)/shard_map/slice | solution.py:598
  55.0 0.7 %copy-done.1 = bf16[256,768]{1,0:T(8,128)(2,1)} copy-done((bf16[256,768]{1,0:T(8,128)(2,1)}, bf16[256,768]{1,0:T(8,128)(2,1)S(1)}, u32[]{:S(2)}) %copy-start.1) | copy-done | bytes 393240
  55.7 0.2 copy-done.2
  55.8 5.2 %shard_map.241 = f32[1,256,768]{2,1,0:T(8,128)} custom-call(f32[256,768]{1,0:T(8,128)} %get-tuple-element.17.gr_ref, bf16[768,256]{1,0:T(8,128)(2,1)} %get-tuple-element.18.dqt_ref, bf16[512,768]{1,0:T(8,128)(2,1)} %get-tuple-element.19.dk_ref, bf16[512,768]{1,0:T(8,128)(2,1)} %get-tuple-element.20.dv_ref, bf16[256,768]{1,0:T(8,128)(2,1)} %copy-done.2, ...), custom_call_target="tpu_custom_call" | custom-call | tf_op jit(solution)/shard_map/pallas_call | solution.py:509
  (12 shorter events, 0.1 us)
Async XLA Ops:
  0.6 5.3 %collective-permute-start = (bf16[1,256,768]{2,1,0:T(8,128)(2,1)}, bf16[1,256,768]{2,1,0:T(8,128)(2,1)S(1)}, u32[]{:S(2)}, u32[]{:S(2)}) collective-permute-start(bf16[1,256,768]{2,1,0:T(8,128)(2,1)} %x_hbm.1), channel_id=1, source_target_pairs={{0,1},{1,0},{2,3},{3,2},{4,5},{5,4},{6,7},{7,6},{8,9},{9,8},{10,11... | collective-permute-start | bytes 1179656 | tf_op jit(solution)/shard_map/ppermute | solution.py:576
  5.9 0.7 %copy-start.3 = (bf16[1,256,768]{2,1,0:T(8,128)(2,1)}, bf16[1,256,768]{2,1,0:T(8,128)(2,1)S(1)}, u32[]{:S(2)}) copy-start(bf16[1,256,768]{2,1,0:T(8,128)(2,1)S(1)} %collective-permute-done.other_hbm) | copy-start | bytes 1179652
  32.3 17.3 %copy-start = (bf16[512,768]{1,0:T(8,128)(2,1)S(1)}, bf16[512,768]{1,0:T(8,128)(2,1)}, u32[]{:S(2)}) copy-start(bf16[512,768]{1,0:T(8,128)(2,1)} %get-tuple-element.20.dv_ref) | copy-start | bytes 2359300
  33.3 1.3 %collective-permute-start.3 = (bf16[48,768]{1,0:T(8,128)(2,1)S(1)}, bf16[48,768]{1,0:T(8,128)(2,1)S(1)}, u32[]{:S(2)}, u32[]{:S(2)}) collective-permute-start(bf16[48,768]{1,0:T(8,128)(2,1)S(1)} %convert_element_type.39), channel_id=1, source_target_pairs={{0,1},{1,0},{2,3},{3,2},{4,5},{5,4},{6,7},{7,6},{8,9},{9,8},{10,11... | collective-permute-start | bytes 221192 | tf_op jit(solution)/shard_map/ppermute | solution.py:534
  35.6 6.5 %collective-permute-start.6 = (bf16[48,768]{1,0:T(8,128)(2,1)S(1)}, bf16[48,768]{1,0:T(8,128)(2,1)S(1)}, u32[]{:S(2)}, u32[]{:S(2)}) collective-permute-start(bf16[48,768]{1,0:T(8,128)(2,1)S(1)} %add_convert_fusion.1), channel_id=1, source_target_pairs={{0,6},{2,4},{4,2},{6,0},{8,14},{10,12},{12,10},{14,8},{16,22},{18,... | collective-permute-start | bytes 221192 | tf_op jit(solution)/shard_map/ppermute | solution.py:534
  39.2 4.4 %collective-permute-start.5 = (bf16[48,768]{1,0:T(8,128)(2,1)S(1)}, bf16[48,768]{1,0:T(8,128)(2,1)S(1)}, u32[]{:S(2)}, u32[]{:S(2)}) collective-permute-start(bf16[48,768]{1,0:T(8,128)(2,1)S(1)} %add_convert_fusion.1), channel_id=1, source_target_pairs={{0,4},{2,6},{4,0},{6,2},{8,12},{10,14},{12,8},{14,10},{16,20},{18,... | collective-permute-start | bytes 221192 | tf_op jit(solution)/shard_map/ppermute | solution.py:534
  39.8 4.4 %collective-permute-start.4 = (bf16[48,768]{1,0:T(8,128)(2,1)S(1)}, bf16[48,768]{1,0:T(8,128)(2,1)S(1)}, u32[]{:S(2)}, u32[]{:S(2)}) collective-permute-start(bf16[48,768]{1,0:T(8,128)(2,1)S(1)} %add_convert_fusion.1), channel_id=1, source_target_pairs={{0,2},{2,0},{4,6},{6,4},{8,10},{10,8},{12,14},{14,12},{16,18},{18,... | collective-permute-start | bytes 221192 | tf_op jit(solution)/shard_map/ppermute | solution.py:534
  44.2 6.8 %collective-permute-start.9 = (bf16[48,768]{1,0:T(8,128)(2,1)S(1)}, bf16[48,768]{1,0:T(8,128)(2,1)S(1)}, u32[]{:S(2)}, u32[]{:S(2)}) collective-permute-start(bf16[48,768]{1,0:T(8,128)(2,1)S(1)} %add_convert_fusion), channel_id=1, source_target_pairs={{0,24},{2,26},{4,28},{6,30},{8,16},{10,18},{12,20},{14,22},{16,8},... | collective-permute-start | bytes 221192 | tf_op jit(solution)/shard_map/ppermute | solution.py:534
  47.8 5.8 %collective-permute-start.8 = (bf16[48,768]{1,0:T(8,128)(2,1)S(1)}, bf16[48,768]{1,0:T(8,128)(2,1)S(1)}, u32[]{:S(2)}, u32[]{:S(2)}) collective-permute-start(bf16[48,768]{1,0:T(8,128)(2,1)S(1)} %add_convert_fusion), channel_id=1, source_target_pairs={{0,16},{2,18},{4,20},{6,22},{8,24},{10,26},{12,28},{14,30},{16,0},... | collective-permute-start | bytes 221192 | tf_op jit(solution)/shard_map/ppermute | solution.py:534
  47.8 5.8 %collective-permute-start.7 = (bf16[48,768]{1,0:T(8,128)(2,1)S(1)}, bf16[48,768]{1,0:T(8,128)(2,1)S(1)}, u32[]{:S(2)}, u32[]{:S(2)}) collective-permute-start(bf16[48,768]{1,0:T(8,128)(2,1)S(1)} %add_convert_fusion), channel_id=1, source_target_pairs={{0,8},{2,10},{4,12},{6,14},{8,0},{10,2},{12,4},{14,6},{16,24},{18,... | collective-permute-start | bytes 221192 | tf_op jit(solution)/shard_map/ppermute | solution.py:534
  49.7 5.3 %collective-permute-start.2 = (bf16[256,768]{1,0:T(8,128)(2,1)S(1)}, bf16[256,768]{1,0:T(8,128)(2,1)S(1)}, u32[]{:S(2)}, u32[]{:S(2)}) collective-permute-start(bf16[256,768]{1,0:T(8,128)(2,1)S(1)} %slice.31), channel_id=1, source_target_pairs={{0,1},{1,0},{2,3},{3,2},{4,5},{5,4},{6,7},{7,6},{8,9},{9,8},{10,11... | collective-permute-start | bytes 1179656 | tf_op jit(solution)/shard_map/ppermute | solution.py:590
  49.8 5.2 %collective-permute-start.1 = (bf16[256,768]{1,0:T(8,128)(2,1)S(1)}, bf16[256,768]{1,0:T(8,128)(2,1)S(1)}, u32[]{:S(2)}, u32[]{:S(2)}) collective-permute-start(bf16[256,768]{1,0:T(8,128)(2,1)S(1)} %slice.30), channel_id=1, source_target_pairs={{0,1},{1,0},{2,3},{3,2},{4,5},{5,4},{6,7},{7,6},{8,9},{9,8},{10,11... | collective-permute-start | bytes 1179656 | tf_op jit(solution)/shard_map/ppermute | solution.py:589
  54.9 0.7 %copy-start.1 = (bf16[256,768]{1,0:T(8,128)(2,1)}, bf16[256,768]{1,0:T(8,128)(2,1)S(1)}, u32[]{:S(2)}) copy-start(bf16[256,768]{1,0:T(8,128)(2,1)S(1)} %collective-permute-done.2.hv_ref) | copy-start | bytes 1179652
  55.0 0.9 %copy-start.2 = (bf16[256,768]{1,0:T(8,128)(2,1)}, bf16[256,768]{1,0:T(8,128)(2,1)S(1)}, u32[]{:S(2)}) copy-start(bf16[256,768]{1,0:T(8,128)(2,1)S(1)} %collective-permute-done.1.hk_ref) | copy-start | bytes 1179652

commit v3 on v2

v3 whole, which is shorter than its diff:
```python
import functools
import math

import jax
import jax.numpy as jnp
from jax import lax
from jax.experimental import pallas as pl
from jax.experimental.pallas import tpu as pltpu
from jax.sharding import PartitionSpec as P

DH = 64
LANES = 128
EPSILON = 1e-05
LOG2_E = math.log2(math.e)
FAR_AWAY = -1e30
BF16 = jnp.bfloat16
F32 = jnp.float32
NN = ((1,), (0,))
NT = ((1,), (1,))
TN = ((0,), (0,))
TT = ((0,), (1,))


def dot(former, latter, dims=NN):
    return lax.dot_general(former, latter, (dims, ((), ())), preferred_element_type=F32)


def normed(values):
    centred = values - jnp.mean(values, axis=-1, keepdims=True)
    variance = jnp.mean(centred * centred, axis=-1, keepdims=True)
    inverse = lax.rsqrt(variance + EPSILON)
    return centred * inverse, inverse


def norm_back(grad, normal, inverse):
    return inverse * (
        grad
        - jnp.mean(grad, axis=-1, keepdims=True)
        - normal * jnp.mean(grad * normal, axis=-1, keepdims=True)
    )


def gelu_and_slope(values):
    size = jnp.abs(values)
    inv = 1.0 / (1.0 + (0.3275911 / math.sqrt(2.0)) * size)
    bell = jnp.exp2(values * values * (-0.5 * LOG2_E))
    tail = inv * (
        0.5 * 0.254829592
        + inv
        * (
            0.5 * -0.284496736
            + inv * (0.5 * 1.421413741 + inv * (0.5 * -1.453152027 + inv * (0.5 * 1.061405429)))
        )
    )
    tail = tail * bell
    below = jnp.where(values < 0.0, tail, 1.0 - tail)
    return values * below, below + values * bell * (1.0 / math.sqrt(2.0 * math.pi))


def segment_codes(lengths_ref, start_near, start_far, rows):
    row = lax.broadcasted_iota(jnp.int32, (rows, LANES), 0)
    half = rows // 2
    place = jnp.where(row < half, start_near + row, start_far + row - half)
    segment = jnp.zeros_like(place)
    end = jnp.int32(0)
    for pair in range(lengths_ref.shape[1]):
        end = end + lengths_ref[0, pair]
        segment = segment + (place >= end).astype(jnp.int32)
    return segment


def crosses_widely(lengths_ref, middle, half):
    end = jnp.int32(0)
    left = jnp.int32(middle)
    right = jnp.int32(middle)
    for pair in range(lengths_ref.shape[1]):
        end = end + lengths_ref[0, pair]
        left = jnp.where(end < middle, middle - end, left)
        right = jnp.where(end >= middle, jnp.minimum(right, end - middle), right)
    return (right > 0) & ((left > half) | (right > half))


def in_hbm(*arrays):
    return [pltpu.with_memory_space_constraint(a, pltpu.HBM) for a in arrays]


def own_rows(side, half):
    return pl.multiple_of((1 - side) * half, half), pl.multiple_of(side * half, half)


def project_kernel(
    x_hbm,
    wq_hbm,
    wk_hbm,
    wv_hbm,
    aqt_hbm,
    bq_hbm,
    avt_hbm,
    bv_hbm,
    x_ref,
    q_ref,
    k_ref,
    v_ref,
    kt_ref,
    vt_ref,
    qlow_ref,
    vlow_ref,
    wk,
    wv,
    bq,
    avt,
    bv,
    wq,
    aqt,
    sems,
):
    tokens = x_hbm.shape[1]
    half = tokens // 2
    near, far = own_rows(lax.axis_index("seq"), half)
    pairs = (
        (x_hbm.at[0, pl.ds(near, half)], x_ref.at[pl.ds(0, half)]),
        (x_hbm.at[0, pl.ds(far, half)], x_ref.at[pl.ds(half, half)]),
        (wk_hbm, wk),
        (aqt_hbm, aqt),
        (bq_hbm, bq),
        (avt_hbm, avt),
        (bv_hbm, bv),
        (wq_hbm, wq),
        (wv_hbm, wv),
    )
    copies = [pltpu.make_async_copy(a, b, sems.at[i]) for i, (a, b) in enumerate(pairs)]
    for copy in copies:
        copy.start()
    for copy in copies[:3]:
        copy.wait()
    x = x_ref[...]
    keys = dot(x, wk[...]).astype(BF16)
    k_ref[...] = keys
    kt_ref[...] = keys.T
    for copy in copies[3:]:
        copy.wait()
    qlow_t = dot(aqt[...], x, NT).astype(BF16)
    vlow_t = dot(avt[...], x, NT).astype(BF16)
    qlow_ref[...] = qlow_t
    vlow_ref[...] = vlow_t
    q_ref[...] = (
        (dot(x, wq[...]) + 2.0 * dot(qlow_t, bq[...], TN)) * (LOG2_E / math.sqrt(DH))
    ).astype(BF16)
    vals = (dot(x, wv[...]) + 2.0 * dot(vlow_t, bv[...], TN)).astype(BF16)
    v_ref[...] = vals
    vt_ref[...] = vals.T


def call_project(x, wq, wk, wv, lows):
    _, tokens, width = x.shape
    rank = lows[1].shape[0]
    shape = jax.ShapeDtypeStruct
    rows, columns = shape((tokens, width), BF16), shape((width, tokens), BF16)
    low = shape((rank, tokens), BF16)
    square, flat = shape((width, width), BF16), shape((rank, width), BF16)
    return pl.pallas_call(
        project_kernel,
        out_shape=(rows,) * 4 + (columns,) * 2 + (low,) * 2 + (square,) * 2 + (flat,) * 3,
        in_specs=[pl.BlockSpec(memory_space=pltpu.HBM)] * 8,
        out_specs=(pl.BlockSpec(memory_space=pltpu.VMEM),) * 13,
        scratch_shapes=[
            pltpu.VMEM((width, width), BF16),
            pltpu.VMEM((rank, width), BF16),
            pltpu.SemaphoreType.DMA((9,)),
        ],
        compiler_params=pltpu.CompilerParams(vmem_limit_bytes=14 * 2**20),
        cost_estimate=pl.CostEstimate(flops=10**9, bytes_accessed=8 * 10**6, transcendentals=0),
    )(*in_hbm(x, wq, wk, wv, *lows))


def layer_kernel(
    lengths_ref,
    x_ref,
    q_s,
    k_s,
    v_s,
    kt_s,
    vt_s,
    qlow_ref,
    vlow_ref,
    wk,
    wv,
    bq_ref,
    avt_ref,
    bv_ref,
    other_ref,
    gain_one_hbm,
    shift_one_hbm,
    gain_two_hbm,
    shift_two_hbm,
    wo_hbm,
    wu_hbm,
    wd_hbm,
    cot_hbm,
    out_hbm,
    gr_s,
    dqt_s,
    dk_s,
    dv_s,
    halo_s,
    packed_ref,
    gain_one_s,
    shift_one_s,
    gain_two_s,
    shift_two_s,
    x_s,
    wo,
    wu,
    wd,
    cot_s,
    kh_s,
    vh_s,
    kht_s,
    vht_s,
    po_s,
    ph_s,
    inv_s,
    ct_s,
    normal_s,
    rstd_s,
    hidden_s,
    active_s,
    slope_s,
    total_s,
    out_s,
    dot_s,
    sems,
):
    tokens, width = x_ref.shape
    half = tokens // 2
    hidden = wu_hbm.shape[1]
    rank = bq_ref.shape[0]
    heads = width // DH
    side = lax.axis_index("seq")
    near, far = own_rows(side, half)

    copies = []

    def fetch(source, target):
        copy = pltpu.make_async_copy(source, target, sems.at[len(copies)])
        copies.append(copy)
        copy.start()
        return copy

    get_o = [
        fetch(wo_hbm, wo),
        fetch(gain_one_hbm, gain_one_s),
        fetch(shift_one_hbm, shift_one_s),
        fetch(gain_two_hbm, gain_two_s),
        fetch(shift_two_hbm, shift_two_s),
    ]
    chunks = hidden // width
    get_u, get_d = [], []
    for c in range(chunks):
        part = pl.ds(c * width, width)
        get_u.append(fetch(wu_hbm.at[:, part], wu.at[:, part]))
        get_d.append(fetch(wd_hbm.at[part], wd.at[part]))
    get_cot = [
        fetch(cot_hbm.at[0, pl.ds(near, half)], cot_s.at[pl.ds(0, half)]),
        fetch(cot_hbm.at[0, pl.ds(far, half)], cot_s.at[pl.ds(half, half)]),
    ]

    wide = crosses_widely(lengths_ref, tokens, half)
    own_segment = segment_codes(lengths_ref, side * tokens + near, side * tokens + far, tokens)
    halo_base = (1 - side) * tokens
    halo_segment = segment_codes(lengths_ref, halo_base + far, halo_base + near, tokens)
    lane = lax.broadcasted_iota(jnp.int32, (tokens, LANES), 1)
    code = lane & (DH - 1)
    low_half = lane < DH
    marks = lengths_ref.shape[1] + 1
    q_code = jnp.where(code == own_segment, 1.0, 0.0).astype(BF16)

    def key_code(segment):
        return jnp.where((code < marks) & (code != segment), FAR_AWAY, 0.0).astype(BF16)

    ko_code = key_code(own_segment)
    kh_code = key_code(halo_segment)

    bq, avt, bv = bq_ref[...], avt_ref[...], bv_ref[...]
    qlow_t, vlow_t = qlow_ref[...], vlow_ref[...]
    x_s[pl.ds(0, half)] = other_ref[0, pl.ds(far, half)]
    x_s[pl.ds(half, half)] = other_ref[0, pl.ds(near, half)]
    halo_low_t = dot(avt, x_s[...], NT).astype(BF16)

    def project_halo(start):
        rows = pl.ds(start, half)
        x_halo = x_s[rows]
        keys = dot(x_halo, wk[...]).astype(BF16)
        kh_s[rows] = keys
        kht_s[:, rows] = keys.T
        low_t = halo_low_t[:, start : start + half]
        vals = (dot(x_halo, wv[...]) + 2.0 * dot(low_t, bv, TN)).astype(BF16)
        vh_s[rows] = vals
        vht_s[:, rows] = vals.T

    project_halo(0)

    @pl.when(wide)
    def _():
        project_halo(half)

    def joined(own, halo, reach, join):
        if reach == tokens:
            return join(own, halo)
        return jnp.concatenate([join(own[:, :reach], halo), own[:, reach:]], axis=1)

    def attend(pair, reach):
        lanes = pl.ds(pl.multiple_of(pair * LANES, LANES), LANES)
        q_pair = q_s[:, lanes]
        ko_pair = k_s[:, lanes]
        kh_pair = kh_s[pl.ds(0, reach), lanes]
        for odd in range(2):
            head = 2 * pair + odd
            rows = pl.ds(pl.multiple_of(head * DH, DH), DH)

            def mixed(values, codes):
                mask = low_half[: values.shape[0]]
                if odd:
                    return jnp.where(mask, codes, values)
                return jnp.where(mask, values, codes)

            q_head = mixed(q_pair, q_code)
            own = dot(mixed(ko_pair, ko_code), q_head, NT)
            halo = dot(mixed(kh_pair, kh_code[:reach]), q_head[:reach], NT)
            peak = joined(
                jnp.max(own, axis=0, keepdims=True),
                jnp.max(halo, axis=0, keepdims=True),
                reach,
                jnp.maximum,
            )
            own = jnp.exp2(own - peak)
            halo = jnp.exp2(halo - peak[:, :reach])
            inverse = 1.0 / joined(
                jnp.sum(own, axis=0, keepdims=True),
                jnp.sum(halo, axis=0, keepdims=True),
                reach,
                jnp.add,
            )
            own, halo = own.astype(BF16), halo.astype(BF16)
            po_s[head] = own
            ph_s[head, pl.ds(0, reach), pl.ds(0, reach)] = halo
            inv_s[head] = jnp.broadcast_to(inverse, inv_s.shape[1:])
            context = joined(
                dot(vt_s[rows, :], own),
                dot(vht_s[rows, pl.ds(0, reach)], halo),
                reach,
                jnp.add,
            )
            ct_s[rows, :] = (context * inverse).astype(BF16)

    def attend_back(pair, reach):
        lanes = pl.ds(pl.multiple_of(pair * LANES, LANES), LANES)
        q_pair = q_s[:, lanes]
        vo_pair = v_s[:, lanes]
        vh_pair = vh_s[pl.ds(0, reach), lanes]
        dv_own, dv_halo, dk_own, dk_halo = [], [], [], []
        for odd in range(2):
            head = 2 * pair + odd
            rows = pl.ds(pl.multiple_of(head * DH, DH), DH)
            inverse = inv_s[head, pl.ds(0, 1), :]
            grad = (dot_s[rows, :] * inverse).astype(BF16)
            blank = jnp.zeros_like(grad)
            grad = jnp.concatenate([blank, grad] if odd else [grad, blank], axis=0)
            po, ph = po_s[head], ph_s[head, pl.ds(0, reach), pl.ds(0, reach)]
            own = po.astype(F32) * dot(vo_pair, grad)
            halo = ph.astype(F32) * dot(vh_pair, grad[:, :reach])
            inner = inverse * joined(
                jnp.sum(own, axis=0, keepdims=True),
                jnp.sum(halo, axis=0, keepdims=True),
                reach,
                jnp.add,
            )
            own = (own - po.astype(F32) * inner).astype(BF16)
            halo = (halo - ph.astype(F32) * inner[:, :reach]).astype(BF16)
            dv_own.append(dot(po, grad, NT))
            dv_halo.append(dot(ph, grad[:, :reach], NT))
            dk_own.append(dot(own, q_pair))
            dk_halo.append(dot(halo, q_pair[:reach]))
            dqt = joined(
                dot(kt_s[rows, :], own),
                dot(kht_s[rows, pl.ds(0, reach)], halo),
                reach,
                jnp.add,
            )
            dqt_s[rows, :] = (dqt * (1.0 / math.sqrt(DH))).astype(BF16)
        unscale = 1.0 / LOG2_E
        dv_s[:, lanes] = (dv_own[0] + dv_own[1]).astype(BF16)
        halo_s[pl.ds(tokens, reach), lanes] = (dv_halo[0] + dv_halo[1]).astype(BF16)
        dk_s[:, lanes] = (
            jnp.where(low_half, dk_own[0], dk_own[1]) * unscale
        ).astype(BF16)
        halo_s[pl.ds(0, reach), lanes] = (
            jnp.where(low_half[:reach], dk_halo[0], dk_halo[1]) * unscale
        ).astype(BF16)

    def for_pairs(step):
        @pl.when(jnp.logical_not(wide))
        def _():
            for pair in range(heads // 2):
                step(pair, half)

        @pl.when(wide)
        def _():
            lax.fori_loop(0, heads // 2, lambda pair, none: step(pair, tokens), None)

    for_pairs(attend)

    for copy in get_o:
        copy.wait()
    resid_one = x_ref[...].astype(F32) + dot(ct_s[...], wo[...], TN)
    normal, inverse = normed(resid_one)
    normal_s[...] = normal
    rstd_s[...] = jnp.broadcast_to(inverse, rstd_s.shape)
    gain_one, shift_one = gain_one_s[...].reshape(1, width), shift_one_s[...].reshape(1, width)
    gain_two, shift_two = gain_two_s[...].reshape(1, width), shift_two_s[...].reshape(1, width)
    hidden_one = normal * gain_one + shift_one
    hidden_s[...] = hidden_one.astype(BF16)
    total_s[...] = hidden_one
    for copy in get_u + get_d:
        copy.wait()
    for c in range(chunks):
        part = pl.ds(c * width, width)
        upward = dot(hidden_s[...], wu[:, part])
        value, slope = gelu_and_slope(upward)
        active_s[:, part] = value.astype(BF16)
        slope_s[:, part] = slope.astype(BF16)
        total_s[...] += dot(active_s[:, part], wd[part, :])
    normal_two, inverse_two = normed(total_s[...])
    out_s[...] = (normal_two * gain_two + shift_two).astype(BF16)

    def put(source, target):
        return fetch(source, target)

    puts = [
        put(out_s.at[pl.ds(0, half)], out_hbm.at[0, pl.ds(near, half)]),
        put(out_s.at[pl.ds(half, half)], out_hbm.at[0, pl.ds(far, half)]),
    ]
    for copy in get_cot:
        copy.wait()
    grad_out = cot_s[...].astype(F32)
    grad_gain_two = jnp.sum(grad_out * normal_two, axis=0, keepdims=True)
    grad_shift_two = jnp.sum(grad_out, axis=0, keepdims=True)
    grad_two = norm_back(grad_out * gain_two, normal_two, inverse_two)
    hidden_s[...] = grad_two.astype(BF16)
    total_s[...] = grad_two
    for c in range(chunks):
        part = pl.ds(c * width, width)
        grad_up = slope_s[:, part].astype(F32) * dot(hidden_s[...], wd[part, :], NT)
        active_s[:, part] = grad_up.astype(BF16)
        total_s[...] += dot(active_s[:, part], wu[:, part], NT)
    grad_hidden = total_s[...]
    normal = normal_s[...]
    grad_gain_one = jnp.sum(grad_hidden * normal, axis=0, keepdims=True)
    grad_shift_one = jnp.sum(grad_hidden, axis=0, keepdims=True)
    grad_one = norm_back(grad_hidden * gain_one, normal, rstd_s[:, :1])
    gr_s[...] = grad_one
    dot_s[...] = dot(wo[...], grad_one.astype(BF16), NT)

    @pl.when(jnp.logical_not(wide))
    def _():
        halo_s[pl.ds(half, half)] = jnp.zeros((half, width), BF16)
        halo_s[pl.ds(tokens + half, half)] = jnp.zeros((half, width), BF16)

    for_pairs(attend_back)

    dv_halo = halo_s[pl.ds(tokens, tokens)]
    x_own = x_ref[...]
    grad_qlow_t = (2.0 * dot(bq, dqt_s[...])).astype(BF16)
    grad_vlow_t = (2.0 * dot(bv, dv_s[...], NT)).astype(BF16)
    grad_halo_t = (2.0 * dot(bv, dv_halo, NT)).astype(BF16)
    rows = [
        dot(grad_qlow_t, x_own),
        2.0 * dot(qlow_t, dqt_s[...], NT),
        dot(grad_vlow_t, x_own) + dot(grad_halo_t, x_s[...]),
        2.0 * (dot(vlow_t, dv_s[...]) + dot(halo_low_t, dv_halo)),
        grad_gain_one,
        grad_shift_one,
        grad_gain_two,
        grad_shift_two,
    ]
    spare = packed_ref.shape[0] - 4 * rank - 4
    rows.append(jnp.zeros((spare, width), F32))
    packed_ref[...] = jnp.concatenate(rows, axis=0).astype(BF16)
    for copy in puts:
        copy.wait()


def call_layer(lengths, projected, other, gains, wo, wu, wd, cotangent):
    _, tokens, width = other.shape
    hidden = wu.shape[1]
    heads = width // DH
    rank = projected[-1].shape[0]
    packed_rows = -(-(4 * rank + 4) // 16) * 16
    hbm = pl.BlockSpec(memory_space=pltpu.HBM)
    here = pl.BlockSpec(memory_space=pltpu.VMEM)
    shape = jax.ShapeDtypeStruct
    vmem = pltpu.VMEM
    return pl.pallas_call(
        layer_kernel,
        out_shape=(
            shape((1, tokens, width), BF16),
            shape((tokens, width), F32),
            shape((width, tokens), BF16),
            shape((tokens, width), BF16),
            shape((tokens, width), BF16),
            shape((2 * tokens, width), BF16),
            shape((packed_rows, width), BF16),
        ),
        in_specs=[pl.BlockSpec(memory_space=pltpu.SMEM)] + [here] * 14 + [hbm] * 8,
        out_specs=(hbm,) + (here,) * 6,
        scratch_shapes=[
            vmem((width,), F32),
            vmem((width,), F32),
            vmem((width,), F32),
            vmem((width,), F32),
            vmem((tokens, width), BF16),
            vmem(wo.shape, BF16),
            vmem(wu.shape, BF16),
            vmem(wd.shape, BF16),
            vmem((tokens, width), BF16),
            vmem((tokens, width), BF16),
            vmem((tokens, width), BF16),
            vmem((width, tokens), BF16),
            vmem((width, tokens), BF16),
            vmem((heads, tokens, tokens), BF16),
            vmem((heads, tokens, tokens), BF16),
            vmem((heads, 8, tokens), F32),
            vmem((width, tokens), BF16),
            vmem((tokens, width), F32),
            vmem((tokens, LANES), F32),
            vmem((tokens, width), BF16),
            vmem((tokens, hidden), BF16),
            vmem((tokens, hidden), BF16),
            vmem((tokens, width), F32),
            vmem((tokens, width), BF16),
            vmem((width, tokens), F32),
            pltpu.SemaphoreType.DMA((32,)),
        ],
        compiler_params=pltpu.CompilerParams(vmem_limit_bytes=44 * 2**20),
        cost_estimate=pl.CostEstimate(flops=9 * 10**9, bytes_accessed=15 * 10**6, transcendentals=0),
    )(lengths, *projected, other, *in_hbm(*gains, wo, wu, wd, cotangent))


def inputs_kernel(
    halo_ref,
    gr,
    dqt,
    dk,
    dv,
    wq_hbm,
    wk_hbm,
    wv_hbm,
    aqt_hbm,
    bq_hbm,
    avt_hbm,
    bv_hbm,
    out_hbm,
    wq,
    wk,
    wv,
    aqt,
    bq,
    avt,
    bv,
    out_s,
    sems,
):
    tokens, width = gr.shape
    half = tokens // 2
    near, far = own_rows(lax.axis_index("seq"), half)
    pairs = (
        (wq_hbm, wq),
        (wk_hbm, wk),
        (wv_hbm, wv),
        (bq_hbm, bq),
        (aqt_hbm, aqt),
        (bv_hbm, bv),
        (avt_hbm, avt),
    )
    copies = [pltpu.make_async_copy(a, b, sems.at[i]) for i, (a, b) in enumerate(pairs)]
    for copy in copies:
        copy.start()
    for copy in copies:
        copy.wait()
    grad_k = (dk[...].astype(F32) + halo_ref[pl.ds(0, tokens)].astype(F32)).astype(BF16)
    grad_v = (dv[...].astype(F32) + halo_ref[pl.ds(tokens, tokens)].astype(F32)).astype(BF16)
    grad_qlow_t = (2.0 * dot(bq[...], dqt[...])).astype(BF16)
    grad_vlow_t = (2.0 * dot(bv[...], grad_v, NT)).astype(BF16)
    out_s[...] = (
        gr[...]
        + dot(dqt[...], wq[...], TT)
        + dot(grad_k, wk[...], NT)
        + dot(grad_v, wv[...], NT)
        + dot(grad_qlow_t, aqt[...], TN)
        + dot(grad_vlow_t, avt[...], TN)
    )
    puts = [
        pltpu.make_async_copy(
            out_s.at[pl.ds(0, half)], out_hbm.at[0, pl.ds(near, half)], sems.at[11]
        ),
        pltpu.make_async_copy(
            out_s.at[pl.ds(half, half)], out_hbm.at[0, pl.ds(far, half)], sems.at[12]
        ),
    ]
    for copy in puts:
        copy.start()
    for copy in puts:
        copy.wait()


def call_inputs(halo, gr, dqt, dk, dv, wq, wk, wv, lows):
    tokens, width = gr.shape
    weights = (wq, wk, wv, *lows)
    return pl.pallas_call(
        inputs_kernel,
        out_shape=jax.ShapeDtypeStruct((1, tokens, width), F32),
        in_specs=[pl.BlockSpec(memory_space=pltpu.VMEM)] * 5
        + [pl.BlockSpec(memory_space=pltpu.HBM)] * len(weights),
        out_specs=pl.BlockSpec(memory_space=pltpu.HBM),
        scratch_shapes=[pltpu.VMEM(a.shape, a.dtype) for a in weights]
        + [pltpu.VMEM((tokens, width), F32), pltpu.SemaphoreType.DMA((13,))],
        compiler_params=pltpu.CompilerParams(vmem_limit_bytes=10 * 2**20),
        cost_estimate=pl.CostEstimate(flops=2 * 10**9, bytes_accessed=6 * 10**6, transcendentals=0),
    )(halo, gr, dqt, dk, dv, *in_hbm(*weights))


def finish_kernel(rank, count, *refs):
    ins, outs = refs[:count], refs[count : count + 8]
    scratch, singles, sems = refs[-6], refs[-5:-1], refs[-1]
    total = ins[0][...].astype(F32)
    for one in ins[1:]:
        total = total + one[...].astype(F32)
    scratch[...] = total
    copies = []
    for i, out in enumerate(outs):
        if i < 4:
            source = scratch.at[pl.ds(i * rank, rank)]
        else:
            source = singles[i - 4]
            source[...] = total[4 * rank + i - 4]
        copies.append(pltpu.make_async_copy(source, out, sems.at[i]))
    for copy in copies:
        copy.start()
    for copy in copies:
        copy.wait()


def call_finish(rank, parts):
    rows, width = parts[0].shape
    shape = jax.ShapeDtypeStruct
    return pl.pallas_call(
        functools.partial(finish_kernel, rank, len(parts)),
        out_shape=(shape((rank, width), F32),) * 4 + (shape((width,), F32),) * 4,
        in_specs=[pl.BlockSpec(memory_space=pltpu.VMEM)] * len(parts),
        out_specs=(pl.BlockSpec(memory_space=pltpu.HBM),) * 8,
        scratch_shapes=[pltpu.VMEM((rows, width), F32)]
        + [pltpu.VMEM((width,), F32)] * 4
        + [pltpu.SemaphoreType.DMA((8,))],
        compiler_params=pltpu.CompilerParams(vmem_limit_bytes=4 * 2**20),
    )(*parts)


def swapped(values, axis, partners):
    size = lax.axis_size(axis)
    return [values] + [
        lax.ppermute(values, axis, [(i, i ^ p) for i in range(size)]) for p in partners
    ]


def added(parts):
    total = parts[0].astype(F32)
    for one in parts[1:]:
        total = total + one.astype(F32)
    return total.astype(BF16)


def parts_of_sum(values, beside):
    parts = swapped(values, "seq", (1,))
    stride, size = 1, lax.axis_size("dp")
    while stride < size:
        radix = min(4, size // stride)
        parts = swapped(added(parts), "dp", [stride * k for k in range(1, radix)])
        if stride == 1:
            *parts, beside = lax.optimization_barrier((*parts, beside))
        stride *= radix
    return parts, beside


def body(
    inputs,
    pair_lengths,
    w_query,
    w_key,
    w_value,
    w_out,
    w_up,
    w_down,
    a_query,
    b_query,
    a_value,
    b_value,
    gain_one,
    shift_one,
    gain_two,
    shift_two,
    cotangent,
):
    rank = a_query.shape[1]
    swap = [(0, 1), (1, 0)]
    other = lax.ppermute(inputs, "seq", swap)
    lows = (a_query.T, b_query, a_value.T, b_value)
    gains = (gain_one, shift_one, gain_two, shift_two)
    projected = call_project(inputs, w_query, w_key, w_value, lows)
    output, gr, dqt, dk, dv, halo, packed = call_layer(
        pair_lengths, projected, other, gains, w_out, w_up, w_down, cotangent
    )
    halo = lax.ppermute(halo, "seq", swap)
    grad_inputs = call_inputs(halo, gr, dqt, dk, dv, w_query, w_key, w_value, lows)
    parts, grad_inputs = parts_of_sum(packed, grad_inputs)
    gaq, gbq, gav, gbv, *norms = call_finish(rank, parts)
    return (output, grad_inputs, gaq.T, gbq, gav.T, gbv, *norms)


def solution(mesh):
    tokens = P("dp", "seq", None)
    in_specs = (tokens, P("dp", None)) + (P(),) * 14 + (tokens,)
    out_specs = (tokens, tokens) + (P(),) * 8
    return jax.shard_map(body, mesh=mesh, in_specs=in_specs, out_specs=out_specs, check_vma=False)
```

time: 61.6 us -> 46.7 us (0.76)
  local copies, waits for them, and re-layouts: 6.7 us -> 0.01 us
  other arithmetic: 3.99 us -> 0.06 us
  Pallas kernels: 30.8 us -> 28.3 us
  waiting for transfers between devices: 8.82 us -> 7.15 us
    pallas_call x1, Pallas kernels: 25.7 us -> 19.2 us  [call_layer(): pl.pallas_call(layer_kernel, out_shape=(shape((1, tokens, width), BF16),...]
    pallas_call x1 -> x3, Pallas kernels: 5.17 us -> 9.08 us  [the longest x1 4.44 us: call_inputs(): pl.pallas_call(inputs_kernel, out_shape=jax.ShapeDtypeStruct((1, tokens,...]
    another operation x4 -> x0, local copies, waits for them, and re-layouts: 2.76 us -> none  [body(): gains = jnp.stack([gain_one, shift_one, gain_two, shift_two])]
    slice x4 -> x0, local copies, waits for them, and re-layouts: 2.31 us -> none  [the longest x1 1.02 us: body(): hk = lax.ppermute(dk[tokens:], 'seq', swap)]
    convert_element_type x3 -> x2, other arithmetic: 1.96 us -> 0.06 us  [added(): return total.astype(BF16)]
    ppermute x9 -> x8, waiting for transfers between devices: 8.81 us -> 7.15 us  [the longest x7 7.15 us: swapped(): lax.ppermute(values, axis, [(i, i ^ p) for i in range(size)])]
    unnamed x8 -> x2, local copies, waits for them, and re-layouts: 1.64 us -> 0.01 us
    concatenate x1 -> x0, other arithmetic: 1.37 us -> none  [body(): small = jnp.concatenate([a_query.T, b_query, a_value.T, b_value])]
  transfers between devices with their start and end apart: 10 -> 9, of which waited for: 6 -> 3; matrix products, arithmetic and copies ran while one was open for 12% -> 0% of each run, Pallas kernels for 0% -> 18%
where the time goes in v3:
time: 46.7 us; the launch traced here: 46.5 us
  Pallas kernels  28.3 us (61%)
  starting transfers between devices  10.1 us (22%)
  waiting for transfers between devices  7.15 us (15%)
  between operations  0.9 us (2%)
    pallas_call x1, Pallas kernels, call_layer(): pl.pallas_call(layer_kernel, out_shape=(shape((1, tokens, width), BF16),...  19.2 us
    ppermute x7, starting transfers between devices, swapped(): lax.ppermute(values, axis, [(i, i ^ p) for i in range(size)])  9.46 us
    ppermute x7, waiting for transfers between devices, swapped(): lax.ppermute(values, axis, [(i, i ^ p) for i in range(size)])  7.15 us
    pallas_call x1, Pallas kernels, call_inputs(): pl.pallas_call(inputs_kernel, out_shape=jax.ShapeDtypeStruct((1, tokens,...  4.44 us
    pallas_call x1, Pallas kernels, call_project(): pl.pallas_call(project_kernel, out_shape=(rows,) * 4 + (columns,) * 2 + (...  3.89 us
  transfers between devices with their start and end apart: 9, of which 3 were waited for; matrix products, arithmetic and copies ran while one was open for 0% of the time, Pallas kernels for 18%

profile of v3, /device:TPU:0, one launch (start us, length us, event | category | flops | bytes accessed | tf_op | source)
XLA Modules:
  0.0 46.5 jit_solution(15242480760121349265)
XLA Ops:
  0.6 0.5 %collective-permute-start = (bf16[1,256,768]{2,1,0:T(8,128)(2,1)}, bf16[1,256,768]{2,1,0:T(8,128)(2,1)S(1)}, u32[]{:S(2)}, u32[]{:S(2)}) collective-permute-start(bf16[1,256,768]{2,1,0:T(8,128)(2,1)} %x_hbm.1), channel_id=1, source_target_pairs={{0,1},{1,0},{2,3},{3,2},{4,5},{5,4},{6,7},{7,6},{8,9},{9,8},{10,11... | collective-permute-start | bytes 1179656 | tf_op jit(solution)/shard_map/ppermute | solution.py:715
  1.2 0.0 copy-start
  1.2 3.9 %shard_map.240 = (bf16[256,768]{1,0:T(8,128)(2,1)S(1)}, bf16[256,768]{1,0:T(8,128)(2,1)S(1)}, bf16[256,768]{1,0:T(8,128)(2,1)S(1)}, bf16[256,768]{1,0:T(8,128)(2...) custom-call(bf16[1,256,768]{2,1,0:T(8,128)(2,1)} %x_hbm.1, ...), custom_call_target="tpu_custom_call" | custom-call | flops 1000000000 | bytes 8000000 | tf_op jit(solution)/shard_map/pallas_call | solution.py:161
  5.1 0.0 collective-permute-done.other_ref
  5.1 0.0 copy-done
  5.1 19.2 %shard_map.241 = (bf16[1,256,768]{2,1,0:T(8,128)(2,1)}, f32[256,768]{1,0:T(8,128)S(1)}, bf16[768,256]{1,0:T(8,128)(2,1)S(1)}, bf16[256,768]{1,0:T(8,128)(2,1)S(1...) custom-call(s32[1,8]{1,0:T(1,128)S(1)} %copy-done, ...), custom_call_target="tpu_custom_call" | custom-call | flops 8999999488 | bytes 15000000 | tf_op jit(solution)/shard_map/pallas_call | solution.py:503
  24.3 0.1 collective-permute-start.5
  24.4 0.4 collective-permute-start.1
  24.9 1.9 %collective-permute-done.1 = bf16[48,768]{1,0:T(8,128)(2,1)S(1)} collective-permute-done((bf16[48,768]{1,0:T(8,128)(2,1)S(1)}, bf16[48,768]{1,0:T(8,128)(2,1)S(1)}, u32[]{:S(2)}, u32[]{:S(2)}) %collective-permute-start.1) | collective-permute-done | bytes 73760 | tf_op jit(solution)/shard_map/ppermute | solution.py:671
  26.8 3.7 %collective-permute-start.4 = (bf16[48,768]{1,0:T(8,128)(2,1)S(1)}, bf16[48,768]{1,0:T(8,128)(2,1)S(1)}, u32[]{:S(2)}, u32[]{:S(2)}) collective-permute-start(bf16[48,768]{1,0:T(8,128)(2,1)S(1)} %add_convert_fusion.1), channel_id=1, source_target_pairs={{0,6},{2,4},{4,2},{6,0},{8,14},{10,12},{12,10},{14,8},{16,22},{18,... | collective-permute-start | bytes 221192 | tf_op jit(solution)/shard_map/ppermute | solution.py:671
  30.4 0.5 %collective-permute-start.3 = (bf16[48,768]{1,0:T(8,128)(2,1)S(1)}, bf16[48,768]{1,0:T(8,128)(2,1)S(1)}, u32[]{:S(2)}, u32[]{:S(2)}) collective-permute-start(bf16[48,768]{1,0:T(8,128)(2,1)S(1)} %add_convert_fusion.1), channel_id=1, source_target_pairs={{0,4},{2,6},{4,0},{6,2},{8,12},{10,14},{12,8},{14,10},{16,20},{18,... | collective-permute-start | bytes 221192 | tf_op jit(solution)/shard_map/ppermute | solution.py:671
  31.0 0.1 collective-permute-start.2
  31.1 0.0 collective-permute-done.5.halo_ref
  31.1 4.4 %shard_map.242 = f32[1,256,768]{2,1,0:T(8,128)} custom-call(bf16[512,768]{1,0:T(8,128)(2,1)S(1)} %collective-permute-done.5.halo_ref, f32[256,768]{1,0:T(8,128)S(1)} %get-tuple-element.59.gr, bf16[768,256]{1,0:T(8,128)(2,1)S(1)} %get-tuple-element.60.dqt, bf16[256,768]{1,0:T(8,128)(2,1)S(1)} %get-tuple-element.61.dk, ...), custom_call_target="tpu_custom_call" | custom-call | flops 2000000000 | bytes 6000000 | tf_op jit(solution)/shard_map/pallas_call | solution.py:619
  35.5 0.0 collective-permute-done.4
  35.5 0.0 collective-permute-done.3
  35.6 0.0 collective-permute-done.2
  35.6 4.1 %collective-permute-start.8 = (bf16[48,768]{1,0:T(8,128)(2,1)S(1)}, bf16[48,768]{1,0:T(8,128)(2,1)S(1)}, u32[]{:S(2)}, u32[]{:S(2)}) collective-permute-start(bf16[48,768]{1,0:T(8,128)(2,1)S(1)} %add_convert_fusion.refs_0_), channel_id=1, source_target_pairs={{0,24},{2,26},{4,28},{6,30},{8,16},{10,18},{12,20},{14,22},{16,8},... | collective-permute-start | bytes 221192 | tf_op jit(solution)/shard_map/ppermute | solution.py:671
  39.7 0.0 collective-permute-start.7
  39.7 0.6 %collective-permute-start.6 = (bf16[48,768]{1,0:T(8,128)(2,1)S(1)}, bf16[48,768]{1,0:T(8,128)(2,1)S(1)}, u32[]{:S(2)}, u32[]{:S(2)}) collective-permute-start(bf16[48,768]{1,0:T(8,128)(2,1)S(1)} %add_convert_fusion.refs_0_), channel_id=1, source_target_pairs={{0,8},{2,10},{4,12},{6,14},{8,0},{10,2},{12,4},{14,6},{16,24},{18,... | collective-permute-start | bytes 221192 | tf_op jit(solution)/shard_map/ppermute | solution.py:671
  40.3 2.4 %collective-permute-done.8.refs_3_ = bf16[48,768]{1,0:T(8,128)(2,1)S(1)} collective-permute-done((bf16[48,768]{1,0:T(8,128)(2,1)S(1)}, bf16[48,768]{1,0:T(8,128)(2,1)S(1)}, u32[]{:S(2)}, u32[]{:S(2)}) %collective-permute-start.8) | collective-permute-done | bytes 73760 | tf_op jit(solution)/shard_map/ppermute | solution.py:671
  42.7 2.9 %collective-permute-done.7.refs_2_ = bf16[48,768]{1,0:T(8,128)(2,1)S(1)} collective-permute-done((bf16[48,768]{1,0:T(8,128)(2,1)S(1)}, bf16[48,768]{1,0:T(8,128)(2,1)S(1)}, u32[]{:S(2)}, u32[]{:S(2)}) %collective-permute-start.7) | collective-permute-done | bytes 73760 | tf_op jit(solution)/shard_map/ppermute | solution.py:671
  45.6 0.0 collective-permute-done.6.refs_1_
  45.6 0.7 %shard_map.243 = (f32[8,768]{1,0:T(8,128)}, f32[8,768]{1,0:T(8,128)}, f32[8,768]{1,0:T(8,128)}, f32[8,768]{1,0:T(8,128)}, f32[768]{0:T(1024)}, /*index=5*/f32[768]{0:T(1024)}, f32[768]{0:T(1024)}, f32[768]{0:T(1024)}) custom-call(bf16[48,768]{1,0:T(8,128)(2,1)S(1)} %add_convert_fusion.refs_0_, bf16[48,768]{1,0:T(8,128)(2,1)S(1)} %collective-permute-done.6.refs_1_, ...), custom_call_target="tpu_custom_call" | custom-call | tf_op jit(solution)/shard_map/pallas_call | solution.py:656
  (2 shorter events, 0.1 us)
Async XLA Ops:
  0.6 4.4 %collective-permute-start = (bf16[1,256,768]{2,1,0:T(8,128)(2,1)}, bf16[1,256,768]{2,1,0:T(8,128)(2,1)S(1)}, u32[]{:S(2)}, u32[]{:S(2)}) collective-permute-start(bf16[1,256,768]{2,1,0:T(8,128)(2,1)} %x_hbm.1), channel_id=1, source_target_pairs={{0,1},{1,0},{2,3},{3,2},{4,5},{5,4},{6,7},{7,6},{8,9},{9,8},{10,11... | collective-permute-start | bytes 1179656 | tf_op jit(solution)/shard_map/ppermute | solution.py:715
  1.2 3.9 %copy-start = (s32[1,8]{1,0:T(1,128)S(1)}, s32[1,8]{1,0:T(1,128)}, u32[]{:S(2)}) copy-start(s32[1,8]{1,0:T(1,128)} %lengths_ref.1) | copy-start | bytes 100
  24.3 6.8 %collective-permute-start.5 = (bf16[512,768]{1,0:T(8,128)(2,1)S(1)}, bf16[512,768]{1,0:T(8,128)(2,1)S(1)}, u32[]{:S(2)}, u32[]{:S(2)}) collective-permute-start(bf16[512,768]{1,0:T(8,128)(2,1)S(1)} %get-tuple-element.58), channel_id=1, source_target_pairs={{0,1},{1,0},{2,3},{3,2},{4,5},{5,4},{6,7},{7,6},{8,9},{9,8},{10,11... | collective-permute-start | bytes 2359304 | tf_op jit(solution)/shard_map/ppermute | solution.py:722
  24.4 2.3 %collective-permute-start.1 = (bf16[48,768]{1,0:T(8,128)(2,1)S(1)}, bf16[48,768]{1,0:T(8,128)(2,1)S(1)}, u32[]{:S(2)}, u32[]{:S(2)}) collective-permute-start(bf16[48,768]{1,0:T(8,128)(2,1)S(1)} %get-tuple-element.57), channel_id=1, source_target_pairs={{0,1},{1,0},{2,3},{3,2},{4,5},{5,4},{6,7},{7,6},{8,9},{9,8},{10,11... | collective-permute-start | bytes 221192 | tf_op jit(solution)/shard_map/ppermute | solution.py:671
  26.8 8.8 %collective-permute-start.4 = (bf16[48,768]{1,0:T(8,128)(2,1)S(1)}, bf16[48,768]{1,0:T(8,128)(2,1)S(1)}, u32[]{:S(2)}, u32[]{:S(2)}) collective-permute-start(bf16[48,768]{1,0:T(8,128)(2,1)S(1)} %add_convert_fusion.1), channel_id=1, source_target_pairs={{0,6},{2,4},{4,2},{6,0},{8,14},{10,12},{12,10},{14,8},{16,22},{18,... | collective-permute-start | bytes 221192 | tf_op jit(solution)/shard_map/ppermute | solution.py:671
  30.4 5.1 %collective-permute-start.3 = (bf16[48,768]{1,0:T(8,128)(2,1)S(1)}, bf16[48,768]{1,0:T(8,128)(2,1)S(1)}, u32[]{:S(2)}, u32[]{:S(2)}) collective-permute-start(bf16[48,768]{1,0:T(8,128)(2,1)S(1)} %add_convert_fusion.1), channel_id=1, source_target_pairs={{0,4},{2,6},{4,0},{6,2},{8,12},{10,14},{12,8},{14,10},{16,20},{18,... | collective-permute-start | bytes 221192 | tf_op jit(solution)/shard_map/ppermute | solution.py:671
  31.0 4.6 %collective-permute-start.2 = (bf16[48,768]{1,0:T(8,128)(2,1)S(1)}, bf16[48,768]{1,0:T(8,128)(2,1)S(1)}, u32[]{:S(2)}, u32[]{:S(2)}) collective-permute-start(bf16[48,768]{1,0:T(8,128)(2,1)S(1)} %add_convert_fusion.1), channel_id=1, source_target_pairs={{0,2},{2,0},{4,6},{6,4},{8,10},{10,8},{12,14},{14,12},{16,18},{18,... | collective-permute-start | bytes 221192 | tf_op jit(solution)/shard_map/ppermute | solution.py:671
  35.6 7.1 %collective-permute-start.8 = (bf16[48,768]{1,0:T(8,128)(2,1)S(1)}, bf16[48,768]{1,0:T(8,128)(2,1)S(1)}, u32[]{:S(2)}, u32[]{:S(2)}) collective-permute-start(bf16[48,768]{1,0:T(8,128)(2,1)S(1)} %add_convert_fusion.refs_0_), channel_id=1, source_target_pairs={{0,24},{2,26},{4,28},{6,30},{8,16},{10,18},{12,20},{14,22},{16,8},... | collective-permute-start | bytes 221192 | tf_op jit(solution)/shard_map/ppermute | solution.py:671
  39.7 5.9 %collective-permute-start.7 = (bf16[48,768]{1,0:T(8,128)(2,1)S(1)}, bf16[48,768]{1,0:T(8,128)(2,1)S(1)}, u32[]{:S(2)}, u32[]{:S(2)}) collective-permute-start(bf16[48,768]{1,0:T(8,128)(2,1)S(1)} %add_convert_fusion.refs_0_), channel_id=1, source_target_pairs={{0,16},{2,18},{4,20},{6,22},{8,24},{10,26},{12,28},{14,30},{16,0},... | collective-permute-start | bytes 221192 | tf_op jit(solution)/shard_map/ppermute | solution.py:671
  39.7 5.9 %collective-permute-start.6 = (bf16[48,768]{1,0:T(8,128)(2,1)S(1)}, bf16[48,768]{1,0:T(8,128)(2,1)S(1)}, u32[]{:S(2)}, u32[]{:S(2)}) collective-permute-start(bf16[48,768]{1,0:T(8,128)(2,1)S(1)} %add_convert_fusion.refs_0_), channel_id=1, source_target_pairs={{0,8},{2,10},{4,12},{6,14},{8,0},{10,2},{12,4},{14,6},{16,24},{18,... | collective-permute-start | bytes 221192 | tf_op jit(solution)/shard_map/ppermute | solution.py:671

commit v4 on v3

--- a/solution.py
+++ b/solution.py
@@ -10,6 +10,7 @@
 
 DH = 64
 LANES = 128
+EARLY = 3
 EPSILON = 1e-05
 LOG2_E = math.log2(math.e)
 FAR_AWAY = -1e30
@@ -41,19 +42,8 @@
 
 
 def gelu_and_slope(values):
-    size = jnp.abs(values)
-    inv = 1.0 / (1.0 + (0.3275911 / math.sqrt(2.0)) * size)
+    below = 0.5 + 0.5 * lax.erf(values * (1.0 / math.sqrt(2.0)))
     bell = jnp.exp2(values * values * (-0.5 * LOG2_E))
-    tail = inv * (
-        0.5 * 0.254829592
-        + inv
-        * (
-            0.5 * -0.284496736
-            + inv * (0.5 * 1.421413741 + inv * (0.5 * -1.453152027 + inv * (0.5 * 1.061405429)))
-        )
-    )
-    tail = tail * bell
-    below = jnp.where(values < 0.0, tail, 1.0 - tail)
     return values * below, below + values * bell * (1.0 / math.sqrt(2.0 * math.pi))
 
 
@@ -97,6 +87,8 @@
     bq_hbm,
     avt_hbm,
     bv_hbm,
+    wo_hbm,
+    wu_hbm,
     x_ref,
     q_ref,
     k_ref,
@@ -110,6 +102,8 @@
     bq,
     avt,
     bv,
+    wo,
+    wu,
     wq,
     aqt,
     sems,
@@ -127,6 +121,8 @@
         (bv_hbm, bv),
         (wq_hbm, wq),
         (wv_hbm, wv),
+        (wo_hbm, wo),
+        (wu_hbm.at[:, pl.ds(0, wu.shape[1])], wu),
     )
     copies = [pltpu.make_async_copy(a, b, sems.at[i]) for i, (a, b) in enumerate(pairs)]
     for copy in copies:
@@ -137,7 +133,7 @@
     keys = dot(x, wk[...]).astype(BF16)
     k_ref[...] = keys
     kt_ref[...] = keys.T
-    for copy in copies[3:]:
+    for copy in copies[3:9]:
         copy.wait()
     qlow_t = dot(aqt[...], x, NT).astype(BF16)
     vlow_t = dot(avt[...], x, NT).astype(BF16)
@@ -149,9 +145,11 @@
     vals = (dot(x, wv[...]) + 2.0 * dot(vlow_t, bv[...], TN)).astype(BF16)
     v_ref[...] = vals
     vt_ref[...] = vals.T
-
-
-def call_project(x, wq, wk, wv, lows):
+    for copy in copies[9:]:
+        copy.wait()
+
+
+def call_project(x, wq, wk, wv, lows, wo, wu):
     _, tokens, width = x.shape
     rank = lows[1].shape[0]
     shape = jax.ShapeDtypeStruct
@@ -160,17 +158,22 @@
     square, flat = shape((width, width), BF16), shape((rank, width), BF16)
     return pl.pallas_call(
         project_kernel,
-        out_shape=(rows,) * 4 + (columns,) * 2 + (low,) * 2 + (square,) * 2 + (flat,) * 3,
-        in_specs=[pl.BlockSpec(memory_space=pltpu.HBM)] * 8,
-        out_specs=(pl.BlockSpec(memory_space=pltpu.VMEM),) * 13,
+        out_shape=(rows,) * 4
+        + (columns,) * 2
+        + (low,) * 2
+        + (square,) * 2
+        + (flat,) * 3
+        + (square, shape((width, EARLY * width), BF16)),
+        in_specs=[pl.BlockSpec(memory_space=pltpu.HBM)] * 10,
+        out_specs=(pl.BlockSpec(memory_space=pltpu.VMEM),) * 15,
         scratch_shapes=[
             pltpu.VMEM((width, width), BF16),
             pltpu.VMEM((rank, width), BF16),
-            pltpu.SemaphoreType.DMA((9,)),
+            pltpu.SemaphoreType.DMA((11,)),
         ],
-        compiler_params=pltpu.CompilerParams(vmem_limit_bytes=14 * 2**20),
+        compiler_params=pltpu.CompilerParams(vmem_limit_bytes=20 * 2**20),
         cost_estimate=pl.CostEstimate(flops=10**9, bytes_accessed=8 * 10**6, transcendentals=0),
-    )(*in_hbm(x, wq, wk, wv, *lows))
+    )(*in_hbm(x, wq, wk, wv, *lows, wo, wu))
 
 
 def layer_kernel(
@@ -188,12 +191,13 @@
     bq_ref,
     avt_ref,
     bv_ref,
+    wo,
+    wu_early,
     other_ref,
     gain_one_hbm,
     shift_one_hbm,
     gain_two_hbm,
     shift_two_hbm,
-    wo_hbm,
     wu_hbm,
     wd_hbm,
     cot_hbm,
@@ -209,16 +213,14 @@
     gain_two_s,
     shift_two_s,
     x_s,
-    wo,
-    wu,
+    wu_late,
     wd,
     cot_s,
     kh_s,
     vh_s,
     kht_s,
     vht_s,
-    po_s,
-    ph_s,
+    p_s,
     inv_s,
     ct_s,
     normal_s,
@@ -247,19 +249,25 @@
         copy.start()
         return copy
 
-    get_o = [
-        fetch(wo_hbm, wo),
+    get_gains = [
         fetch(gain_one_hbm, gain_one_s),
         fetch(shift_one_hbm, shift_one_s),
         fetch(gain_two_hbm, gain_two_s),
         fetch(shift_two_hbm, shift_two_s),
     ]
     chunks = hidden // width
-    get_u, get_d = [], []
+    early = wu_early.shape[1]
+    get_ffn = [fetch(wu_hbm.at[:, pl.ds(early, hidden - early)], wu_late)]
     for c in range(chunks):
         part = pl.ds(c * width, width)
-        get_u.append(fetch(wu_hbm.at[:, part], wu.at[:, part]))
-        get_d.append(fetch(wd_hbm.at[part], wd.at[part]))
+        get_ffn.append(fetch(wd_hbm.at[part], wd.at[part]))
+
+    def wu_part(c):
+        start = c * width
+        if start < early:
+            return wu_early[:, pl.ds(start, width)]
+        return wu_late[:, pl.ds(start - early, width)]
+
     get_cot = [
         fetch(cot_hbm.at[0, pl.ds(near, half)], cot_s.at[pl.ds(0, half)]),
         fetch(cot_hbm.at[0, pl.ds(far, half)], cot_s.at[pl.ds(half, half)]),
@@ -271,7 +279,7 @@
     halo_segment = segment_codes(lengths_ref, halo_base + far, halo_base + near, tokens)
     lane = lax.broadcasted_iota(jnp.int32, (tokens, LANES), 1)
     code = lane & (DH - 1)
-    low_half = lane < DH
+    low_lanes = lax.broadcasted_iota(jnp.int32, (2 * tokens, LANES), 1) < DH
     marks = lengths_ref.shape[1] + 1
     q_code = jnp.where(code == own_segment, 1.0, 0.0).astype(BF16)
 
@@ -309,108 +317,149 @@
             return join(own, halo)
         return jnp.concatenate([join(own[:, :reach], halo), own[:, reach:]], axis=1)
 
-    def attend(pair, reach):
-        lanes = pl.ds(pl.multiple_of(pair * LANES, LANES), LANES)
+    def padded(halo, reach):
+        if reach == tokens:
+            return halo
+        return jnp.concatenate([halo, jnp.zeros((reach, tokens - reach), halo.dtype)], axis=1)
+
+    def lanes_of(pair):
+        return pl.ds(pl.multiple_of(pair * LANES, LANES), LANES)
+
+    def rows_of(pair, odd):
+        return pl.ds(pl.multiple_of(pair * LANES + odd * DH, DH), DH)
+
+    def score(pair, odd, reach):
+        lanes = lanes_of(pair)
+
+        def mixed(values, codes):
+            mask = low_lanes[: values.shape[0]]
+            if odd:
+                return jnp.where(mask, codes, values)
+            return jnp.where(mask, values, codes)
+
+        k_pair = jnp.concatenate([k_s[:, lanes], kh_s[pl.ds(0, reach), lanes]], axis=0)
+        k_code = jnp.concatenate([ko_code, kh_code[:reach]], axis=0)
+        return dot(mixed(k_pair, k_code), mixed(q_s[:, lanes], q_code), NT)
+
+    def soften(pair, odd, reach, scores):
+        head = 2 * pair + odd
+        own, halo = scores[:tokens], scores[tokens:, :reach]
+        peak = joined(
+            jnp.max(own, axis=0, keepdims=True),
+            jnp.max(halo, axis=0, keepdims=True),
+            reach,
+            jnp.maximum,
+        )
+        own = jnp.exp2(own - peak)
+        halo = jnp.exp2(halo - peak[:, :reach])
+        inverse = 1.0 / joined(
+            jnp.sum(own, axis=0, keepdims=True),
+            jnp.sum(halo, axis=0, keepdims=True),
+            reach,
+            jnp.add,
+        )
+        own, halo = own.astype(BF16), padded(halo.astype(BF16), reach)
+        p_s[head, pl.ds(0, tokens)] = own
+        p_s[head, pl.ds(tokens, reach)] = halo
+        inv_s[head] = jnp.broadcast_to(inverse, inv_s.shape[1:])
+        return own, halo, inverse
+
+    def attend(pair, odd, reach, soft):
+        own, halo, inverse = soft
+        rows = rows_of(pair, odd)
+        context = dot(vt_s[rows, :], own) + dot(vht_s[rows, pl.ds(0, reach)], halo)
+        ct_s[rows, :] = (context * inverse).astype(BF16)
+
+    def back_score(pair, odd, reach):
+        lanes = lanes_of(pair)
+        inverse = inv_s[2 * pair + odd, pl.ds(0, 1), :]
+        grad = (dot_s[rows_of(pair, odd), :] * inverse).astype(BF16)
+        blank = jnp.zeros_like(grad)
+        grad = jnp.concatenate([blank, grad] if odd else [grad, blank], axis=0)
+        own = dot(v_s[:, lanes], grad)
+        halo = dot(vh_s[pl.ds(0, reach), lanes], grad[:, :reach])
+        return inverse, grad, own, halo
+
+    evens = {}
+
+    def back_soften(pair, odd, reach, slopes):
+        head = 2 * pair + odd
+        inverse, grad, own, halo = slopes
+        p_own, p_halo = p_s[head, pl.ds(0, tokens)], p_s[head, pl.ds(tokens, reach), pl.ds(0, reach)]
+        po, ph = p_own.astype(F32), p_halo.astype(F32)
+        own, halo = po * own, ph * halo
+        inner = inverse * joined(
+            jnp.sum(own, axis=0, keepdims=True),
+            jnp.sum(halo, axis=0, keepdims=True),
+            reach,
+            jnp.add,
+        )
+        own = (own - po * inner).astype(BF16)
+        halo = (halo - ph * inner[:, :reach]).astype(BF16)
+        return grad, p_own, p_halo, own, halo
+
+    def attend_back(pair, odd, reach, soft):
+        lanes, rows = lanes_of(pair), rows_of(pair, odd)
+        grad, p_own, p_halo, own, halo = soft
         q_pair = q_s[:, lanes]
-        ko_pair = k_s[:, lanes]
-        kh_pair = kh_s[pl.ds(0, reach), lanes]
-        for odd in range(2):
-            head = 2 * pair + odd
-            rows = pl.ds(pl.multiple_of(head * DH, DH), DH)
-
-            def mixed(values, codes):
-                mask = low_half[: values.shape[0]]
-                if odd:
-                    return jnp.where(mask, codes, values)
-                return jnp.where(mask, values, codes)
-
-            q_head = mixed(q_pair, q_code)
-            own = dot(mixed(ko_pair, ko_code), q_head, NT)
-            halo = dot(mixed(kh_pair, kh_code[:reach]), q_head[:reach], NT)
-            peak = joined(
-                jnp.max(own, axis=0, keepdims=True),
-                jnp.max(halo, axis=0, keepdims=True),
-                reach,
-                jnp.maximum,
-            )
-            own = jnp.exp2(own - peak)
-            halo = jnp.exp2(halo - peak[:, :reach])
-            inverse = 1.0 / joined(
-                jnp.sum(own, axis=0, keepdims=True),
-                jnp.sum(halo, axis=0, keepdims=True),
-                reach,
-                jnp.add,
-            )
-            own, halo = own.astype(BF16), halo.astype(BF16)
-            po_s[head] = own
-            ph_s[head, pl.ds(0, reach), pl.ds(0, reach)] = halo
-            inv_s[head] = jnp.broadcast_to(inverse, inv_s.shape[1:])
-            context = joined(
-                dot(vt_s[rows, :], own),
-                dot(vht_s[rows, pl.ds(0, reach)], halo),
-                reach,
-                jnp.add,
-            )
-            ct_s[rows, :] = (context * inverse).astype(BF16)
-
-    def attend_back(pair, reach):
-        lanes = pl.ds(pl.multiple_of(pair * LANES, LANES), LANES)
-        q_pair = q_s[:, lanes]
-        vo_pair = v_s[:, lanes]
-        vh_pair = vh_s[pl.ds(0, reach), lanes]
-        dv_own, dv_halo, dk_own, dk_halo = [], [], [], []
-        for odd in range(2):
-            head = 2 * pair + odd
-            rows = pl.ds(pl.multiple_of(head * DH, DH), DH)
-            inverse = inv_s[head, pl.ds(0, 1), :]
-            grad = (dot_s[rows, :] * inverse).astype(BF16)
-            blank = jnp.zeros_like(grad)
-            grad = jnp.concatenate([blank, grad] if odd else [grad, blank], axis=0)
-            po, ph = po_s[head], ph_s[head, pl.ds(0, reach), pl.ds(0, reach)]
-            own = po.astype(F32) * dot(vo_pair, grad)
-            halo = ph.astype(F32) * dot(vh_pair, grad[:, :reach])
-            inner = inverse * joined(
-                jnp.sum(own, axis=0, keepdims=True),
-                jnp.sum(halo, axis=0, keepdims=True),
-                reach,
-                jnp.add,
-            )
-            own = (own - po.astype(F32) * inner).astype(BF16)
-            halo = (halo - ph.astype(F32) * inner[:, :reach]).astype(BF16)
-            dv_own.append(dot(po, grad, NT))
-            dv_halo.append(dot(ph, grad[:, :reach], NT))
-            dk_own.append(dot(own, q_pair))
-            dk_halo.append(dot(halo, q_pair[:reach]))
-            dqt = joined(
-                dot(kt_s[rows, :], own),
-                dot(kht_s[rows, pl.ds(0, reach)], halo),
-                reach,
-                jnp.add,
-            )
-            dqt_s[rows, :] = (dqt * (1.0 / math.sqrt(DH))).astype(BF16)
+        parts = (
+            dot(p_own, grad, NT),
+            dot(p_halo, grad[:, :reach], NT),
+            dot(own, q_pair),
+            dot(halo, q_pair[:reach]),
+        )
+        dq = joined(
+            dot(kt_s[rows, :], own),
+            dot(kht_s[rows, pl.ds(0, reach)], halo),
+            reach,
+            jnp.add,
+        )
+        dqt_s[rows, :] = (dq * (1.0 / math.sqrt(DH))).astype(BF16)
+        if not odd:
+            evens[0] = parts
+            return
+        even = evens.pop(0)
         unscale = 1.0 / LOG2_E
-        dv_s[:, lanes] = (dv_own[0] + dv_own[1]).astype(BF16)
-        halo_s[pl.ds(tokens, reach), lanes] = (dv_halo[0] + dv_halo[1]).astype(BF16)
+        dv_s[:, lanes] = (even[0] + parts[0]).astype(BF16)
+        halo_s[pl.ds(tokens, reach), lanes] = (even[1] + parts[1]).astype(BF16)
         dk_s[:, lanes] = (
-            jnp.where(low_half, dk_own[0], dk_own[1]) * unscale
+            jnp.where(low_lanes[:tokens], even[2], parts[2]) * unscale
         ).astype(BF16)
         halo_s[pl.ds(0, reach), lanes] = (
-            jnp.where(low_half[:reach], dk_halo[0], dk_halo[1]) * unscale
+            jnp.where(low_lanes[:reach], even[3], parts[3]) * unscale
         ).astype(BF16)
 
-    def for_pairs(step):
+    def for_heads(first, second, third, lags):
         @pl.when(jnp.logical_not(wide))
         def _():
-            for pair in range(heads // 2):
-                step(pair, half)
+            todo = [(pair, odd) for pair in range(heads // 2) for odd in range(2)]
+            one, two = {}, {}
+            for at in range(len(todo) + lags[1]):
+                if at < len(todo):
+                    one[at] = first(*todo[at], half)
+                back = at - lags[0]
+                if 0 <= back < len(todo):
+                    two[back] = second(*todo[back], half, one.pop(back))
+                back = at - lags[1]
+                if 0 <= back:
+                    third(*todo[back], half, two.pop(back))
 
         @pl.when(wide)
         def _():
-            lax.fori_loop(0, heads // 2, lambda pair, none: step(pair, tokens), None)
-
-    for_pairs(attend)
-
-    for copy in get_o:
+            def step(pair, none):
+                for odd in range(2):
+                    third(
+                        pair,
+                        odd,
+                        tokens,
+                        second(pair, odd, tokens, first(pair, odd, tokens)),
+                    )
+
+            lax.fori_loop(0, heads // 2, step, None)
+
+    for_heads(score, soften, attend, (2, 4))
+
+    for copy in get_gains:
         copy.wait()
     resid_one = x_ref[...].astype(F32) + dot(ct_s[...], wo[...], TN)
     normal, inverse = normed(resid_one)
@@ -421,11 +470,11 @@
     hidden_one = normal * gain_one + shift_one
     hidden_s[...] = hidden_one.astype(BF16)
     total_s[...] = hidden_one
-    for copy in get_u + get_d:
+    for copy in get_ffn:
         copy.wait()
     for c in range(chunks):
         part = pl.ds(c * width, width)
-        upward = dot(hidden_s[...], wu[:, part])
+        upward = dot(hidden_s[...], wu_part(c))
         value, slope = gelu_and_slope(upward)
         active_s[:, part] = value.astype(BF16)
         slope_s[:, part] = slope.astype(BF16)
@@ -452,7 +501,7 @@
         part = pl.ds(c * width, width)
         grad_up = slope_s[:, part].astype(F32) * dot(hidden_s[...], wd[part, :], NT)
         active_s[:, part] = grad_up.astype(BF16)
-        total_s[...] += dot(active_s[:, part], wu[:, part], NT)
+        total_s[...] += dot(active_s[:, part], wu_part(c), NT)
     grad_hidden = total_s[...]
     normal = normal_s[...]
     grad_gain_one = jnp.sum(grad_hidden * normal, axis=0, keepdims=True)
@@ -466,7 +515,7 @@
         halo_s[pl.ds(half, half)] = jnp.zeros((half, width), BF16)
         halo_s[pl.ds(tokens + half, half)] = jnp.zeros((half, width), BF16)
 
-    for_pairs(attend_back)
+    for_heads(back_score, back_soften, attend_back, (2, 4))
 
     dv_halo = halo_s[pl.ds(tokens, tokens)]
     x_own = x_ref[...]
@@ -490,12 +539,12 @@
         copy.wait()
 
 
-def call_layer(lengths, projected, other, gains, wo, wu, wd, cotangent):
+def call_layer(lengths, projected, other, gains, wu, wd, cotangent):
     _, tokens, width = other.shape
     hidden = wu.shape[1]
     heads = width // DH
-    rank = projected[-1].shape[0]
-    packed_rows = -(-(4 * rank + 4) // 16) * 16
+    rank = projected[6].shape[0]
+    packed_rows = -(-(4 * rank + 4) // 8) * 8
     hbm = pl.BlockSpec(memory_space=pltpu.HBM)
     here = pl.BlockSpec(memory_space=pltpu.VMEM)
     shape = jax.ShapeDtypeStruct
@@ -511,7 +560,7 @@
             shape((2 * tokens, width), BF16),
             shape((packed_rows, width), BF16),
         ),
-        in_specs=[pl.BlockSpec(memory_space=pltpu.SMEM)] + [here] * 14 + [hbm] * 8,
+        in_specs=[pl.BlockSpec(memory_space=pltpu.SMEM)] + [here] * 16 + [hbm] * 7,
         out_specs=(hbm,) + (here,) * 6,
         scratch_shapes=[
             vmem((width,), F32),
@@ -519,16 +568,14 @@
             vmem((width,), F32),
             vmem((width,), F32),
             vmem((tokens, width), BF16),
-            vmem(wo.shape, BF16),
-            vmem(wu.shape, BF16),
+            vmem((width, hidden - EARLY * width), BF16),
             vmem(wd.shape, BF16),
             vmem((tokens, width), BF16),
             vmem((tokens, width), BF16),
             vmem((tokens, width), BF16),
             vmem((width, tokens), BF16),
             vmem((width, tokens), BF16),
-            vmem((heads, tokens, tokens), BF16),
-            vmem((heads, tokens, tokens), BF16),
+            vmem((heads, 2 * tokens, tokens), BF16),
             vmem((heads, 8, tokens), F32),
             vmem((width, tokens), BF16),
             vmem((tokens, width), F32),
@@ -541,9 +588,9 @@
             vmem((width, tokens), F32),
             pltpu.SemaphoreType.DMA((32,)),
         ],
-        compiler_params=pltpu.CompilerParams(vmem_limit_bytes=44 * 2**20),
+        compiler_params=pltpu.CompilerParams(vmem_limit_bytes=36 * 2**20),
         cost_estimate=pl.CostEstimate(flops=9 * 10**9, bytes_accessed=15 * 10**6, transcendentals=0),
-    )(lengths, *projected, other, *in_hbm(*gains, wo, wu, wd, cotangent))
+    )(lengths, *projected, other, *in_hbm(*gains, wu, wd, cotangent))
 
 
 def inputs_kernel(
@@ -683,10 +730,11 @@
     parts = swapped(values, "seq", (1,))
     stride, size = 1, lax.axis_size("dp")
     while stride < size:
+        values = added(parts)
+        if stride == 1:
+            beside, values = lax.optimization_barrier((beside, values))
         radix = min(4, size // stride)
-        parts = swapped(added(parts), "dp", [stride * k for k in range(1, radix)])
-        if stride == 1:
-            *parts, beside = lax.optimization_barrier((*parts, beside))
+        parts = swapped(values, "dp", [stride * k for k in range(1, radix)])
         stride *= radix
     return parts, beside
 
@@ -715,13 +763,14 @@
     other = lax.ppermute(inputs, "seq", swap)
     lows = (a_query.T, b_query, a_value.T, b_value)
     gains = (gain_one, shift_one, gain_two, shift_two)
-    projected = call_project(inputs, w_query, w_key, w_value, lows)
+    projected = call_project(inputs, w_query, w_key, w_value, lows, w_out, w_up)
     output, gr, dqt, dk, dv, halo, packed = call_layer(
-        pair_lengths, projected, other, gains, w_out, w_up, w_down, cotangent
+        pair_lengths, projected, other, gains, w_up, w_down, cotangent
     )
+    parts, halo = parts_of_sum(packed, halo)
     halo = lax.ppermute(halo, "seq", swap)
     grad_inputs = call_inputs(halo, gr, dqt, dk, dv, w_query, w_key, w_value, lows)
-    parts, grad_inputs = parts_of_sum(packed, grad_inputs)
+    *parts, grad_inputs = lax.optimization_barrier((*parts, grad_inputs))
     gaq, gbq, gav, gbv, *norms = call_finish(rank, parts)
     return (output, grad_inputs, gaq.T, gbq, gav.T, gbv, *norms)
 

time: 46.7 us -> 39.9 us (0.85)
  Pallas kernels: 28.3 us -> 23.7 us
  waiting for transfers between devices: 7.15 us -> 5.37 us
    pallas_call x1, Pallas kernels: 19.2 us -> 14.7 us  [call_layer(): pl.pallas_call(layer_kernel, out_shape=(shape((1, tokens, width), BF16),...]
    ppermute x7, waiting for transfers between devices: 7.15 us -> 5.36 us  [swapped(): lax.ppermute(values, axis, [(i, i ^ p) for i in range(size)])]
    ppermute x7, starting transfers between devices: 9.46 us -> 8.93 us  [swapped(): lax.ppermute(values, axis, [(i, i ^ p) for i in range(size)])]
  transfers between devices with their start and end apart: 9 -> 9, of which waited for: 3 -> 4; matrix products, arithmetic and copies ran while one was open for 0% -> 0% of each run, Pallas kernels for 18% -> 21%
where the time goes in v4:
time: 39.9 us; the launch traced here: 39.7 us
  Pallas kernels  23.7 us (59%)
  starting transfers between devices  9.67 us (24%)
  waiting for transfers between devices  5.37 us (13%)
  between operations  0.9 us (2%)
    pallas_call x1, Pallas kernels, call_layer(): pl.pallas_call(layer_kernel, out_shape=(shape((1, tokens, width), BF16),...  14.7 us
    ppermute x7, starting transfers between devices, swapped(): lax.ppermute(values, axis, [(i, i ^ p) for i in range(size)])  8.93 us
    ppermute x7, waiting for transfers between devices, swapped(): lax.ppermute(values, axis, [(i, i ^ p) for i in range(size)])  5.36 us
    pallas_call x1, Pallas kernels, call_inputs(): pl.pallas_call(inputs_kernel, out_shape=jax.ShapeDtypeStruct((1, tokens,...  4.44 us
    pallas_call x1, Pallas kernels, call_project(): pl.pallas_call(project_kernel, out_shape=(rows,) * 4 + (columns,) * 2 + (...  3.91 us
  transfers between devices with their start and end apart: 9, of which 4 were waited for; matrix products, arithmetic and copies ran while one was open for 0% of the time, Pallas kernels for 21%

profile of v4, /device:TPU:0, one launch (start us, length us, event | category | flops | bytes accessed | tf_op | source)
XLA Modules:
  0.0 39.7 jit_solution(1358042385098127033)
XLA Ops:
  0.6 0.5 %collective-permute-start = (bf16[1,256,768]{2,1,0:T(8,128)(2,1)}, bf16[1,256,768]{2,1,0:T(8,128)(2,1)S(1)}, u32[]{:S(2)}, u32[]{:S(2)}) collective-permute-start(bf16[1,256,768]{2,1,0:T(8,128)(2,1)} %x_hbm.1), channel_id=1, source_target_pairs={{0,1},{1,0},{2,3},{3,2},{4,5},{5,4},{6,7},{7,6},{8,9},{9,8},{10,11... | collective-permute-start | bytes 1179656 | tf_op jit(solution)/shard_map/ppermute | solution.py:763
  1.2 0.0 copy-start
  1.2 3.9 %shard_map.240 = (bf16[256,768]{1,0:T(8,128)(2,1)S(1)}, bf16[256,768]{1,0:T(8,128)(2,1)S(1)}, bf16[256,768]{1,0:T(8,128)(2,1)S(1)}, bf16[256,768]{1,0:T(8,128)(2...) custom-call(bf16[1,256,768]{2,1,0:T(8,128)(2,1)} %x_hbm.1, ...), custom_call_target="tpu_custom_call" | custom-call | flops 1000000000 | bytes 8000000 | tf_op jit(solution)/shard_map/pallas_call | solution.py:159
  5.1 0.0 collective-permute-done.other_ref
  5.1 0.0 copy-done
  5.1 14.7 %shard_map.241 = (bf16[1,256,768]{2,1,0:T(8,128)(2,1)}, f32[256,768]{1,0:T(8,128)S(1)}, bf16[768,256]{1,0:T(8,128)(2,1)S(1)}, bf16[256,768]{1,0:T(8,128)(2,1)S(1...) custom-call(s32[1,8]{1,0:T(1,128)S(1)} %copy-done, ...), custom_call_target="tpu_custom_call" | custom-call | flops 8999999488 | bytes 15000000 | tf_op jit(solution)/shard_map/pallas_call | solution.py:552
  19.8 0.1 collective-permute-start.1
  19.9 1.2 %collective-permute-done.1 = bf16[40,768]{1,0:T(8,128)(2,1)S(1)} collective-permute-done((bf16[40,768]{1,0:T(8,128)(2,1)S(1)}, bf16[40,768]{1,0:T(8,128)(2,1)S(1)}, u32[]{:S(2)}, u32[]{:S(2)}) %collective-permute-start.1) | collective-permute-done | bytes 61472 | tf_op jit(solution)/shard_map/ppermute | solution.py:718
  21.1 0.2 collective-permute-start.8
  21.3 3.8 %collective-permute-start.4 = (bf16[40,768]{1,0:T(8,128)(2,1)S(1)}, bf16[40,768]{1,0:T(8,128)(2,1)S(1)}, u32[]{:S(2)}, u32[]{:S(2)}) collective-permute-start(bf16[40,768]{1,0:T(8,128)(2,1)S(1)} %add_convert_fusion.1), channel_id=1, source_target_pairs={{0,6},{2,4},{4,2},{6,0},{8,14},{10,12},{12,10},{14,8},{16,22},{18,... | collective-permute-start | bytes 184328 | tf_op jit(solution)/shard_map/ppermute | solution.py:718
  25.1 0.5 %collective-permute-start.3 = (bf16[40,768]{1,0:T(8,128)(2,1)S(1)}, bf16[40,768]{1,0:T(8,128)(2,1)S(1)}, u32[]{:S(2)}, u32[]{:S(2)}) collective-permute-start(bf16[40,768]{1,0:T(8,128)(2,1)S(1)} %add_convert_fusion.1), channel_id=1, source_target_pairs={{0,4},{2,6},{4,0},{6,2},{8,12},{10,14},{12,8},{14,10},{16,20},{18,... | collective-permute-start | bytes 184328 | tf_op jit(solution)/shard_map/ppermute | solution.py:718
  25.6 0.1 collective-permute-start.2
  25.7 1.8 %collective-permute-done.4 = bf16[40,768]{1,0:T(8,128)(2,1)S(1)} collective-permute-done((bf16[40,768]{1,0:T(8,128)(2,1)S(1)}, bf16[40,768]{1,0:T(8,128)(2,1)S(1)}, u32[]{:S(2)}, u32[]{:S(2)}) %collective-permute-start.4) | collective-permute-done | bytes 61472 | tf_op jit(solution)/shard_map/ppermute | solution.py:718
  27.4 1.9 %collective-permute-done.3 = bf16[40,768]{1,0:T(8,128)(2,1)S(1)} collective-permute-done((bf16[40,768]{1,0:T(8,128)(2,1)S(1)}, bf16[40,768]{1,0:T(8,128)(2,1)S(1)}, u32[]{:S(2)}, u32[]{:S(2)}) %collective-permute-start.3) | collective-permute-done | bytes 61472 | tf_op jit(solution)/shard_map/ppermute | solution.py:718
  29.3 0.5 %collective-permute-done.2 = bf16[40,768]{1,0:T(8,128)(2,1)S(1)} collective-permute-done((bf16[40,768]{1,0:T(8,128)(2,1)S(1)}, bf16[40,768]{1,0:T(8,128)(2,1)S(1)}, u32[]{:S(2)}, u32[]{:S(2)}) %collective-permute-start.2) | collective-permute-done | bytes 61472 | tf_op jit(solution)/shard_map/ppermute | solution.py:718
  29.9 3.7 %collective-permute-start.7 = (bf16[40,768]{1,0:T(8,128)(2,1)S(1)}, bf16[40,768]{1,0:T(8,128)(2,1)S(1)}, u32[]{:S(2)}, u32[]{:S(2)}) collective-permute-start(bf16[40,768]{1,0:T(8,128)(2,1)S(1)} %add_convert_fusion.refs_0_), channel_id=1, source_target_pairs={{0,24},{2,26},{4,28},{6,30},{8,16},{10,18},{12,20},{14,22},{16,8},... | collective-permute-start | bytes 184328 | tf_op jit(solution)/shard_map/ppermute | solution.py:718
  33.6 0.0 collective-permute-start.6
  33.6 0.8 %collective-permute-start.5 = (bf16[40,768]{1,0:T(8,128)(2,1)S(1)}, bf16[40,768]{1,0:T(8,128)(2,1)S(1)}, u32[]{:S(2)}, u32[]{:S(2)}) collective-permute-start(bf16[40,768]{1,0:T(8,128)(2,1)S(1)} %add_convert_fusion.refs_0_), channel_id=1, source_target_pairs={{0,8},{2,10},{4,12},{6,14},{8,0},{10,2},{12,4},{14,6},{16,24},{18,... | collective-permute-start | bytes 184328 | tf_op jit(solution)/shard_map/ppermute | solution.py:718
  34.3 0.0 collective-permute-done.8.halo_ref
  34.3 4.4 %shard_map.242 = f32[1,256,768]{2,1,0:T(8,128)} custom-call(bf16[512,768]{1,0:T(8,128)(2,1)S(1)} %collective-permute-done.8.halo_ref, f32[256,768]{1,0:T(8,128)S(1)} %get-tuple-element.67.gr, bf16[768,256]{1,0:T(8,128)(2,1)S(1)} %get-tuple-element.68.dqt, bf16[256,768]{1,0:T(8,128)(2,1)S(1)} %get-tuple-element.69.dk, ...), custom_call_target="tpu_custom_call" | custom-call | flops 2000000000 | bytes 6000000 | tf_op jit(solution)/shard_map/pallas_call | solution.py:666
  38.8 0.0 collective-permute-done.7.refs_3_
  38.8 0.0 collective-permute-done.6.refs_2_
  38.8 0.0 collective-permute-done.5.refs_1_
  38.8 0.7 %shard_map.243 = (f32[8,768]{1,0:T(8,128)}, f32[8,768]{1,0:T(8,128)}, f32[8,768]{1,0:T(8,128)}, f32[8,768]{1,0:T(8,128)}, f32[768]{0:T(1024)}, /*index=5*/f32[768]{0:T(1024)}, f32[768]{0:T(1024)}, f32[768]{0:T(1024)}) custom-call(bf16[40,768]{1,0:T(8,128)(2,1)S(1)} %add_convert_fusion.refs_0_, bf16[40,768]{1,0:T(8,128)(2,1)S(1)} %collective-permute-done.5.refs_1_, ...), custom_call_target="tpu_custom_call" | custom-call | tf_op jit(solution)/shard_map/pallas_call | solution.py:703
  (2 shorter events, 0.1 us)
Async XLA Ops:
  0.6 4.4 %collective-permute-start = (bf16[1,256,768]{2,1,0:T(8,128)(2,1)}, bf16[1,256,768]{2,1,0:T(8,128)(2,1)S(1)}, u32[]{:S(2)}, u32[]{:S(2)}) collective-permute-start(bf16[1,256,768]{2,1,0:T(8,128)(2,1)} %x_hbm.1), channel_id=1, source_target_pairs={{0,1},{1,0},{2,3},{3,2},{4,5},{5,4},{6,7},{7,6},{8,9},{9,8},{10,11... | collective-permute-start | bytes 1179656 | tf_op jit(solution)/shard_map/ppermute | solution.py:763
  1.2 3.9 %copy-start = (s32[1,8]{1,0:T(1,128)S(1)}, s32[1,8]{1,0:T(1,128)}, u32[]{:S(2)}) copy-start(s32[1,8]{1,0:T(1,128)} %lengths_ref.1) | copy-start | bytes 100
  19.8 1.3 %collective-permute-start.1 = (bf16[40,768]{1,0:T(8,128)(2,1)S(1)}, bf16[40,768]{1,0:T(8,128)(2,1)S(1)}, u32[]{:S(2)}, u32[]{:S(2)}) collective-permute-start(bf16[40,768]{1,0:T(8,128)(2,1)S(1)} %get-tuple-element.64), channel_id=1, source_target_pairs={{0,1},{1,0},{2,3},{3,2},{4,5},{5,4},{6,7},{7,6},{8,9},{9,8},{10,11... | collective-permute-start | bytes 184328 | tf_op jit(solution)/shard_map/ppermute | solution.py:718
  21.1 13.2 %collective-permute-start.8 = (bf16[512,768]{1,0:T(8,128)(2,1)S(1)}, bf16[512,768]{1,0:T(8,128)(2,1)S(1)}, u32[]{:S(2)}, u32[]{:S(2)}) collective-permute-start(bf16[512,768]{1,0:T(8,128)(2,1)S(1)} %get-tuple-element.66), channel_id=1, source_target_pairs={{0,1},{1,0},{2,3},{3,2},{4,5},{5,4},{6,7},{7,6},{8,9},{9,8},{10,11... | collective-permute-start | bytes 2359304 | tf_op jit(solution)/shard_map/ppermute | solution.py:771
  21.3 6.1 %collective-permute-start.4 = (bf16[40,768]{1,0:T(8,128)(2,1)S(1)}, bf16[40,768]{1,0:T(8,128)(2,1)S(1)}, u32[]{:S(2)}, u32[]{:S(2)}) collective-permute-start(bf16[40,768]{1,0:T(8,128)(2,1)S(1)} %add_convert_fusion.1), channel_id=1, source_target_pairs={{0,6},{2,4},{4,2},{6,0},{8,14},{10,12},{12,10},{14,8},{16,22},{18,... | collective-permute-start | bytes 184328 | tf_op jit(solution)/shard_map/ppermute | solution.py:718
  25.1 4.2 %collective-permute-start.3 = (bf16[40,768]{1,0:T(8,128)(2,1)S(1)}, bf16[40,768]{1,0:T(8,128)(2,1)S(1)}, u32[]{:S(2)}, u32[]{:S(2)}) collective-permute-start(bf16[40,768]{1,0:T(8,128)(2,1)S(1)} %add_convert_fusion.1), channel_id=1, source_target_pairs={{0,4},{2,6},{4,0},{6,2},{8,12},{10,14},{12,8},{14,10},{16,20},{18,... | collective-permute-start | bytes 184328 | tf_op jit(solution)/shard_map/ppermute | solution.py:718
  25.6 4.2 %collective-permute-start.2 = (bf16[40,768]{1,0:T(8,128)(2,1)S(1)}, bf16[40,768]{1,0:T(8,128)(2,1)S(1)}, u32[]{:S(2)}, u32[]{:S(2)}) collective-permute-start(bf16[40,768]{1,0:T(8,128)(2,1)S(1)} %add_convert_fusion.1), channel_id=1, source_target_pairs={{0,2},{2,0},{4,6},{6,4},{8,10},{10,8},{12,14},{14,12},{16,18},{18,... | collective-permute-start | bytes 184328 | tf_op jit(solution)/shard_map/ppermute | solution.py:718
  29.9 8.9 %collective-permute-start.7 = (bf16[40,768]{1,0:T(8,128)(2,1)S(1)}, bf16[40,768]{1,0:T(8,128)(2,1)S(1)}, u32[]{:S(2)}, u32[]{:S(2)}) collective-permute-start(bf16[40,768]{1,0:T(8,128)(2,1)S(1)} %add_convert_fusion.refs_0_), channel_id=1, source_target_pairs={{0,24},{2,26},{4,28},{6,30},{8,16},{10,18},{12,20},{14,22},{16,8},... | collective-permute-start | bytes 184328 | tf_op jit(solution)/shard_map/ppermute | solution.py:718
  33.6 5.2 %collective-permute-start.6 = (bf16[40,768]{1,0:T(8,128)(2,1)S(1)}, bf16[40,768]{1,0:T(8,128)(2,1)S(1)}, u32[]{:S(2)}, u32[]{:S(2)}) collective-permute-start(bf16[40,768]{1,0:T(8,128)(2,1)S(1)} %add_convert_fusion.refs_0_), channel_id=1, source_target_pairs={{0,16},{2,18},{4,20},{6,22},{8,24},{10,26},{12,28},{14,30},{16,0},... | collective-permute-start | bytes 184328 | tf_op jit(solution)/shard_map/ppermute | solution.py:718
  33.6 5.3 %collective-permute-start.5 = (bf16[40,768]{1,0:T(8,128)(2,1)S(1)}, bf16[40,768]{1,0:T(8,128)(2,1)S(1)}, u32[]{:S(2)}, u32[]{:S(2)}) collective-permute-start(bf16[40,768]{1,0:T(8,128)(2,1)S(1)} %add_convert_fusion.refs_0_), channel_id=1, source_target_pairs={{0,8},{2,10},{4,12},{6,14},{8,0},{10,2},{12,4},{14,6},{16,24},{18,... | collective-permute-start | bytes 184328 | tf_op jit(solution)/shard_map/ppermute | solution.py:718

commit v5 on v4

--- a/solution.py
+++ b/solution.py
@@ -163,14 +163,10 @@
         + (low,) * 2
         + (square,) * 2
         + (flat,) * 3
-        + (square, shape((width, EARLY * width), BF16)),
+        + (square, shape((width, EARLY * width), BF16), square, flat),
         in_specs=[pl.BlockSpec(memory_space=pltpu.HBM)] * 10,
-        out_specs=(pl.BlockSpec(memory_space=pltpu.VMEM),) * 15,
-        scratch_shapes=[
-            pltpu.VMEM((width, width), BF16),
-            pltpu.VMEM((rank, width), BF16),
-            pltpu.SemaphoreType.DMA((11,)),
-        ],
+        out_specs=(pl.BlockSpec(memory_space=pltpu.VMEM),) * 17,
+        scratch_shapes=[pltpu.SemaphoreType.DMA((11,))],
         compiler_params=pltpu.CompilerParams(vmem_limit_bytes=20 * 2**20),
         cost_estimate=pl.CostEstimate(flops=10**9, bytes_accessed=8 * 10**6, transcendentals=0),
     )(*in_hbm(x, wq, wk, wv, *lows, wo, wu))
@@ -204,7 +200,7 @@
     out_hbm,
     gr_s,
     dqt_s,
-    dk_s,
+    ds_s,
     dv_s,
     halo_s,
     packed_ref,
@@ -306,12 +302,6 @@
         vh_s[rows] = vals
         vht_s[:, rows] = vals.T
 
-    project_halo(0)
-
-    @pl.when(wide)
-    def _():
-        project_halo(half)
-
     def joined(own, halo, reach, join):
         if reach == tokens:
             return join(own, halo)
@@ -396,18 +386,14 @@
         )
         own = (own - po * inner).astype(BF16)
         halo = (halo - ph * inner[:, :reach]).astype(BF16)
+        ds_s[head, pl.ds(0, tokens)] = own
+        ds_s[head, pl.ds(tokens, reach), pl.ds(0, reach)] = halo
         return grad, p_own, p_halo, own, halo
 
     def attend_back(pair, odd, reach, soft):
         lanes, rows = lanes_of(pair), rows_of(pair, odd)
         grad, p_own, p_halo, own, halo = soft
-        q_pair = q_s[:, lanes]
-        parts = (
-            dot(p_own, grad, NT),
-            dot(p_halo, grad[:, :reach], NT),
-            dot(own, q_pair),
-            dot(halo, q_pair[:reach]),
-        )
+        parts = (dot(p_own, grad, NT), dot(p_halo, grad[:, :reach], NT))
         dq = joined(
             dot(kt_s[rows, :], own),
             dot(kht_s[rows, pl.ds(0, reach)], halo),
@@ -419,124 +405,127 @@
             evens[0] = parts
             return
         even = evens.pop(0)
-        unscale = 1.0 / LOG2_E
         dv_s[:, lanes] = (even[0] + parts[0]).astype(BF16)
-        halo_s[pl.ds(tokens, reach), lanes] = (even[1] + parts[1]).astype(BF16)
-        dk_s[:, lanes] = (
-            jnp.where(low_lanes[:tokens], even[2], parts[2]) * unscale
-        ).astype(BF16)
-        halo_s[pl.ds(0, reach), lanes] = (
-            jnp.where(low_lanes[:reach], even[3], parts[3]) * unscale
-        ).astype(BF16)
-
-    def for_heads(first, second, third, lags):
-        @pl.when(jnp.logical_not(wide))
-        def _():
-            todo = [(pair, odd) for pair in range(heads // 2) for odd in range(2)]
-            one, two = {}, {}
-            for at in range(len(todo) + lags[1]):
-                if at < len(todo):
-                    one[at] = first(*todo[at], half)
-                back = at - lags[0]
-                if 0 <= back < len(todo):
-                    two[back] = second(*todo[back], half, one.pop(back))
-                back = at - lags[1]
-                if 0 <= back:
-                    third(*todo[back], half, two.pop(back))
-
-        @pl.when(wide)
-        def _():
+        halo_s[pl.ds(0, reach), lanes] = (even[1] + parts[1]).astype(BF16)
+
+    def for_heads(reach, first, second, third, lags):
+        if reach == tokens:
+
             def step(pair, none):
                 for odd in range(2):
-                    third(
-                        pair,
-                        odd,
-                        tokens,
-                        second(pair, odd, tokens, first(pair, odd, tokens)),
-                    )
+                    soft = second(pair, odd, tokens, first(pair, odd, tokens))
+                    third(pair, odd, tokens, soft)
 
             lax.fori_loop(0, heads // 2, step, None)
-
-    for_heads(score, soften, attend, (2, 4))
-
-    for copy in get_gains:
-        copy.wait()
-    resid_one = x_ref[...].astype(F32) + dot(ct_s[...], wo[...], TN)
-    normal, inverse = normed(resid_one)
-    normal_s[...] = normal
-    rstd_s[...] = jnp.broadcast_to(inverse, rstd_s.shape)
-    gain_one, shift_one = gain_one_s[...].reshape(1, width), shift_one_s[...].reshape(1, width)
-    gain_two, shift_two = gain_two_s[...].reshape(1, width), shift_two_s[...].reshape(1, width)
-    hidden_one = normal * gain_one + shift_one
-    hidden_s[...] = hidden_one.astype(BF16)
-    total_s[...] = hidden_one
-    for copy in get_ffn:
-        copy.wait()
-    for c in range(chunks):
-        part = pl.ds(c * width, width)
-        upward = dot(hidden_s[...], wu_part(c))
-        value, slope = gelu_and_slope(upward)
-        active_s[:, part] = value.astype(BF16)
-        slope_s[:, part] = slope.astype(BF16)
-        total_s[...] += dot(active_s[:, part], wd[part, :])
-    normal_two, inverse_two = normed(total_s[...])
-    out_s[...] = (normal_two * gain_two + shift_two).astype(BF16)
-
-    def put(source, target):
-        return fetch(source, target)
-
-    puts = [
-        put(out_s.at[pl.ds(0, half)], out_hbm.at[0, pl.ds(near, half)]),
-        put(out_s.at[pl.ds(half, half)], out_hbm.at[0, pl.ds(far, half)]),
-    ]
-    for copy in get_cot:
-        copy.wait()
-    grad_out = cot_s[...].astype(F32)
-    grad_gain_two = jnp.sum(grad_out * normal_two, axis=0, keepdims=True)
-    grad_shift_two = jnp.sum(grad_out, axis=0, keepdims=True)
-    grad_two = norm_back(grad_out * gain_two, normal_two, inverse_two)
-    hidden_s[...] = grad_two.astype(BF16)
-    total_s[...] = grad_two
-    for c in range(chunks):
-        part = pl.ds(c * width, width)
-        grad_up = slope_s[:, part].astype(F32) * dot(hidden_s[...], wd[part, :], NT)
-        active_s[:, part] = grad_up.astype(BF16)
-        total_s[...] += dot(active_s[:, part], wu_part(c), NT)
-    grad_hidden = total_s[...]
-    normal = normal_s[...]
-    grad_gain_one = jnp.sum(grad_hidden * normal, axis=0, keepdims=True)
-    grad_shift_one = jnp.sum(grad_hidden, axis=0, keepdims=True)
-    grad_one = norm_back(grad_hidden * gain_one, normal, rstd_s[:, :1])
-    gr_s[...] = grad_one
-    dot_s[...] = dot(wo[...], grad_one.astype(BF16), NT)
+            return
+        todo = [(pair, odd) for pair in range(heads // 2) for odd in range(2)]
+        one, two = {}, {}
+        for at in range(len(todo) + lags[1]):
+            if at < len(todo):
+                one[at] = first(*todo[at], reach)
+            back = at - lags[0]
+            if 0 <= back < len(todo):
+                two[back] = second(*todo[back], reach, one.pop(back))
+            back = at - lags[1]
+            if 0 <= back:
+                third(*todo[back], reach, two.pop(back))
+
+    def run(reach):
+        project_halo(0)
+        if reach == tokens:
+            project_halo(half)
+        for_heads(reach, score, soften, attend, (2, 4))
+
+        for copy in get_gains:
+            copy.wait()
+        resid_one = x_ref[...].astype(F32) + dot(ct_s[...], wo[...], TN)
+        normal, inverse = normed(resid_one)
+        normal_s[...] = normal
+        rstd_s[...] = jnp.broadcast_to(inverse, rstd_s.shape)
+        gain_one, shift_one = gain_one_s[...].reshape(1, width), shift_one_s[...].reshape(1, width)
+        gain_two, shift_two = gain_two_s[...].reshape(1, width), shift_two_s[...].reshape(1, width)
+        hidden_one = normal * gain_one + shift_one
+        hidden_s[...] = hidden_one.astype(BF16)
+        total_s[...] = hidden_one
+        for copy in get_ffn:
+            copy.wait()
+        upward = dot(hidden_s[...], wu_part(0))
+        for c in range(chunks):
+            part = pl.ds(c * width, width)
+            ahead = dot(hidden_s[...], wu_part(c + 1)) if c + 1 < chunks else None
+            value, slope = gelu_and_slope(upward)
+            active_s[:, part] = value.astype(BF16)
+            slope_s[:, part] = slope.astype(BF16)
+            total_s[...] += dot(active_s[:, part], wd[part, :])
+            upward = ahead
+        normal_two, inverse_two = normed(total_s[...])
+        out_s[...] = (normal_two * gain_two + shift_two).astype(BF16)
+
+        def put(source, target):
+            return fetch(source, target)
+
+        puts = [
+            put(out_s.at[pl.ds(0, half)], out_hbm.at[0, pl.ds(near, half)]),
+            put(out_s.at[pl.ds(half, half)], out_hbm.at[0, pl.ds(far, half)]),
+        ]
+        for copy in get_cot:
+            copy.wait()
+        grad_out = cot_s[...].astype(F32)
+        grad_gain_two = jnp.sum(grad_out * normal_two, axis=0, keepdims=True)
+        grad_shift_two = jnp.sum(grad_out, axis=0, keepdims=True)
+        grad_two = norm_back(grad_out * gain_two, normal_two, inverse_two)
+        hidden_s[...] = grad_two.astype(BF16)
+        total_s[...] = grad_two
+        grad_active = dot(hidden_s[...], wd[pl.ds(0, width), :], NT)
+        for c in range(chunks):
+            part = pl.ds(c * width, width)
+            ahead = None
+            if c + 1 < chunks:
+                ahead = dot(hidden_s[...], wd[pl.ds((c + 1) * width, width), :], NT)
+            active_s[:, part] = (slope_s[:, part].astype(F32) * grad_active).astype(BF16)
+            total_s[...] += dot(active_s[:, part], wu_part(c), NT)
+            grad_active = ahead
+        grad_hidden = total_s[...]
+        normal = normal_s[...]
+        grad_gain_one = jnp.sum(grad_hidden * normal, axis=0, keepdims=True)
+        grad_shift_one = jnp.sum(grad_hidden, axis=0, keepdims=True)
+        grad_one = norm_back(grad_hidden * gain_one, normal, rstd_s[:, :1])
+        gr_s[...] = grad_one
+        dot_s[...] = dot(wo[...], grad_one.astype(BF16), NT)
+
+        if reach < tokens:
+            halo_s[pl.ds(half, half)] = jnp.zeros((half, width), BF16)
+
+        for_heads(reach, back_score, back_soften, attend_back, (2, 4))
+
+        dv_halo = halo_s[...]
+        x_own = x_ref[...]
+        grad_qlow_t = (2.0 * dot(bq, dqt_s[...])).astype(BF16)
+        grad_vlow_t = (2.0 * dot(bv, dv_s[...], NT)).astype(BF16)
+        grad_halo_t = (2.0 * dot(bv, dv_halo, NT)).astype(BF16)
+        rows = [
+            dot(grad_qlow_t, x_own),
+            2.0 * dot(qlow_t, dqt_s[...], NT),
+            dot(grad_vlow_t, x_own) + dot(grad_halo_t, x_s[...]),
+            2.0 * (dot(vlow_t, dv_s[...]) + dot(halo_low_t, dv_halo)),
+            grad_gain_one,
+            grad_shift_one,
+            grad_gain_two,
+            grad_shift_two,
+        ]
+        spare = packed_ref.shape[0] - 4 * rank - 4
+        rows.append(jnp.zeros((spare, width), F32))
+        packed_ref[...] = jnp.concatenate(rows, axis=0).astype(BF16)
+        for copy in puts:
+            copy.wait()
 
     @pl.when(jnp.logical_not(wide))
     def _():
-        halo_s[pl.ds(half, half)] = jnp.zeros((half, width), BF16)
-        halo_s[pl.ds(tokens + half, half)] = jnp.zeros((half, width), BF16)
-
-    for_heads(back_score, back_soften, attend_back, (2, 4))
-
-    dv_halo = halo_s[pl.ds(tokens, tokens)]
-    x_own = x_ref[...]
-    grad_qlow_t = (2.0 * dot(bq, dqt_s[...])).astype(BF16)
-    grad_vlow_t = (2.0 * dot(bv, dv_s[...], NT)).astype(BF16)
-    grad_halo_t = (2.0 * dot(bv, dv_halo, NT)).astype(BF16)
-    rows = [
-        dot(grad_qlow_t, x_own),
-        2.0 * dot(qlow_t, dqt_s[...], NT),
-        dot(grad_vlow_t, x_own) + dot(grad_halo_t, x_s[...]),
-        2.0 * (dot(vlow_t, dv_s[...]) + dot(halo_low_t, dv_halo)),
-        grad_gain_one,
-        grad_shift_one,
-        grad_gain_two,
-        grad_shift_two,
-    ]
-    spare = packed_ref.shape[0] - 4 * rank - 4
-    rows.append(jnp.zeros((spare, width), F32))
-    packed_ref[...] = jnp.concatenate(rows, axis=0).astype(BF16)
-    for copy in puts:
-        copy.wait()
+        run(half)
+
+    @pl.when(wide)
+    def _():
+        run(tokens)
 
 
 def call_layer(lengths, projected, other, gains, wu, wd, cotangent):
@@ -555,9 +544,9 @@
             shape((1, tokens, width), BF16),
             shape((tokens, width), F32),
             shape((width, tokens), BF16),
+            shape((heads, 2 * tokens, tokens), BF16),
             shape((tokens, width), BF16),
             shape((tokens, width), BF16),
-            shape((2 * tokens, width), BF16),
             shape((packed_rows, width), BF16),
         ),
         in_specs=[pl.BlockSpec(memory_space=pltpu.SMEM)] + [here] * 16 + [hbm] * 7,
@@ -593,20 +582,86 @@
     )(lengths, *projected, other, *in_hbm(*gains, wu, wd, cotangent))
 
 
+def keys_kernel(
+    lengths_ref,
+    q_ref,
+    ds_ref,
+    dv_ref,
+    wk,
+    wv,
+    avt,
+    bv,
+    dk_ref,
+    sent_ref,
+    halo_s,
+):
+    tokens, width = q_ref.shape
+    half = tokens // 2
+    wide = crosses_widely(lengths_ref, tokens, half)
+    low_lanes = lax.broadcasted_iota(jnp.int32, (tokens, LANES), 1) < DH
+    unscale = 1.0 / LOG2_E
+
+    def step(pair, reach):
+        lanes = pl.ds(pl.multiple_of(pair * LANES, LANES), LANES)
+        q_pair = q_ref[:, lanes]
+        own = [dot(ds_ref[2 * pair + odd, pl.ds(0, tokens)], q_pair) for odd in range(2)]
+        halo = [
+            dot(ds_ref[2 * pair + odd, pl.ds(tokens, reach), pl.ds(0, reach)], q_pair[:reach])
+            for odd in range(2)
+        ]
+        dk_ref[:, lanes] = (jnp.where(low_lanes, *own) * unscale).astype(BF16)
+        halo_s[pl.ds(0, reach), lanes] = (
+            jnp.where(low_lanes[:reach], *halo) * unscale
+        ).astype(BF16)
+
+    def send(reach):
+        rows = pl.ds(0, reach)
+        grad_v = dv_ref[rows]
+        low_t = (2.0 * dot(bv[...], grad_v, NT)).astype(BF16)
+        sent_ref[rows] = (
+            dot(halo_s[rows], wk[...], NT) + dot(grad_v, wv[...], NT) + dot(low_t, avt[...], TN)
+        ).astype(BF16)
+
+    @pl.when(jnp.logical_not(wide))
+    def _():
+        for pair in range(width // LANES):
+            step(pair, half)
+
+    @pl.when(wide)
+    def _():
+        lax.fori_loop(0, width // LANES, lambda pair, none: step(pair, tokens), None)
+
+    @pl.when(jnp.logical_not(wide))
+    def _():
+        sent_ref[pl.ds(half, half)] = jnp.zeros((half, width), BF16)
+        send(half)
+
+    @pl.when(wide)
+    def _():
+        send(tokens)
+
+
+def call_keys(lengths, q, ds, dv_halo, wk, wv, avt, bv):
+    tokens, width = q.shape
+    rows = jax.ShapeDtypeStruct((tokens, width), BF16)
+    return pl.pallas_call(
+        keys_kernel,
+        out_shape=(rows, rows),
+        in_specs=[pl.BlockSpec(memory_space=pltpu.SMEM)]
+        + [pl.BlockSpec(memory_space=pltpu.VMEM)] * 7,
+        out_specs=(pl.BlockSpec(memory_space=pltpu.VMEM),) * 2,
+        scratch_shapes=[pltpu.VMEM((tokens, width), BF16)],
+        compiler_params=pltpu.CompilerParams(vmem_limit_bytes=6 * 2**20),
+        cost_estimate=pl.CostEstimate(flops=2 * 10**9, bytes_accessed=6 * 10**6, transcendentals=0),
+    )(lengths, q, ds, dv_halo, wk, wv, avt, bv)
+
+
 def inputs_kernel(
-    halo_ref,
+    received_ref,
     gr,
     dqt,
     dk,
     dv,
-    wq_hbm,
-    wk_hbm,
-    wv_hbm,
-    aqt_hbm,
-    bq_hbm,
-    avt_hbm,
-    bv_hbm,
-    out_hbm,
     wq,
     wk,
     wv,
@@ -614,44 +669,30 @@
     bq,
     avt,
     bv,
+    out_hbm,
     out_s,
     sems,
 ):
     tokens, width = gr.shape
     half = tokens // 2
     near, far = own_rows(lax.axis_index("seq"), half)
-    pairs = (
-        (wq_hbm, wq),
-        (wk_hbm, wk),
-        (wv_hbm, wv),
-        (bq_hbm, bq),
-        (aqt_hbm, aqt),
-        (bv_hbm, bv),
-        (avt_hbm, avt),
-    )
-    copies = [pltpu.make_async_copy(a, b, sems.at[i]) for i, (a, b) in enumerate(pairs)]
-    for copy in copies:
-        copy.start()
-    for copy in copies:
-        copy.wait()
-    grad_k = (dk[...].astype(F32) + halo_ref[pl.ds(0, tokens)].astype(F32)).astype(BF16)
-    grad_v = (dv[...].astype(F32) + halo_ref[pl.ds(tokens, tokens)].astype(F32)).astype(BF16)
     grad_qlow_t = (2.0 * dot(bq[...], dqt[...])).astype(BF16)
-    grad_vlow_t = (2.0 * dot(bv[...], grad_v, NT)).astype(BF16)
+    grad_vlow_t = (2.0 * dot(bv[...], dv[...], NT)).astype(BF16)
     out_s[...] = (
         gr[...]
+        + received_ref[...].astype(F32)
+        + dot(dk[...], wk[...], NT)
+        + dot(dv[...], wv[...], NT)
         + dot(dqt[...], wq[...], TT)
-        + dot(grad_k, wk[...], NT)
-        + dot(grad_v, wv[...], NT)
         + dot(grad_qlow_t, aqt[...], TN)
         + dot(grad_vlow_t, avt[...], TN)
     )
     puts = [
         pltpu.make_async_copy(
-            out_s.at[pl.ds(0, half)], out_hbm.at[0, pl.ds(near, half)], sems.at[11]
+            out_s.at[pl.ds(0, half)], out_hbm.at[0, pl.ds(near, half)], sems.at[0]
         ),
         pltpu.make_async_copy(
-            out_s.at[pl.ds(half, half)], out_hbm.at[0, pl.ds(far, half)], sems.at[12]
+            out_s.at[pl.ds(half, half)], out_hbm.at[0, pl.ds(far, half)], sems.at[1]
         ),
     ]
     for copy in puts:
@@ -660,20 +701,17 @@
         copy.wait()
 
 
-def call_inputs(halo, gr, dqt, dk, dv, wq, wk, wv, lows):
+def call_inputs(received, gr, dqt, dk, dv, *weights):
     tokens, width = gr.shape
-    weights = (wq, wk, wv, *lows)
     return pl.pallas_call(
         inputs_kernel,
         out_shape=jax.ShapeDtypeStruct((1, tokens, width), F32),
-        in_specs=[pl.BlockSpec(memory_space=pltpu.VMEM)] * 5
-        + [pl.BlockSpec(memory_space=pltpu.HBM)] * len(weights),
+        in_specs=[pl.BlockSpec(memory_space=pltpu.VMEM)] * 12,
         out_specs=pl.BlockSpec(memory_space=pltpu.HBM),
-        scratch_shapes=[pltpu.VMEM(a.shape, a.dtype) for a in weights]
-        + [pltpu.VMEM((tokens, width), F32), pltpu.SemaphoreType.DMA((13,))],
-        compiler_params=pltpu.CompilerParams(vmem_limit_bytes=10 * 2**20),
+        scratch_shapes=[pltpu.VMEM((tokens, width), F32), pltpu.SemaphoreType.DMA((2,))],
+        compiler_params=pltpu.CompilerParams(vmem_limit_bytes=6 * 2**20),
         cost_estimate=pl.CostEstimate(flops=2 * 10**9, bytes_accessed=6 * 10**6, transcendentals=0),
-    )(halo, gr, dqt, dk, dv, *in_hbm(*weights))
+    )(received, gr, dqt, dk, dv, *weights)
 
 
 def finish_kernel(rank, count, *refs):
@@ -730,11 +768,10 @@
     parts = swapped(values, "seq", (1,))
     stride, size = 1, lax.axis_size("dp")
     while stride < size:
-        values = added(parts)
+        radix = min(4, size // stride)
+        parts = swapped(added(parts), "dp", [stride * k for k in range(1, radix)])
         if stride == 1:
-            beside, values = lax.optimization_barrier((beside, values))
-        radix = min(4, size // stride)
-        parts = swapped(values, "dp", [stride * k for k in range(1, radix)])
+            *parts, beside = lax.optimization_barrier((*parts, beside))
         stride *= radix
     return parts, beside
 
@@ -763,13 +800,15 @@
     other = lax.ppermute(inputs, "seq", swap)
     lows = (a_query.T, b_query, a_value.T, b_value)
     gains = (gain_one, shift_one, gain_two, shift_two)
-    projected = call_project(inputs, w_query, w_key, w_value, lows, w_out, w_up)
-    output, gr, dqt, dk, dv, halo, packed = call_layer(
+    *projected, wq, aqt = call_project(inputs, w_query, w_key, w_value, lows, w_out, w_up)
+    wk, wv, bq, avt, bv = projected[8:13]
+    output, gr, dqt, ds, dv, dv_halo, packed = call_layer(
         pair_lengths, projected, other, gains, w_up, w_down, cotangent
     )
-    parts, halo = parts_of_sum(packed, halo)
-    halo = lax.ppermute(halo, "seq", swap)
-    grad_inputs = call_inputs(halo, gr, dqt, dk, dv, w_query, w_key, w_value, lows)
+    beside = call_keys(pair_lengths, projected[1], ds, dv_halo, wk, wv, avt, bv)
+    parts, (dk, sent) = parts_of_sum(packed, beside)
+    received = lax.ppermute(sent, "seq", swap)
+    grad_inputs = call_inputs(received, gr, dqt, dk, dv, wq, wk, wv, aqt, bq, avt, bv)
     *parts, grad_inputs = lax.optimization_barrier((*parts, grad_inputs))
     gaq, gbq, gav, gbv, *norms = call_finish(rank, parts)
     return (output, grad_inputs, gaq.T, gbq, gav.T, gbv, *norms)

time: 39.9 us -> 39.5 us (0.990)
  Pallas kernels: 23.7 us -> 23.3 us
    pallas_call x0 -> x1, Pallas kernels: none -> 2.21 us  [call_keys(): pl.pallas_call(keys_kernel, out_shape=(rows, rows), in_specs=[pl.BlockSpe...]
    pallas_call x1, Pallas kernels: 4.44 us -> 2.37 us  [call_inputs(): pl.pallas_call(inputs_kernel, out_shape=jax.ShapeDtypeStruct((1, tokens,...]
    pallas_call x1, Pallas kernels: 14.7 us -> 14.1 us  [call_layer(): pl.pallas_call(layer_kernel, out_shape=(shape((1, tokens, width), BF16),...]
  transfers between devices with their start and end apart: 9 -> 9, of which waited for: 4 -> 4; matrix products, arithmetic and copies ran while one was open for 0% -> 0% of each run, Pallas kernels for 21% -> 22%
where the time goes in v5:
time: 39.5 us; the launch traced here: 39.4 us
  Pallas kernels  23.3 us (59%)
  starting transfers between devices  9.42 us (24%)
  waiting for transfers between devices  5.64 us (14%)
  between operations  0.9 us (2%)
    pallas_call x1, Pallas kernels, call_layer(): pl.pallas_call(layer_kernel, out_shape=(shape((1, tokens, width), BF16),...  14.1 us
    ppermute x7, starting transfers between devices, swapped(): lax.ppermute(values, axis, [(i, i ^ p) for i in range(size)])  8.9 us
    ppermute x7, waiting for transfers between devices, swapped(): lax.ppermute(values, axis, [(i, i ^ p) for i in range(size)])  5.64 us
    pallas_call x1, Pallas kernels, call_project(): pl.pallas_call(project_kernel, out_shape=(rows,) * 4 + (columns,) * 2 + (...  3.92 us
    pallas_call x1, Pallas kernels, call_inputs(): pl.pallas_call(inputs_kernel, out_shape=jax.ShapeDtypeStruct((1, tokens,...  2.37 us
    pallas_call x1, Pallas kernels, call_keys(): pl.pallas_call(keys_kernel, out_shape=(rows, rows), in_specs=[pl.BlockSpe...  2.21 us
  transfers between devices with their start and end apart: 9, of which 4 were waited for; matrix products, arithmetic and copies ran while one was open for 0% of the time, Pallas kernels for 22%

profile of v5, /device:TPU:0, one launch (start us, length us, event | category | flops | bytes accessed | tf_op | source)
XLA Modules:
  0.0 39.4 jit_solution(2289345800885405301)
XLA Ops:
  0.6 0.5 %collective-permute-start = (bf16[1,256,768]{2,1,0:T(8,128)(2,1)}, bf16[1,256,768]{2,1,0:T(8,128)(2,1)S(1)}, u32[]{:S(2)}, u32[]{:S(2)}) collective-permute-start(bf16[1,256,768]{2,1,0:T(8,128)(2,1)} %x_hbm.1), channel_id=1, source_target_pairs={{0,1},{1,0},{2,3},{3,2},{4,5},{5,4},{6,7},{7,6},{8,9},{9,8},{10,11... | collective-permute-start | bytes 1179656 | tf_op jit(solution)/shard_map/ppermute | solution.py:800
  1.2 0.0 copy-start
  1.2 3.9 %shard_map.240 = (bf16[256,768]{1,0:T(8,128)(2,1)S(1)}, bf16[256,768]{1,0:T(8,128)(2,1)S(1)}, bf16[256,768]{1,0:T(8,128)(2,1)S(1)}, bf16[256,768]{1,0:T(8,128)(2...) custom-call(bf16[1,256,768]{2,1,0:T(8,128)(2,1)} %x_hbm.1, ...), custom_call_target="tpu_custom_call" | custom-call | flops 1000000000 | bytes 8000000 | tf_op jit(solution)/shard_map/pallas_call | solution.py:159
  5.1 0.0 collective-permute-done.other_ref
  5.1 0.0 copy-done
  5.1 14.1 %shard_map.241 = (bf16[1,256,768]{2,1,0:T(8,128)(2,1)}, f32[256,768]{1,0:T(8,128)S(1)}, bf16[768,256]{1,0:T(8,128)(2,1)S(1)}, bf16[12,512,256]{2,1,0:T(8,128)(2,...) custom-call(s32[1,8]{1,0:T(1,128)S(1)} %copy-done, ...), custom_call_target="tpu_custom_call" | custom-call | flops 8999999488 | bytes 15000000 | tf_op jit(solution)/shard_map/pallas_call | solution.py:541
  19.2 0.1 collective-permute-start.1
  19.3 1.2 %collective-permute-done.1 = bf16[40,768]{1,0:T(8,128)(2,1)S(1)} collective-permute-done((bf16[40,768]{1,0:T(8,128)(2,1)S(1)}, bf16[40,768]{1,0:T(8,128)(2,1)S(1)}, u32[]{:S(2)}, u32[]{:S(2)}) %collective-permute-start.1) | collective-permute-done | bytes 61472 | tf_op jit(solution)/shard_map/ppermute | solution.py:756
  20.5 3.7 %collective-permute-start.4 = (bf16[40,768]{1,0:T(8,128)(2,1)S(1)}, bf16[40,768]{1,0:T(8,128)(2,1)S(1)}, u32[]{:S(2)}, u32[]{:S(2)}) collective-permute-start(bf16[40,768]{1,0:T(8,128)(2,1)S(1)} %add_convert_fusion.1), channel_id=1, source_target_pairs={{0,6},{2,4},{4,2},{6,0},{8,14},{10,12},{12,10},{14,8},{16,22},{18,... | collective-permute-start | bytes 184328 | tf_op jit(solution)/shard_map/ppermute | solution.py:756
  24.2 0.5 %collective-permute-start.3 = (bf16[40,768]{1,0:T(8,128)(2,1)S(1)}, bf16[40,768]{1,0:T(8,128)(2,1)S(1)}, u32[]{:S(2)}, u32[]{:S(2)}) collective-permute-start(bf16[40,768]{1,0:T(8,128)(2,1)S(1)} %add_convert_fusion.1), channel_id=1, source_target_pairs={{0,4},{2,6},{4,0},{6,2},{8,12},{10,14},{12,8},{14,10},{16,20},{18,... | collective-permute-start | bytes 184328 | tf_op jit(solution)/shard_map/ppermute | solution.py:756
  24.7 0.1 collective-permute-start.2
  24.9 2.2 %shard_map.242 = (bf16[256,768]{1,0:T(8,128)(2,1)S(1)}, bf16[256,768]{1,0:T(8,128)(2,1)S(1)}) custom-call(s32[1,8]{1,0:T(1,128)S(1)} %copy-done, bf16[256,768]{1,0:T(8,128)(2,1)S(1)} %get-tuple-element.56.q_s.q_ref, bf16[12,512,256]{2,1,0:T(8,128)(2,1)S(1)} %get-tuple-element.72.ds_ref, bf16[256,768]{1,0:T(8,128)(2,1)S(1)} %get-tuple-element.73.dv_ref, ...), custom_call_target="tpu_custom_call" | custom-call | flops 2000000000 | bytes 6000000 | tf_op jit(solution)/shard_map/pallas_call | solution.py:647
  27.1 0.0 collective-permute-done.4
  27.1 1.4 %collective-permute-done.3 = bf16[40,768]{1,0:T(8,128)(2,1)S(1)} collective-permute-done((bf16[40,768]{1,0:T(8,128)(2,1)S(1)}, bf16[40,768]{1,0:T(8,128)(2,1)S(1)}, u32[]{:S(2)}, u32[]{:S(2)}) %collective-permute-start.3) | collective-permute-done | bytes 61472 | tf_op jit(solution)/shard_map/ppermute | solution.py:756
  28.4 0.5 %collective-permute-done.2 = bf16[40,768]{1,0:T(8,128)(2,1)S(1)} collective-permute-done((bf16[40,768]{1,0:T(8,128)(2,1)S(1)}, bf16[40,768]{1,0:T(8,128)(2,1)S(1)}, u32[]{:S(2)}, u32[]{:S(2)}) %collective-permute-start.2) | collective-permute-done | bytes 61472 | tf_op jit(solution)/shard_map/ppermute | solution.py:756
  28.9 0.0 collective-permute-start.8
  29.0 3.7 %collective-permute-start.7 = (bf16[40,768]{1,0:T(8,128)(2,1)S(1)}, bf16[40,768]{1,0:T(8,128)(2,1)S(1)}, u32[]{:S(2)}, u32[]{:S(2)}) collective-permute-start(bf16[40,768]{1,0:T(8,128)(2,1)S(1)} %add_convert_fusion.refs_0_), channel_id=1, source_target_pairs={{0,24},{2,26},{4,28},{6,30},{8,16},{10,18},{12,20},{14,22},{16,8},... | collective-permute-start | bytes 184328 | tf_op jit(solution)/shard_map/ppermute | solution.py:756
  32.7 0.0 collective-permute-start.6
  32.7 0.8 %collective-permute-start.5 = (bf16[40,768]{1,0:T(8,128)(2,1)S(1)}, bf16[40,768]{1,0:T(8,128)(2,1)S(1)}, u32[]{:S(2)}, u32[]{:S(2)}) collective-permute-start(bf16[40,768]{1,0:T(8,128)(2,1)S(1)} %add_convert_fusion.refs_0_), channel_id=1, source_target_pairs={{0,8},{2,10},{4,12},{6,14},{8,0},{10,2},{12,4},{14,6},{16,24},{18,... | collective-permute-start | bytes 184328 | tf_op jit(solution)/shard_map/ppermute | solution.py:756
  33.5 0.0 collective-permute-done.8.received_ref
  33.5 2.4 %shard_map.243 = f32[1,256,768]{2,1,0:T(8,128)} custom-call(bf16[256,768]{1,0:T(8,128)(2,1)S(1)} %collective-permute-done.8.received_ref, f32[256,768]{1,0:T(8,128)S(1)} %get-tuple-element.81.gr, bf16[768,256]{1,0:T(8,128)(2,1)S(1)} %get-tuple-element.82.dqt, bf16[256,768]{1,0:T(8,128)(2,1)S(1)} %get-tuple-element.83.dk, ...), custom_call_target="tpu_custom_call" | custom-call | flops 2000000000 | bytes 6000000 | tf_op jit(solution)/shard_map/pallas_call | solution.py:706
  35.8 0.0 collective-permute-done.7.refs_3_
  35.8 2.6 %collective-permute-done.6.refs_2_ = bf16[40,768]{1,0:T(8,128)(2,1)S(1)} collective-permute-done((bf16[40,768]{1,0:T(8,128)(2,1)S(1)}, bf16[40,768]{1,0:T(8,128)(2,1)S(1)}, u32[]{:S(2)}, u32[]{:S(2)}) %collective-permute-start.6) | collective-permute-done | bytes 61472 | tf_op jit(solution)/shard_map/ppermute | solution.py:756
  38.4 0.0 collective-permute-done.5.refs_1_
  38.4 0.7 %shard_map.244 = (f32[8,768]{1,0:T(8,128)}, f32[8,768]{1,0:T(8,128)}, f32[8,768]{1,0:T(8,128)}, f32[8,768]{1,0:T(8,128)}, f32[768]{0:T(1024)}, /*index=5*/f32[768]{0:T(1024)}, f32[768]{0:T(1024)}, f32[768]{0:T(1024)}) custom-call(bf16[40,768]{1,0:T(8,128)(2,1)S(1)} %add_convert_fusion.refs_0_, bf16[40,768]{1,0:T(8,128)(2,1)S(1)} %collective-permute-done.5.refs_1_, ...), custom_call_target="tpu_custom_call" | custom-call | tf_op jit(solution)/shard_map/pallas_call | solution.py:741
  (2 shorter events, 0.1 us)
Async XLA Ops:
  0.6 4.5 %collective-permute-start = (bf16[1,256,768]{2,1,0:T(8,128)(2,1)}, bf16[1,256,768]{2,1,0:T(8,128)(2,1)S(1)}, u32[]{:S(2)}, u32[]{:S(2)}) collective-permute-start(bf16[1,256,768]{2,1,0:T(8,128)(2,1)} %x_hbm.1), channel_id=1, source_target_pairs={{0,1},{1,0},{2,3},{3,2},{4,5},{5,4},{6,7},{7,6},{8,9},{9,8},{10,11... | collective-permute-start | bytes 1179656 | tf_op jit(solution)/shard_map/ppermute | solution.py:800
  1.2 3.9 %copy-start = (s32[1,8]{1,0:T(1,128)S(1)}, s32[1,8]{1,0:T(1,128)}, u32[]{:S(2)}) copy-start(s32[1,8]{1,0:T(1,128)} %lengths_ref.3) | copy-start | bytes 100
  19.2 1.3 %collective-permute-start.1 = (bf16[40,768]{1,0:T(8,128)(2,1)S(1)}, bf16[40,768]{1,0:T(8,128)(2,1)S(1)}, u32[]{:S(2)}, u32[]{:S(2)}) collective-permute-start(bf16[40,768]{1,0:T(8,128)(2,1)S(1)} %get-tuple-element.71), channel_id=1, source_target_pairs={{0,1},{1,0},{2,3},{3,2},{4,5},{5,4},{6,7},{7,6},{8,9},{9,8},{10,11... | collective-permute-start | bytes 184328 | tf_op jit(solution)/shard_map/ppermute | solution.py:756
  20.5 6.5 %collective-permute-start.4 = (bf16[40,768]{1,0:T(8,128)(2,1)S(1)}, bf16[40,768]{1,0:T(8,128)(2,1)S(1)}, u32[]{:S(2)}, u32[]{:S(2)}) collective-permute-start(bf16[40,768]{1,0:T(8,128)(2,1)S(1)} %add_convert_fusion.1), channel_id=1, source_target_pairs={{0,6},{2,4},{4,2},{6,0},{8,14},{10,12},{12,10},{14,8},{16,22},{18,... | collective-permute-start | bytes 184328 | tf_op jit(solution)/shard_map/ppermute | solution.py:756
  24.2 4.2 %collective-permute-start.3 = (bf16[40,768]{1,0:T(8,128)(2,1)S(1)}, bf16[40,768]{1,0:T(8,128)(2,1)S(1)}, u32[]{:S(2)}, u32[]{:S(2)}) collective-permute-start(bf16[40,768]{1,0:T(8,128)(2,1)S(1)} %add_convert_fusion.1), channel_id=1, source_target_pairs={{0,4},{2,6},{4,0},{6,2},{8,12},{10,14},{12,8},{14,10},{16,20},{18,... | collective-permute-start | bytes 184328 | tf_op jit(solution)/shard_map/ppermute | solution.py:756
  24.7 4.2 %collective-permute-start.2 = (bf16[40,768]{1,0:T(8,128)(2,1)S(1)}, bf16[40,768]{1,0:T(8,128)(2,1)S(1)}, u32[]{:S(2)}, u32[]{:S(2)}) collective-permute-start(bf16[40,768]{1,0:T(8,128)(2,1)S(1)} %add_convert_fusion.1), channel_id=1, source_target_pairs={{0,2},{2,0},{4,6},{6,4},{8,10},{10,8},{12,14},{14,12},{16,18},{18,... | collective-permute-start | bytes 184328 | tf_op jit(solution)/shard_map/ppermute | solution.py:756
  28.9 4.5 %collective-permute-start.8 = (bf16[256,768]{1,0:T(8,128)(2,1)S(1)}, bf16[256,768]{1,0:T(8,128)(2,1)S(1)}, u32[]{:S(2)}, u32[]{:S(2)}) collective-permute-start(bf16[256,768]{1,0:T(8,128)(2,1)S(1)} %get-tuple-element.80), channel_id=1, source_target_pairs={{0,1},{1,0},{2,3},{3,2},{4,5},{5,4},{6,7},{7,6},{8,9},{9,8},{10,11... | collective-permute-start | bytes 1179656 | tf_op jit(solution)/shard_map/ppermute | solution.py:810
  29.0 6.9 %collective-permute-start.7 = (bf16[40,768]{1,0:T(8,128)(2,1)S(1)}, bf16[40,768]{1,0:T(8,128)(2,1)S(1)}, u32[]{:S(2)}, u32[]{:S(2)}) collective-permute-start(bf16[40,768]{1,0:T(8,128)(2,1)S(1)} %add_convert_fusion.refs_0_), channel_id=1, source_target_pairs={{0,24},{2,26},{4,28},{6,30},{8,16},{10,18},{12,20},{14,22},{16,8},... | collective-permute-start | bytes 184328 | tf_op jit(solution)/shard_map/ppermute | solution.py:756
  32.7 5.8 %collective-permute-start.6 = (bf16[40,768]{1,0:T(8,128)(2,1)S(1)}, bf16[40,768]{1,0:T(8,128)(2,1)S(1)}, u32[]{:S(2)}, u32[]{:S(2)}) collective-permute-start(bf16[40,768]{1,0:T(8,128)(2,1)S(1)} %add_convert_fusion.refs_0_), channel_id=1, source_target_pairs={{0,16},{2,18},{4,20},{6,22},{8,24},{10,26},{12,28},{14,30},{16,0},... | collective-permute-start | bytes 184328 | tf_op jit(solution)/shard_map/ppermute | solution.py:756
  32.7 5.8 %collective-permute-start.5 = (bf16[40,768]{1,0:T(8,128)(2,1)S(1)}, bf16[40,768]{1,0:T(8,128)(2,1)S(1)}, u32[]{:S(2)}, u32[]{:S(2)}) collective-permute-start(bf16[40,768]{1,0:T(8,128)(2,1)S(1)} %add_convert_fusion.refs_0_), channel_id=1, source_target_pairs={{0,8},{2,10},{4,12},{6,14},{8,0},{10,2},{12,4},{14,6},{16,24},{18,... | collective-permute-start | bytes 184328 | tf_op jit(solution)/shard_map/ppermute | solution.py:756

commit v6 on v5

--- a/solution.py
+++ b/solution.py
@@ -139,12 +139,12 @@
     vlow_t = dot(avt[...], x, NT).astype(BF16)
     qlow_ref[...] = qlow_t
     vlow_ref[...] = vlow_t
+    vals = (dot(x, wv[...]) + 2.0 * dot(vlow_t, bv[...], TN)).astype(BF16)
+    v_ref[...] = vals
+    vt_ref[...] = vals.T
     q_ref[...] = (
         (dot(x, wq[...]) + 2.0 * dot(qlow_t, bq[...], TN)) * (LOG2_E / math.sqrt(DH))
     ).astype(BF16)
-    vals = (dot(x, wv[...]) + 2.0 * dot(vlow_t, bv[...], TN)).astype(BF16)
-    v_ref[...] = vals
-    vt_ref[...] = vals.T
     for copy in copies[9:]:
         copy.wait()
 
@@ -307,11 +307,6 @@
             return join(own, halo)
         return jnp.concatenate([join(own[:, :reach], halo), own[:, reach:]], axis=1)
 
-    def padded(halo, reach):
-        if reach == tokens:
-            return halo
-        return jnp.concatenate([halo, jnp.zeros((reach, tokens - reach), halo.dtype)], axis=1)
-
     def lanes_of(pair):
         return pl.ds(pl.multiple_of(pair * LANES, LANES), LANES)
 
@@ -348,16 +343,21 @@
             reach,
             jnp.add,
         )
-        own, halo = own.astype(BF16), padded(halo.astype(BF16), reach)
+        own, halo = own.astype(BF16), halo.astype(BF16)
         p_s[head, pl.ds(0, tokens)] = own
-        p_s[head, pl.ds(tokens, reach)] = halo
+        p_s[head, pl.ds(tokens, reach), pl.ds(0, reach)] = halo
         inv_s[head] = jnp.broadcast_to(inverse, inv_s.shape[1:])
         return own, halo, inverse
 
     def attend(pair, odd, reach, soft):
         own, halo, inverse = soft
         rows = rows_of(pair, odd)
-        context = dot(vt_s[rows, :], own) + dot(vht_s[rows, pl.ds(0, reach)], halo)
+        context = joined(
+            dot(vt_s[rows, :], own),
+            dot(vht_s[rows, pl.ds(0, reach)], halo),
+            reach,
+            jnp.add,
+        )
         ct_s[rows, :] = (context * inverse).astype(BF16)
 
     def back_score(pair, odd, reach):
@@ -498,7 +498,7 @@
 
         for_heads(reach, back_score, back_soften, attend_back, (2, 4))
 
-        dv_halo = halo_s[...]
+        dv_halo = halo_s[pl.ds(0, reach)]
         x_own = x_ref[...]
         grad_qlow_t = (2.0 * dot(bq, dqt_s[...])).astype(BF16)
         grad_vlow_t = (2.0 * dot(bv, dv_s[...], NT)).astype(BF16)
@@ -506,8 +506,8 @@
         rows = [
             dot(grad_qlow_t, x_own),
             2.0 * dot(qlow_t, dqt_s[...], NT),
-            dot(grad_vlow_t, x_own) + dot(grad_halo_t, x_s[...]),
-            2.0 * (dot(vlow_t, dv_s[...]) + dot(halo_low_t, dv_halo)),
+            dot(grad_vlow_t, x_own) + dot(grad_halo_t, x_s[pl.ds(0, reach)]),
+            2.0 * (dot(vlow_t, dv_s[...]) + dot(halo_low_t[:, :reach], dv_halo)),
             grad_gain_one,
             grad_shift_one,
             grad_gain_two,

time: 39.5 us -> 39.2 us (level)
  no operation moved by 1% of the time
where the time goes in v6:
time: 39.2 us; the launch traced here: 39.1 us
  Pallas kernels  23.1 us (59%)
  starting transfers between devices  9.42 us (24%)
  waiting for transfers between devices  5.65 us (14%)
  between operations  0.9 us (2%)
    pallas_call x1, Pallas kernels, call_layer(): pl.pallas_call(layer_kernel, out_shape=(shape((1, tokens, width), BF16),...  13.9 us
    ppermute x7, starting transfers between devices, swapped(): lax.ppermute(values, axis, [(i, i ^ p) for i in range(size)])  8.9 us
    ppermute x7, waiting for transfers between devices, swapped(): lax.ppermute(values, axis, [(i, i ^ p) for i in range(size)])  5.64 us
    pallas_call x1, Pallas kernels, call_project(): pl.pallas_call(project_kernel, out_shape=(rows,) * 4 + (columns,) * 2 + (...  3.87 us
    pallas_call x1, Pallas kernels, call_inputs(): pl.pallas_call(inputs_kernel, out_shape=jax.ShapeDtypeStruct((1, tokens,...  2.37 us
    pallas_call x1, Pallas kernels, call_keys(): pl.pallas_call(keys_kernel, out_shape=(rows, rows), in_specs=[pl.BlockSpe...  2.21 us
  transfers between devices with their start and end apart: 9, of which 4 were waited for; matrix products, arithmetic and copies ran while one was open for 0% of the time, Pallas kernels for 22%

profile of v6, /device:TPU:0, one launch (start us, length us, event | category | flops | bytes accessed | tf_op | source)
XLA Modules:
  0.0 39.1 jit_solution(3877979224935235214)
XLA Ops:
  0.6 0.5 %collective-permute-start = (bf16[1,256,768]{2,1,0:T(8,128)(2,1)}, bf16[1,256,768]{2,1,0:T(8,128)(2,1)S(1)}, u32[]{:S(2)}, u32[]{:S(2)}) collective-permute-start(bf16[1,256,768]{2,1,0:T(8,128)(2,1)} %x_hbm.1), channel_id=1, source_target_pairs={{0,1},{1,0},{2,3},{3,2},{4,5},{5,4},{6,7},{7,6},{8,9},{9,8},{10,11... | collective-permute-start | bytes 1179656 | tf_op jit(solution)/shard_map/ppermute | solution.py:800
  1.2 0.0 copy-start
  1.2 3.9 %shard_map.240 = (bf16[256,768]{1,0:T(8,128)(2,1)S(1)}, bf16[256,768]{1,0:T(8,128)(2,1)S(1)}, bf16[256,768]{1,0:T(8,128)(2,1)S(1)}, bf16[256,768]{1,0:T(8,128)(2...) custom-call(bf16[1,256,768]{2,1,0:T(8,128)(2,1)} %x_hbm.1, ...), custom_call_target="tpu_custom_call" | custom-call | flops 1000000000 | bytes 8000000 | tf_op jit(solution)/shard_map/pallas_call | solution.py:159
  5.0 0.0 collective-permute-done.other_ref
  5.1 0.0 copy-done
  5.1 13.9 %shard_map.241 = (bf16[1,256,768]{2,1,0:T(8,128)(2,1)}, f32[256,768]{1,0:T(8,128)S(1)}, bf16[768,256]{1,0:T(8,128)(2,1)S(1)}, bf16[12,512,256]{2,1,0:T(8,128)(2,...) custom-call(s32[1,8]{1,0:T(1,128)S(1)} %copy-done, ...), custom_call_target="tpu_custom_call" | custom-call | flops 8999999488 | bytes 15000000 | tf_op jit(solution)/shard_map/pallas_call | solution.py:541
  18.9 0.1 collective-permute-start.1
  19.1 1.2 %collective-permute-done.1 = bf16[40,768]{1,0:T(8,128)(2,1)S(1)} collective-permute-done((bf16[40,768]{1,0:T(8,128)(2,1)S(1)}, bf16[40,768]{1,0:T(8,128)(2,1)S(1)}, u32[]{:S(2)}, u32[]{:S(2)}) %collective-permute-start.1) | collective-permute-done | bytes 61472 | tf_op jit(solution)/shard_map/ppermute | solution.py:756
  20.3 3.7 %collective-permute-start.4 = (bf16[40,768]{1,0:T(8,128)(2,1)S(1)}, bf16[40,768]{1,0:T(8,128)(2,1)S(1)}, u32[]{:S(2)}, u32[]{:S(2)}) collective-permute-start(bf16[40,768]{1,0:T(8,128)(2,1)S(1)} %add_convert_fusion.1), channel_id=1, source_target_pairs={{0,6},{2,4},{4,2},{6,0},{8,14},{10,12},{12,10},{14,8},{16,22},{18,... | collective-permute-start | bytes 184328 | tf_op jit(solution)/shard_map/ppermute | solution.py:756
  23.9 0.5 %collective-permute-start.3 = (bf16[40,768]{1,0:T(8,128)(2,1)S(1)}, bf16[40,768]{1,0:T(8,128)(2,1)S(1)}, u32[]{:S(2)}, u32[]{:S(2)}) collective-permute-start(bf16[40,768]{1,0:T(8,128)(2,1)S(1)} %add_convert_fusion.1), channel_id=1, source_target_pairs={{0,4},{2,6},{4,0},{6,2},{8,12},{10,14},{12,8},{14,10},{16,20},{18,... | collective-permute-start | bytes 184328 | tf_op jit(solution)/shard_map/ppermute | solution.py:756
  24.4 0.1 collective-permute-start.2
  24.6 2.2 %shard_map.242 = (bf16[256,768]{1,0:T(8,128)(2,1)S(1)}, bf16[256,768]{1,0:T(8,128)(2,1)S(1)}) custom-call(s32[1,8]{1,0:T(1,128)S(1)} %copy-done, bf16[256,768]{1,0:T(8,128)(2,1)S(1)} %get-tuple-element.56.q_s.q_ref, bf16[12,512,256]{2,1,0:T(8,128)(2,1)S(1)} %get-tuple-element.72.ds_ref, bf16[256,768]{1,0:T(8,128)(2,1)S(1)} %get-tuple-element.73.dv_ref, ...), custom_call_target="tpu_custom_call" | custom-call | flops 2000000000 | bytes 6000000 | tf_op jit(solution)/shard_map/pallas_call | solution.py:647
  26.8 0.0 collective-permute-done.4
  26.8 1.3 %collective-permute-done.3 = bf16[40,768]{1,0:T(8,128)(2,1)S(1)} collective-permute-done((bf16[40,768]{1,0:T(8,128)(2,1)S(1)}, bf16[40,768]{1,0:T(8,128)(2,1)S(1)}, u32[]{:S(2)}, u32[]{:S(2)}) %collective-permute-start.3) | collective-permute-done | bytes 61472 | tf_op jit(solution)/shard_map/ppermute | solution.py:756
  28.2 0.5 %collective-permute-done.2 = bf16[40,768]{1,0:T(8,128)(2,1)S(1)} collective-permute-done((bf16[40,768]{1,0:T(8,128)(2,1)S(1)}, bf16[40,768]{1,0:T(8,128)(2,1)S(1)}, u32[]{:S(2)}, u32[]{:S(2)}) %collective-permute-start.2) | collective-permute-done | bytes 61472 | tf_op jit(solution)/shard_map/ppermute | solution.py:756
  28.7 0.0 collective-permute-start.8
  28.7 3.7 %collective-permute-start.7 = (bf16[40,768]{1,0:T(8,128)(2,1)S(1)}, bf16[40,768]{1,0:T(8,128)(2,1)S(1)}, u32[]{:S(2)}, u32[]{:S(2)}) collective-permute-start(bf16[40,768]{1,0:T(8,128)(2,1)S(1)} %add_convert_fusion.refs_0_), channel_id=1, source_target_pairs={{0,24},{2,26},{4,28},{6,30},{8,16},{10,18},{12,20},{14,22},{16,8},... | collective-permute-start | bytes 184328 | tf_op jit(solution)/shard_map/ppermute | solution.py:756
  32.4 0.0 collective-permute-start.6
  32.4 0.8 %collective-permute-start.5 = (bf16[40,768]{1,0:T(8,128)(2,1)S(1)}, bf16[40,768]{1,0:T(8,128)(2,1)S(1)}, u32[]{:S(2)}, u32[]{:S(2)}) collective-permute-start(bf16[40,768]{1,0:T(8,128)(2,1)S(1)} %add_convert_fusion.refs_0_), channel_id=1, source_target_pairs={{0,8},{2,10},{4,12},{6,14},{8,0},{10,2},{12,4},{14,6},{16,24},{18,... | collective-permute-start | bytes 184328 | tf_op jit(solution)/shard_map/ppermute | solution.py:756
  33.2 0.0 collective-permute-done.8.received_ref
  33.2 2.4 %shard_map.243 = f32[1,256,768]{2,1,0:T(8,128)} custom-call(bf16[256,768]{1,0:T(8,128)(2,1)S(1)} %collective-permute-done.8.received_ref, f32[256,768]{1,0:T(8,128)S(1)} %get-tuple-element.81.gr, bf16[768,256]{1,0:T(8,128)(2,1)S(1)} %get-tuple-element.82.dqt, bf16[256,768]{1,0:T(8,128)(2,1)S(1)} %get-tuple-element.83.dk, ...), custom_call_target="tpu_custom_call" | custom-call | flops 2000000000 | bytes 6000000 | tf_op jit(solution)/shard_map/pallas_call | solution.py:706
  35.6 0.0 collective-permute-done.7.refs_3_
  35.6 2.6 %collective-permute-done.6.refs_2_ = bf16[40,768]{1,0:T(8,128)(2,1)S(1)} collective-permute-done((bf16[40,768]{1,0:T(8,128)(2,1)S(1)}, bf16[40,768]{1,0:T(8,128)(2,1)S(1)}, u32[]{:S(2)}, u32[]{:S(2)}) %collective-permute-start.6) | collective-permute-done | bytes 61472 | tf_op jit(solution)/shard_map/ppermute | solution.py:756
  38.2 0.0 collective-permute-done.5.refs_1_
  38.2 0.7 %shard_map.244 = (f32[8,768]{1,0:T(8,128)}, f32[8,768]{1,0:T(8,128)}, f32[8,768]{1,0:T(8,128)}, f32[8,768]{1,0:T(8,128)}, f32[768]{0:T(1024)}, /*index=5*/f32[768]{0:T(1024)}, f32[768]{0:T(1024)}, f32[768]{0:T(1024)}) custom-call(bf16[40,768]{1,0:T(8,128)(2,1)S(1)} %add_convert_fusion.refs_0_, bf16[40,768]{1,0:T(8,128)(2,1)S(1)} %collective-permute-done.5.refs_1_, ...), custom_call_target="tpu_custom_call" | custom-call | tf_op jit(solution)/shard_map/pallas_call | solution.py:741
  (2 shorter events, 0.1 us)
Async XLA Ops:
  0.6 4.4 %collective-permute-start = (bf16[1,256,768]{2,1,0:T(8,128)(2,1)}, bf16[1,256,768]{2,1,0:T(8,128)(2,1)S(1)}, u32[]{:S(2)}, u32[]{:S(2)}) collective-permute-start(bf16[1,256,768]{2,1,0:T(8,128)(2,1)} %x_hbm.1), channel_id=1, source_target_pairs={{0,1},{1,0},{2,3},{3,2},{4,5},{5,4},{6,7},{7,6},{8,9},{9,8},{10,11... | collective-permute-start | bytes 1179656 | tf_op jit(solution)/shard_map/ppermute | solution.py:800
  1.2 3.9 %copy-start = (s32[1,8]{1,0:T(1,128)S(1)}, s32[1,8]{1,0:T(1,128)}, u32[]{:S(2)}) copy-start(s32[1,8]{1,0:T(1,128)} %lengths_ref.3) | copy-start | bytes 100
  18.9 1.3 %collective-permute-start.1 = (bf16[40,768]{1,0:T(8,128)(2,1)S(1)}, bf16[40,768]{1,0:T(8,128)(2,1)S(1)}, u32[]{:S(2)}, u32[]{:S(2)}) collective-permute-start(bf16[40,768]{1,0:T(8,128)(2,1)S(1)} %get-tuple-element.71), channel_id=1, source_target_pairs={{0,1},{1,0},{2,3},{3,2},{4,5},{5,4},{6,7},{7,6},{8,9},{9,8},{10,11... | collective-permute-start | bytes 184328 | tf_op jit(solution)/shard_map/ppermute | solution.py:756
  20.3 6.5 %collective-permute-start.4 = (bf16[40,768]{1,0:T(8,128)(2,1)S(1)}, bf16[40,768]{1,0:T(8,128)(2,1)S(1)}, u32[]{:S(2)}, u32[]{:S(2)}) collective-permute-start(bf16[40,768]{1,0:T(8,128)(2,1)S(1)} %add_convert_fusion.1), channel_id=1, source_target_pairs={{0,6},{2,4},{4,2},{6,0},{8,14},{10,12},{12,10},{14,8},{16,22},{18,... | collective-permute-start | bytes 184328 | tf_op jit(solution)/shard_map/ppermute | solution.py:756
  23.9 4.2 %collective-permute-start.3 = (bf16[40,768]{1,0:T(8,128)(2,1)S(1)}, bf16[40,768]{1,0:T(8,128)(2,1)S(1)}, u32[]{:S(2)}, u32[]{:S(2)}) collective-permute-start(bf16[40,768]{1,0:T(8,128)(2,1)S(1)} %add_convert_fusion.1), channel_id=1, source_target_pairs={{0,4},{2,6},{4,0},{6,2},{8,12},{10,14},{12,8},{14,10},{16,20},{18,... | collective-permute-start | bytes 184328 | tf_op jit(solution)/shard_map/ppermute | solution.py:756
  24.4 4.2 %collective-permute-start.2 = (bf16[40,768]{1,0:T(8,128)(2,1)S(1)}, bf16[40,768]{1,0:T(8,128)(2,1)S(1)}, u32[]{:S(2)}, u32[]{:S(2)}) collective-permute-start(bf16[40,768]{1,0:T(8,128)(2,1)S(1)} %add_convert_fusion.1), channel_id=1, source_target_pairs={{0,2},{2,0},{4,6},{6,4},{8,10},{10,8},{12,14},{14,12},{16,18},{18,... | collective-permute-start | bytes 184328 | tf_op jit(solution)/shard_map/ppermute | solution.py:756
  28.7 4.5 %collective-permute-start.8 = (bf16[256,768]{1,0:T(8,128)(2,1)S(1)}, bf16[256,768]{1,0:T(8,128)(2,1)S(1)}, u32[]{:S(2)}, u32[]{:S(2)}) collective-permute-start(bf16[256,768]{1,0:T(8,128)(2,1)S(1)} %get-tuple-element.80), channel_id=1, source_target_pairs={{0,1},{1,0},{2,3},{3,2},{4,5},{5,4},{6,7},{7,6},{8,9},{9,8},{10,11... | collective-permute-start | bytes 1179656 | tf_op jit(solution)/shard_map/ppermute | solution.py:810
  28.7 6.8 %collective-permute-start.7 = (bf16[40,768]{1,0:T(8,128)(2,1)S(1)}, bf16[40,768]{1,0:T(8,128)(2,1)S(1)}, u32[]{:S(2)}, u32[]{:S(2)}) collective-permute-start(bf16[40,768]{1,0:T(8,128)(2,1)S(1)} %add_convert_fusion.refs_0_), channel_id=1, source_target_pairs={{0,24},{2,26},{4,28},{6,30},{8,16},{10,18},{12,20},{14,22},{16,8},... | collective-permute-start | bytes 184328 | tf_op jit(solution)/shard_map/ppermute | solution.py:756
  32.4 5.8 %collective-permute-start.6 = (bf16[40,768]{1,0:T(8,128)(2,1)S(1)}, bf16[40,768]{1,0:T(8,128)(2,1)S(1)}, u32[]{:S(2)}, u32[]{:S(2)}) collective-permute-start(bf16[40,768]{1,0:T(8,128)(2,1)S(1)} %add_convert_fusion.refs_0_), channel_id=1, source_target_pairs={{0,16},{2,18},{4,20},{6,22},{8,24},{10,26},{12,28},{14,30},{16,0},... | collective-permute-start | bytes 184328 | tf_op jit(solution)/shard_map/ppermute | solution.py:756
  32.4 5.8 %collective-permute-start.5 = (bf16[40,768]{1,0:T(8,128)(2,1)S(1)}, bf16[40,768]{1,0:T(8,128)(2,1)S(1)}, u32[]{:S(2)}, u32[]{:S(2)}) collective-permute-start(bf16[40,768]{1,0:T(8,128)(2,1)S(1)} %add_convert_fusion.refs_0_), channel_id=1, source_target_pairs={{0,8},{2,10},{4,12},{6,14},{8,0},{10,2},{12,4},{14,6},{16,24},{18,... | collective-permute-start | bytes 184328 | tf_op jit(solution)/shard_map/ppermute | solution.py:756

commit v7 on v6

--- a/solution.py
+++ b/solution.py
@@ -10,6 +10,7 @@
 
 DH = 64
 LANES = 128
+EDGE = 48
 EARLY = 3
 EPSILON = 1e-05
 LOG2_E = math.log2(math.e)
@@ -68,6 +69,10 @@
         left = jnp.where(end < middle, middle - end, left)
         right = jnp.where(end >= middle, jnp.minimum(right, end - middle), right)
     return (right > 0) & ((left > half) | (right > half))
+
+
+def edge_rows(side, half):
+    return pl.multiple_of((1 - side) * (half - EDGE), 16)
 
 
 def in_hbm(*arrays):
@@ -614,11 +619,10 @@
             jnp.where(low_lanes[:reach], *halo) * unscale
         ).astype(BF16)
 
-    def send(reach):
-        rows = pl.ds(0, reach)
+    def send(rows, target):
         grad_v = dv_ref[rows]
         low_t = (2.0 * dot(bv[...], grad_v, NT)).astype(BF16)
-        sent_ref[rows] = (
+        sent_ref[target] = (
             dot(halo_s[rows], wk[...], NT) + dot(grad_v, wv[...], NT) + dot(low_t, avt[...], TN)
         ).astype(BF16)
 
@@ -631,14 +635,16 @@
     def _():
         lax.fori_loop(0, width // LANES, lambda pair, none: step(pair, tokens), None)
 
+    send(pl.ds(0, half), pl.ds(0, half))
+
     @pl.when(jnp.logical_not(wide))
     def _():
-        sent_ref[pl.ds(half, half)] = jnp.zeros((half, width), BF16)
-        send(half)
+        sent_ref[pl.ds(half, EDGE)] = jnp.zeros((EDGE, width), BF16)
 
     @pl.when(wide)
     def _():
-        send(tokens)
+        other = 1 - lax.axis_index("seq")
+        send(pl.ds(half + edge_rows(other, half), EDGE), pl.ds(half, EDGE))
 
 
 def call_keys(lengths, q, ds, dv_halo, wk, wv, avt, bv):
@@ -646,7 +652,7 @@
     rows = jax.ShapeDtypeStruct((tokens, width), BF16)
     return pl.pallas_call(
         keys_kernel,
-        out_shape=(rows, rows),
+        out_shape=(rows, jax.ShapeDtypeStruct((tokens // 2 + EDGE, width), BF16)),
         in_specs=[pl.BlockSpec(memory_space=pltpu.SMEM)]
         + [pl.BlockSpec(memory_space=pltpu.VMEM)] * 7,
         out_specs=(pl.BlockSpec(memory_space=pltpu.VMEM),) * 2,
@@ -675,18 +681,21 @@
 ):
     tokens, width = gr.shape
     half = tokens // 2
-    near, far = own_rows(lax.axis_index("seq"), half)
+    side = lax.axis_index("seq")
+    near, far = own_rows(side, half)
     grad_qlow_t = (2.0 * dot(bq[...], dqt[...])).astype(BF16)
     grad_vlow_t = (2.0 * dot(bv[...], dv[...], NT)).astype(BF16)
     out_s[...] = (
         gr[...]
-        + received_ref[...].astype(F32)
         + dot(dk[...], wk[...], NT)
         + dot(dv[...], wv[...], NT)
         + dot(dqt[...], wq[...], TT)
         + dot(grad_qlow_t, aqt[...], TN)
         + dot(grad_vlow_t, avt[...], TN)
     )
+    out_s[pl.ds(0, half)] += received_ref[pl.ds(0, half)].astype(F32)
+    edge = pl.ds(half + edge_rows(side, half), EDGE)
+    out_s[edge] += received_ref[pl.ds(half, EDGE)].astype(F32)
     puts = [
         pltpu.make_async_copy(
             out_s.at[pl.ds(0, half)], out_hbm.at[0, pl.ds(near, half)], sems.at[0]

time: 39.2 us -> 39.2 us (level)
  no operation moved by 1% of the time
where the time goes in v7:
time: 39.2 us; the launch traced here: 39.1 us
  Pallas kernels  23.2 us (59%)
  starting transfers between devices  9.42 us (24%)
  waiting for transfers between devices  5.52 us (14%)
  between operations  0.9 us (2%)
    pallas_call x1, Pallas kernels, call_layer(): pl.pallas_call(layer_kernel, out_shape=(shape((1, tokens, width), BF16),...  13.9 us
    ppermute x7, starting transfers between devices, swapped(): lax.ppermute(values, axis, [(i, i ^ p) for i in range(size)])  8.9 us
    ppermute x7, waiting for transfers between devices, swapped(): lax.ppermute(values, axis, [(i, i ^ p) for i in range(size)])  5.52 us
    pallas_call x1, Pallas kernels, call_project(): pl.pallas_call(project_kernel, out_shape=(rows,) * 4 + (columns,) * 2 + (...  3.87 us
    pallas_call x1, Pallas kernels, call_inputs(): pl.pallas_call(inputs_kernel, out_shape=jax.ShapeDtypeStruct((1, tokens,...  2.39 us
    pallas_call x1, Pallas kernels, call_keys(): pl.pallas_call(keys_kernel, out_shape=(rows, jax.ShapeDtypeStruct((tokens...  2.32 us
  transfers between devices with their start and end apart: 9, of which 4 were waited for; matrix products, arithmetic and copies ran while one was open for 0% of the time, Pallas kernels for 22%

profile of v7, /device:TPU:0, one launch (start us, length us, event | category | flops | bytes accessed | tf_op | source)
XLA Modules:
  0.0 39.1 jit_solution(3347717412088974731)
XLA Ops:
  0.6 0.5 %collective-permute-start = (bf16[1,256,768]{2,1,0:T(8,128)(2,1)}, bf16[1,256,768]{2,1,0:T(8,128)(2,1)S(1)}, u32[]{:S(2)}, u32[]{:S(2)}) collective-permute-start(bf16[1,256,768]{2,1,0:T(8,128)(2,1)} %x_hbm.1), channel_id=1, source_target_pairs={{0,1},{1,0},{2,3},{3,2},{4,5},{5,4},{6,7},{7,6},{8,9},{9,8},{10,11... | collective-permute-start | bytes 1179656 | tf_op jit(solution)/shard_map/ppermute | solution.py:809
  1.2 0.0 copy-start
  1.2 3.9 %shard_map.240 = (bf16[256,768]{1,0:T(8,128)(2,1)S(1)}, bf16[256,768]{1,0:T(8,128)(2,1)S(1)}, bf16[256,768]{1,0:T(8,128)(2,1)S(1)}, bf16[256,768]{1,0:T(8,128)(2...) custom-call(bf16[1,256,768]{2,1,0:T(8,128)(2,1)} %x_hbm.1, ...), custom_call_target="tpu_custom_call" | custom-call | flops 1000000000 | bytes 8000000 | tf_op jit(solution)/shard_map/pallas_call | solution.py:164
  5.0 0.0 collective-permute-done.other_ref
  5.1 0.0 copy-done
  5.1 13.9 %shard_map.241 = (bf16[1,256,768]{2,1,0:T(8,128)(2,1)}, f32[256,768]{1,0:T(8,128)S(1)}, bf16[768,256]{1,0:T(8,128)(2,1)S(1)}, bf16[12,512,256]{2,1,0:T(8,128)(2,...) custom-call(s32[1,8]{1,0:T(1,128)S(1)} %copy-done, ...), custom_call_target="tpu_custom_call" | custom-call | flops 8999999488 | bytes 15000000 | tf_op jit(solution)/shard_map/pallas_call | solution.py:546
  18.9 0.1 collective-permute-start.1
  19.1 1.2 %collective-permute-done.1 = bf16[40,768]{1,0:T(8,128)(2,1)S(1)} collective-permute-done((bf16[40,768]{1,0:T(8,128)(2,1)S(1)}, bf16[40,768]{1,0:T(8,128)(2,1)S(1)}, u32[]{:S(2)}, u32[]{:S(2)}) %collective-permute-start.1) | collective-permute-done | bytes 61472 | tf_op jit(solution)/shard_map/ppermute | solution.py:765
  20.3 3.7 %collective-permute-start.4 = (bf16[40,768]{1,0:T(8,128)(2,1)S(1)}, bf16[40,768]{1,0:T(8,128)(2,1)S(1)}, u32[]{:S(2)}, u32[]{:S(2)}) collective-permute-start(bf16[40,768]{1,0:T(8,128)(2,1)S(1)} %add_convert_fusion.1), channel_id=1, source_target_pairs={{0,6},{2,4},{4,2},{6,0},{8,14},{10,12},{12,10},{14,8},{16,22},{18,... | collective-permute-start | bytes 184328 | tf_op jit(solution)/shard_map/ppermute | solution.py:765
  23.9 0.5 %collective-permute-start.3 = (bf16[40,768]{1,0:T(8,128)(2,1)S(1)}, bf16[40,768]{1,0:T(8,128)(2,1)S(1)}, u32[]{:S(2)}, u32[]{:S(2)}) collective-permute-start(bf16[40,768]{1,0:T(8,128)(2,1)S(1)} %add_convert_fusion.1), channel_id=1, source_target_pairs={{0,4},{2,6},{4,0},{6,2},{8,12},{10,14},{12,8},{14,10},{16,20},{18,... | collective-permute-start | bytes 184328 | tf_op jit(solution)/shard_map/ppermute | solution.py:765
  24.4 0.1 collective-permute-start.2
  24.6 2.3 %shard_map.242 = (bf16[256,768]{1,0:T(8,128)(2,1)S(1)}, bf16[176,768]{1,0:T(8,128)(2,1)S(1)}) custom-call(s32[1,8]{1,0:T(1,128)S(1)} %copy-done, bf16[256,768]{1,0:T(8,128)(2,1)S(1)} %get-tuple-element.56.q_s.q_ref, bf16[12,512,256]{2,1,0:T(8,128)(2,1)S(1)} %get-tuple-element.72.ds_ref, bf16[256,768]{1,0:T(8,128)(2,1)S(1)} %get-tuple-element.73.dv_ref, ...), custom_call_target="tpu_custom_call" | custom-call | flops 2000000000 | bytes 6000000 | tf_op jit(solution)/shard_map/pallas_call | solution.py:653
  26.9 0.0 collective-permute-done.4
  26.9 1.2 %collective-permute-done.3 = bf16[40,768]{1,0:T(8,128)(2,1)S(1)} collective-permute-done((bf16[40,768]{1,0:T(8,128)(2,1)S(1)}, bf16[40,768]{1,0:T(8,128)(2,1)S(1)}, u32[]{:S(2)}, u32[]{:S(2)}) %collective-permute-start.3) | collective-permute-done | bytes 61472 | tf_op jit(solution)/shard_map/ppermute | solution.py:765
  28.2 0.5 %collective-permute-done.2 = bf16[40,768]{1,0:T(8,128)(2,1)S(1)} collective-permute-done((bf16[40,768]{1,0:T(8,128)(2,1)S(1)}, bf16[40,768]{1,0:T(8,128)(2,1)S(1)}, u32[]{:S(2)}, u32[]{:S(2)}) %collective-permute-start.2) | collective-permute-done | bytes 61472 | tf_op jit(solution)/shard_map/ppermute | solution.py:765
  28.7 0.0 collective-permute-start.8
  28.7 3.7 %collective-permute-start.7 = (bf16[40,768]{1,0:T(8,128)(2,1)S(1)}, bf16[40,768]{1,0:T(8,128)(2,1)S(1)}, u32[]{:S(2)}, u32[]{:S(2)}) collective-permute-start(bf16[40,768]{1,0:T(8,128)(2,1)S(1)} %add_convert_fusion.refs_0_), channel_id=1, source_target_pairs={{0,24},{2,26},{4,28},{6,30},{8,16},{10,18},{12,20},{14,22},{16,8},... | collective-permute-start | bytes 184328 | tf_op jit(solution)/shard_map/ppermute | solution.py:765
  32.4 0.0 collective-permute-start.6
  32.4 0.8 %collective-permute-start.5 = (bf16[40,768]{1,0:T(8,128)(2,1)S(1)}, bf16[40,768]{1,0:T(8,128)(2,1)S(1)}, u32[]{:S(2)}, u32[]{:S(2)}) collective-permute-start(bf16[40,768]{1,0:T(8,128)(2,1)S(1)} %add_convert_fusion.refs_0_), channel_id=1, source_target_pairs={{0,8},{2,10},{4,12},{6,14},{8,0},{10,2},{12,4},{14,6},{16,24},{18,... | collective-permute-start | bytes 184328 | tf_op jit(solution)/shard_map/ppermute | solution.py:765
  33.2 0.0 collective-permute-done.8.received_ref
  33.2 2.4 %shard_map.243 = f32[1,256,768]{2,1,0:T(8,128)} custom-call(bf16[176,768]{1,0:T(8,128)(2,1)S(1)} %collective-permute-done.8.received_ref, f32[256,768]{1,0:T(8,128)S(1)} %get-tuple-element.81.gr, bf16[768,256]{1,0:T(8,128)(2,1)S(1)} %get-tuple-element.82.dqt, bf16[256,768]{1,0:T(8,128)(2,1)S(1)} %get-tuple-element.83.dk, ...), custom_call_target="tpu_custom_call" | custom-call | flops 2000000000 | bytes 6000000 | tf_op jit(solution)/shard_map/pallas_call | solution.py:715
  35.6 0.0 collective-permute-done.7.refs_3_
  35.6 2.6 %collective-permute-done.6.refs_2_ = bf16[40,768]{1,0:T(8,128)(2,1)S(1)} collective-permute-done((bf16[40,768]{1,0:T(8,128)(2,1)S(1)}, bf16[40,768]{1,0:T(8,128)(2,1)S(1)}, u32[]{:S(2)}, u32[]{:S(2)}) %collective-permute-start.6) | collective-permute-done | bytes 61472 | tf_op jit(solution)/shard_map/ppermute | solution.py:765
  38.2 0.0 collective-permute-done.5.refs_1_
  38.2 0.7 %shard_map.244 = (f32[8,768]{1,0:T(8,128)}, f32[8,768]{1,0:T(8,128)}, f32[8,768]{1,0:T(8,128)}, f32[8,768]{1,0:T(8,128)}, f32[768]{0:T(1024)}, /*index=5*/f32[768]{0:T(1024)}, f32[768]{0:T(1024)}, f32[768]{0:T(1024)}) custom-call(bf16[40,768]{1,0:T(8,128)(2,1)S(1)} %add_convert_fusion.refs_0_, bf16[40,768]{1,0:T(8,128)(2,1)S(1)} %collective-permute-done.5.refs_1_, ...), custom_call_target="tpu_custom_call" | custom-call | tf_op jit(solution)/shard_map/pallas_call | solution.py:750
  (2 shorter events, 0.1 us)
Async XLA Ops:
  0.6 4.4 %collective-permute-start = (bf16[1,256,768]{2,1,0:T(8,128)(2,1)}, bf16[1,256,768]{2,1,0:T(8,128)(2,1)S(1)}, u32[]{:S(2)}, u32[]{:S(2)}) collective-permute-start(bf16[1,256,768]{2,1,0:T(8,128)(2,1)} %x_hbm.1), channel_id=1, source_target_pairs={{0,1},{1,0},{2,3},{3,2},{4,5},{5,4},{6,7},{7,6},{8,9},{9,8},{10,11... | collective-permute-start | bytes 1179656 | tf_op jit(solution)/shard_map/ppermute | solution.py:809
  1.2 3.9 %copy-start = (s32[1,8]{1,0:T(1,128)S(1)}, s32[1,8]{1,0:T(1,128)}, u32[]{:S(2)}) copy-start(s32[1,8]{1,0:T(1,128)} %lengths_ref.3) | copy-start | bytes 100
  18.9 1.3 %collective-permute-start.1 = (bf16[40,768]{1,0:T(8,128)(2,1)S(1)}, bf16[40,768]{1,0:T(8,128)(2,1)S(1)}, u32[]{:S(2)}, u32[]{:S(2)}) collective-permute-start(bf16[40,768]{1,0:T(8,128)(2,1)S(1)} %get-tuple-element.71), channel_id=1, source_target_pairs={{0,1},{1,0},{2,3},{3,2},{4,5},{5,4},{6,7},{7,6},{8,9},{9,8},{10,11... | collective-permute-start | bytes 184328 | tf_op jit(solution)/shard_map/ppermute | solution.py:765
  20.3 6.6 %collective-permute-start.4 = (bf16[40,768]{1,0:T(8,128)(2,1)S(1)}, bf16[40,768]{1,0:T(8,128)(2,1)S(1)}, u32[]{:S(2)}, u32[]{:S(2)}) collective-permute-start(bf16[40,768]{1,0:T(8,128)(2,1)S(1)} %add_convert_fusion.1), channel_id=1, source_target_pairs={{0,6},{2,4},{4,2},{6,0},{8,14},{10,12},{12,10},{14,8},{16,22},{18,... | collective-permute-start | bytes 184328 | tf_op jit(solution)/shard_map/ppermute | solution.py:765
  23.9 4.2 %collective-permute-start.3 = (bf16[40,768]{1,0:T(8,128)(2,1)S(1)}, bf16[40,768]{1,0:T(8,128)(2,1)S(1)}, u32[]{:S(2)}, u32[]{:S(2)}) collective-permute-start(bf16[40,768]{1,0:T(8,128)(2,1)S(1)} %add_convert_fusion.1), channel_id=1, source_target_pairs={{0,4},{2,6},{4,0},{6,2},{8,12},{10,14},{12,8},{14,10},{16,20},{18,... | collective-permute-start | bytes 184328 | tf_op jit(solution)/shard_map/ppermute | solution.py:765
  24.4 4.2 %collective-permute-start.2 = (bf16[40,768]{1,0:T(8,128)(2,1)S(1)}, bf16[40,768]{1,0:T(8,128)(2,1)S(1)}, u32[]{:S(2)}, u32[]{:S(2)}) collective-permute-start(bf16[40,768]{1,0:T(8,128)(2,1)S(1)} %add_convert_fusion.1), channel_id=1, source_target_pairs={{0,2},{2,0},{4,6},{6,4},{8,10},{10,8},{12,14},{14,12},{16,18},{18,... | collective-permute-start | bytes 184328 | tf_op jit(solution)/shard_map/ppermute | solution.py:765
  28.7 4.5 %collective-permute-start.8 = (bf16[176,768]{1,0:T(8,128)(2,1)S(1)}, bf16[176,768]{1,0:T(8,128)(2,1)S(1)}, u32[]{:S(2)}, u32[]{:S(2)}) collective-permute-start(bf16[176,768]{1,0:T(8,128)(2,1)S(1)} %get-tuple-element.80), channel_id=1, source_target_pairs={{0,1},{1,0},{2,3},{3,2},{4,5},{5,4},{6,7},{7,6},{8,9},{9,8},{10,11... | collective-permute-start | bytes 811016 | tf_op jit(solution)/shard_map/ppermute | solution.py:819
  28.7 6.9 %collective-permute-start.7 = (bf16[40,768]{1,0:T(8,128)(2,1)S(1)}, bf16[40,768]{1,0:T(8,128)(2,1)S(1)}, u32[]{:S(2)}, u32[]{:S(2)}) collective-permute-start(bf16[40,768]{1,0:T(8,128)(2,1)S(1)} %add_convert_fusion.refs_0_), channel_id=1, source_target_pairs={{0,24},{2,26},{4,28},{6,30},{8,16},{10,18},{12,20},{14,22},{16,8},... | collective-permute-start | bytes 184328 | tf_op jit(solution)/shard_map/ppermute | solution.py:765
  32.4 5.8 %collective-permute-start.6 = (bf16[40,768]{1,0:T(8,128)(2,1)S(1)}, bf16[40,768]{1,0:T(8,128)(2,1)S(1)}, u32[]{:S(2)}, u32[]{:S(2)}) collective-permute-start(bf16[40,768]{1,0:T(8,128)(2,1)S(1)} %add_convert_fusion.refs_0_), channel_id=1, source_target_pairs={{0,16},{2,18},{4,20},{6,22},{8,24},{10,26},{12,28},{14,30},{16,0},... | collective-permute-start | bytes 184328 | tf_op jit(solution)/shard_map/ppermute | solution.py:765
  32.4 5.8 %collective-permute-start.5 = (bf16[40,768]{1,0:T(8,128)(2,1)S(1)}, bf16[40,768]{1,0:T(8,128)(2,1)S(1)}, u32[]{:S(2)}, u32[]{:S(2)}) collective-permute-start(bf16[40,768]{1,0:T(8,128)(2,1)S(1)} %add_convert_fusion.refs_0_), channel_id=1, source_target_pairs={{0,8},{2,10},{4,12},{6,14},{8,0},{10,2},{12,4},{14,6},{16,24},{18,... | collective-permute-start | bytes 184328 | tf_op jit(solution)/shard_map/ppermute | solution.py:765
